TPU v7x, 32 devices: a whole 2x2x4 slice. The times are simulated.
32 devices in a mesh: band: 8 (over y, x, core), grid: 4 (over z).
Axes of the slice: x: 2, y: 2, z: 4, core: 2. Of those that a mesh axis runs over, the one named last changes fastest.
Arguments:
- orbitals: bfloat16 [64, 72, 5184], P('band', 'grid'), may hold values from -6 to 6
- owners: int32 [2], replicated, may hold values from 0 to 7, as said below
Outputs:
- exchange_field: float32 [64, 72, 5184], P('band', 'grid')
Inputs may be any that keep to these rules, and one draw needn't show every extreme that they name: owners[r] names a band group; the rounds name distinct groups.
All inputs are finite; a program needn't handle non-finite values.
Results may differ from a plain program's by a relative error of at most 0.0077.
Values may be sent and summed in bfloat16 or wider, within the bound.
No kernel may reach another device: no remote copies, remote signals or barrier semaphores. Data moves between devices by JAX's collectives and lax.ppermute only.
A program may use at most 128 MiB of HBM per device.

v0:
```python
import math

import jax
import jax.numpy as jnp
from jax import lax
from jax.sharding import PartitionSpec as P

box_length = 12.0
screening = 0.106


def broadcast(block, axis, holder):
    block = jnp.where(lax.axis_index(axis) == holder, block, jnp.zeros_like(block))
    return lax.psum(block, axis)


def cas_table(length):
    points = jnp.arange(length, dtype=jnp.int32)
    products = points[:, None] * points[None, :] % length
    phase = products.astype(jnp.float32) * (2.0 * math.pi / length)
    return (jnp.cos(phase) + jnp.sin(phase)).astype(jnp.bfloat16)


def screened_kernel(length):
    points = jnp.arange(length, dtype=jnp.int32)
    folded = jnp.minimum(points, length - points).astype(jnp.float32)
    squares = folded * folded
    factor = (2.0 * math.pi / box_length) ** 2
    wave_sq = factor * (squares[:, None, None] + squares[None, :, None] + squares[None, None, :])
    positive = jnp.where(wave_sq > 0.0, wave_sq, 1.0)
    screen = 4.0 * math.pi * (1.0 - jnp.exp(-positive / (4.0 * screening * screening))) / positive
    screen = screen / float(length * length * length)
    return jnp.where(wave_sq > 0.0, screen, 0.0)


def solve_whole(density, table, kernel):
    f32 = jnp.float32
    first = jnp.einsum("pxyz,cz->pxyc", density, table, preferred_element_type=f32).astype(
        jnp.bfloat16
    )
    second = jnp.einsum("pxyc,by->pxbc", first, table, preferred_element_type=f32).astype(
        jnp.bfloat16
    )
    third = (
        jnp.einsum("pxbc,ax->pabc", second, table, preferred_element_type=f32) * kernel[None]
    ).astype(jnp.bfloat16)
    fourth = jnp.einsum("pabc,xa->pxbc", third, table, preferred_element_type=f32).astype(
        jnp.bfloat16
    )
    fifth = jnp.einsum("pxbc,yb->pxyc", fourth, table, preferred_element_type=f32).astype(
        jnp.bfloat16
    )
    return jnp.einsum("pxyc,zc->pxyz", fifth, table, preferred_element_type=f32)


def body(orbitals, owners):
    band_count, slab_width, plane_size = orbitals.shape
    grid_count = lax.axis_size("grid")
    grid_size = slab_width * grid_count
    per_device = band_count // grid_count
    round_count = owners.shape[0]
    table = cas_table(grid_size)
    kernel = screened_kernel(grid_size)
    group_full = lax.all_gather(orbitals, "grid", axis=1, tiled=True)
    own_orbitals = lax.dynamic_slice_in_dim(
        group_full, lax.axis_index("grid") * per_device, per_device, 0
    )
    own_cells = own_orbitals.reshape(per_device, grid_size, grid_size, grid_size)
    running = jnp.zeros((per_device, grid_size, grid_size, grid_size), jnp.float32)
    for round_number in range(round_count):
        owner_group = owners[round_number]
        owner_set = broadcast(group_full, "band", owner_group)
        owner_cells = owner_set.reshape(band_count, grid_size, grid_size, grid_size)

        def update(current, orbital):
            density = (own_cells.astype(jnp.float32) * orbital.astype(jnp.float32)[None]).astype(
                jnp.bfloat16
            )
            potential = solve_whole(density, table, kernel)
            return (current + potential * orbital.astype(jnp.float32)[None], None)

        running, _ = lax.scan(update, running, owner_cells)
    flat_field = running.reshape(per_device, grid_size, plane_size)
    return lax.all_to_all(flat_field, "grid", split_axis=1, concat_axis=0, tiled=True)


def solution(mesh):
    placed = (P("band", "grid", None), P())
    return jax.shard_map(
        body, mesh=mesh, in_specs=placed, out_specs=P("band", "grid", None), check_vma=False
    )
```

profile of v0, /device:TPU:0, one launch (start us, length us, event | category | flops | bytes accessed | tf_op | source)
XLA Modules:
  0.0 1101.6 jit_solution(17294087421720053408)
XLA Ops:
  9.9 113.1 %all-gather.2.cloned.1.call-done = bf16[8,72,5184]{2,0,1:T(8,128)(2,1)} async-done(((bf16[8,18,5184]{2,0,1:T(8,128)(2,1)}), bf16[8,72,5184]{2,0,1:T(8,128)(2,1)}) %all-gather.2.cloned.1.call-update) | async-done | bytes 5971984 | tf_op jit(solution)/shard_map/all_gather | solution.py:64
  123.0 8.1 broadcast_select_fusion
  131.1 17.0 %reshape.71 = bf16[8,72,72,72]{3,2,0,1:T(8,128)(2,1)} reshape(bf16[8,72,5184]{2,0,1:T(8,128)(2,1)} %get-tuple-element.212) | data formatting | bytes 11943936 | tf_op jit(solution)/shard_map/reshape | solution.py:73
  148.1 9.9 copy.48
  158.0 17.0 %reshape.72 = bf16[8,72,72,72]{3,2,0,1:T(8,128)(2,1)} reshape(bf16[8,72,5184]{2,0,1:T(8,128)(2,1)} %get-tuple-element.211) | data formatting | bytes 11943936 | tf_op jit(solution)/shard_map/reshape | solution.py:73
  175.0 9.8 copy.49
  193.2 255.5 %all-reduce.3.cloned.1.call-done = (bf16[8,72,72,72]{3,2,1,0:T(8,128)(2,1)}, bf16[8,72,72,72]{3,2,1,0:T(8,128)(2,1)}) async-done(((bf16[8,72,72,72]{3,2,1,0:T(8,128)(2,1)}, bf16[8,72,72,72]{3,2,1,0:T(8,128)(2,1)}), (bf16[8,72,72,72]{3,2,1,0:T(8,128)(2,1)}, bf16[8,72,72,72]{3,2,1,0:T(8,128)(2,1)})) %all-reduce.3.cloned.1.call-update) | async-done | bytes 11943952 | tf_op jit(solution)/shard_map/psum | solution.py:14
  448.7 282.0 %while.25 = (s32[]{:T(128)}, f32[2,72,72,72]{3,2,1,0:T(8,128)}, bf16[2,72,72,72]{3,2,1,0:T(8,128)(2,1)}, bf16[8,72,72,72]{3,2,1,0:T(8,128)(2,1)}, f32[72]{0:T(12...) while((s32[]{:T(128)}, f32[2,72,72,72]{3,2,1,0:T(8,128)}, ...), condition=%wide.region_2.3_spmd.clone.clone, body=%wide.region_1.2_spmd.clone.clone.sunk | while | flops 658751616 | bytes 27641472 | solution.py:82
  450.2 6.3 convert_bitcast_fusion.10
  464.4 5.9 convert_bitcast_fusion.11
  475.6 7.0 select_add_fusion.2
  484.1 6.3 convert_bitcast_fusion.10
  498.3 5.9 convert_bitcast_fusion.11
  509.4 8.6 select_add_fusion.2
  519.5 6.3 convert_bitcast_fusion.10
  533.8 5.9 convert_bitcast_fusion.11
  544.9 8.6 select_add_fusion.2
  555.0 6.3 convert_bitcast_fusion.10
  569.2 5.9 convert_bitcast_fusion.11
  580.3 8.6 select_add_fusion.2
  590.4 6.3 convert_bitcast_fusion.10
  604.7 5.9 convert_bitcast_fusion.11
  615.8 8.6 select_add_fusion.2
  625.9 6.3 convert_bitcast_fusion.10
  640.1 5.9 convert_bitcast_fusion.11
  651.2 8.6 select_add_fusion.2
  661.3 6.3 convert_bitcast_fusion.10
  675.6 5.9 convert_bitcast_fusion.11
  686.7 8.6 select_add_fusion.2
  696.8 6.3 convert_bitcast_fusion.10
  711.0 5.9 convert_bitcast_fusion.11
  722.1 8.6 select_add_fusion.2
  730.7 282.4 %while.24 = (s32[]{:T(128)}, f32[2,72,72,72]{3,2,1,0:T(8,128)}, bf16[2,72,72,72]{3,2,1,0:T(8,128)(2,1)}, bf16[8,72,72,72]{3,2,1,0:T(8,128)(2,1)}, f32[72]{0:T(128)S(1)}, /*index=5*/f32[72,72]{0,1:T(8,128)S(1)}, s32[]{:T(128)}) while((s32[]{:T(128)}, f32[2,72,72,72]{3,2,1,0:T(8,128)}, bf16[2,72,72,72]{3,2,1,0:T(8,128)(2,1)}, ...), condition=%wide.region_5.6_spmd.clone.clone, body=%wide.region_4.5_spmd.clone.clone.sunk | while | flops 658005120 | bytes 27641456 | solution.py:82
  732.2 6.2 convert_bitcast_fusion.8
  738.5 5.3 copy.62
  746.4 5.8 convert_bitcast_fusion.9
  757.5 8.6 multiply_add_fusion.2
  767.5 6.2 convert_bitcast_fusion.8
  781.7 5.8 convert_bitcast_fusion.9
  792.8 8.6 multiply_add_fusion.2
  802.8 6.2 convert_bitcast_fusion.8
  817.0 5.8 convert_bitcast_fusion.9
  822.8 5.3 copy.63
  828.1 8.6 multiply_add_fusion.2
  838.1 6.2 convert_bitcast_fusion.8
  844.4 5.3 copy.62
  852.3 5.8 convert_bitcast_fusion.9
  863.4 8.6 multiply_add_fusion.2
  873.4 6.2 convert_bitcast_fusion.8
  887.6 5.8 convert_bitcast_fusion.9
  893.4 5.3 copy.63
  898.7 8.6 multiply_add_fusion.2
  908.7 6.2 convert_bitcast_fusion.8
  922.9 5.8 convert_bitcast_fusion.9
  934.0 8.6 multiply_add_fusion.2
  944.0 6.2 convert_bitcast_fusion.8
  950.3 5.3 copy.62
  958.2 5.8 convert_bitcast_fusion.9
  969.3 8.6 multiply_add_fusion.2
  979.3 6.2 convert_bitcast_fusion.8
  993.5 5.8 convert_bitcast_fusion.9
  999.3 5.3 copy.63
  1004.6 8.6 multiply_add_fusion.2
  1019.0 72.3 %all_to_all.18 = f32[2,72,5184]{2,0,1:T(2,128)S(1)} all-to-all(f32[2,72,5184]{2,0,1:T(2,128)S(1)} %copy.50), channel_id=1, replica_groups=mesh['band'=8,'grid'=4] {'grid'}, dimensions={1} | all-to-all | bytes 5971968 | tf_op jit(solution)/shard_map/all_to_all | solution.py:84
  (73 shorter events, 223.1 us)
Async XLA Ops:
  6.5 116.4 %all-gather.2.cloned.1.call-start = ((), (), s32[]{:S(2)}) async-start(), calls=%async_computation.1 | async-start | bytes 7557120 | tf_op jit(solution)/shard_map/all_gather | solution.py:64
  7.3 441.4 %all-reduce.3.cloned.1.call-start = ((), (), s32[]{:S(2)}) async-start(), calls=%async_computation.2 | async-start | bytes 42467328 | tf_op jit(solution)/shard_map/psum | solution.py:14
Sparse Core Ops, SparseCore 0:
  8.9 113.9 all-gather.1
  184.9 263.7 all-reduce.2
where the time goes:
time: 1110 us; the launch traced here: 1100 us
  waiting for transfers between devices  369 us (33%)
  matrix products  329 us (30%)
  local copies, waits for them, and re-layouts  241 us (22%)
  other arithmetic  75 us (7%)
  blocking collectives  72.3 us (7%)
  between operations  14.7 us (1%)
    psum x1, waiting for transfers between devices, broadcast(): return lax.psum(block, axis)  256 us
    dot_general x16, matrix products, solve_whole(): return jnp.einsum('pxyc,zc->pxyz', fifth, table, preferred_element_type=f32)  136 us
    all_gather x1, waiting for transfers between devices, body(): group_full = lax.all_gather(orbitals, 'grid', axis=1, tiled=True)  113 us
    dot_general x16, matrix products, solve_whole(): jnp.einsum('pxyc,by->pxbc', first, table, preferred_element_type=f32)  100 us
    dot_general x16, matrix products, solve_whole(): jnp.einsum('pabc,xa->pxbc', third, table, preferred_element_type=f32)  93.5 us
    convert_element_type x16, local copies, waits for them, and re-layouts, solve_whole(): jnp.einsum('pabc,xa->pxbc', third, table, preferred_element_type=f32)  84.1 us
    convert_element_type x16, local copies, waits for them, and re-layouts, solve_whole(): jnp.einsum('pxyc,by->pxbc', first, table, preferred_element_type=f32)  84.1 us
    all_to_all x1, blocking collectives, body(): lax.all_to_all(flat_field, 'grid', split_axis=1, concat_axis=0, tiled=True)  72.3 us
  transfers between devices with their start and end apart: 2, of which 2 were waited for; matrix products, arithmetic and copies ran while one was open for 1% of the time, Pallas kernels for 0%

commit v1 on v0

v1 whole, which is shorter than its diff:
```python
import functools
import math

import jax
import jax.numpy as jnp
import numpy as np
from jax import lax
from jax.experimental import pallas as pl
from jax.experimental.pallas import tpu as pltpu
from jax.sharding import PartitionSpec as P

box_length = 12.0
screening = 0.106
BF16 = jnp.bfloat16
F32 = jnp.float32
LANES = 256
HALF = 128
PACK = 3


def cas_table(length):
    points = np.arange(length)
    products = points[:, None] * points[None, :] % length
    phase = products.astype(np.float32) * np.float32(2.0 * math.pi / length)
    return (np.cos(phase) + np.sin(phase)).astype(BF16)


def screened_kernel(length):
    points = np.arange(length)
    folded = np.minimum(points, length - points).astype(np.float32)
    squares = folded * folded
    factor = np.float32((2.0 * math.pi / box_length) ** 2)
    wave_sq = factor * (squares[:, None, None] + squares[None, :, None] + squares[None, None, :])
    positive = np.where(wave_sq > 0.0, wave_sq, np.float32(1.0))
    screen = np.float32(4.0 * math.pi) * (
        np.float32(1.0) - np.exp(-positive / np.float32(4.0 * screening * screening))
    )
    screen = screen / positive / np.float32(length**3)
    return np.where(wave_sq > 0.0, screen, np.float32(0.0)).astype(np.float32)


def padded(array, width):
    return np.pad(array, [(0, 0)] * (array.ndim - 1) + [(0, width - array.shape[-1])])


def pack(bands):
    count, planes, side, _ = bands.shape
    split = bands.reshape(count, planes // 6, 2, PACK, side, side).transpose(0, 1, 2, 4, 3, 5)
    joined = split.reshape(count, planes // 6, 2 * side, PACK * side)
    return jnp.pad(joined, ((0, 0), (0, 0), (0, 0), (0, LANES - PACK * side)))


def unpack(packed, side):
    count, steps = packed.shape[:2]
    split = packed[..., : PACK * side].reshape(count, steps, 2, side, PACK, side)
    return split.transpose(0, 1, 2, 4, 3, 5).reshape(count, steps * 6, side, side)


def dot(left, right):
    return lax.dot_general(left, right, (((1,), (0,)), ((), ())), preferred_element_type=F32)


def swap_thirds(values, side):
    pad = jnp.zeros((values[0].shape[0], LANES - PACK * side), values[0].dtype)
    return [
        jnp.concatenate([v[:, side * s : side * s + side] for v in values] + [pad], axis=1)
        for s in range(PACK)
    ]


def make_groups(own_count, band_count):
    groups, left = [], []
    for own in range(own_count):
        full = band_count // PACK * PACK
        for j in range(0, full, PACK):
            groups.append(tuple((own, j + k) for k in range(PACK)))
        left += [(own, j) for j in range(full, band_count)]
    for start in range(0, len(left), PACK):
        groups.append(tuple(left[start : start + PACK]))
    return groups


def solve_body(*refs, side, pitch, sizes, groups, has_start):
    own_ref = refs[0]
    band_refs = refs[1 : 1 + len(sizes)]
    rest = refs[1 + len(sizes) :]
    if has_start:
        start_ref, rest = rest[0], rest[1:]
    kernel_ref, cas2_ref, ahead_ref, back_ref, thirds_ref, total_ref, low, high = rest
    where = [(ref, k) for ref, size in zip(band_refs, sizes) for k in range(size)]
    steps = own_ref.shape[1]
    half = side // 2
    wide = math.gcd(steps, 4)
    many = next(k for k in (12, 9, 6, 4, 3, 2, 1) if half % k == 0)

    def band(j, step):
        return where[j][0][where[j][1], step]

    def put(plane, value):
        low[pl.ds(plane * pitch, side), :] = value[:, :HALF]
        high[pl.ds(plane * pitch, side), :] = value[:, HALF:]

    def get(plane):
        parts = [r[pl.ds(plane * pitch, side), :] for r in (low, high)]
        return jnp.concatenate(parts, axis=1)

    def put_across(row, value):
        low[pl.ds(row, side, stride=pitch), :] = value[:, :HALF]
        high[pl.ds(row, side, stride=pitch), :] = value[:, HALF:]

    def get_across(row):
        parts = [r[pl.ds(row, side, stride=pitch), :] for r in (low, high)]
        return jnp.concatenate(parts, axis=1)

    if has_start:
        total_ref[...] = start_ref[...]
    else:
        total_ref[...] = jnp.zeros_like(total_ref)
    for pairs in groups:
        full = tuple(pairs) + (pairs[-1],) * (PACK - len(pairs))

        def first_two(q, carry):
            work = []
            for w in range(wide):
                step = q * wide + w
                density = [own_ref[i, step] * band(j, step) for i, j in full]
                work += [(6 * step + s, v) for s, v in enumerate(swap_thirds(density, side))]
            along_z = [dot(v, thirds_ref[...]).astype(BF16) for _, v in work]
            along_y = [dot(cas2_ref[...], v) for v in along_z]
            for (plane, _), v in zip(work, along_y):
                put(plane, v[:side])
                put(plane + PACK, v[side:])
            return carry

        def middle_two(q, carry):
            rows = [q * many + w for w in range(many)]
            planes = [
                jnp.concatenate([get_across(2 * r), get_across(2 * r + 1)], axis=0).astype(BF16)
                for r in rows
            ]
            waves = [dot(ahead_ref[...], v) for v in planes]
            waves = [(v * kernel_ref[r]).astype(BF16) for r, v in zip(rows, waves)]
            planes = [dot(back_ref[...], v) for v in waves]
            for r, v in zip(rows, planes):
                put_across(2 * r, v[:side])
                put_across(2 * r + 1, v[side:])
            return carry

        def last_two(q, carry):
            work = [q * wide + w for w in range(wide)]
            halves = [
                [
                    jnp.concatenate([get(6 * t + s), get(6 * t + PACK + s)], axis=0).astype(BF16)
                    for s in range(PACK)
                ]
                for t in work
            ]
            along_y = [[dot(cas2_ref[...], v).astype(BF16) for v in vs] for vs in halves]
            swapped = [swap_thirds(vs, side) for vs in along_y]
            potential = [[dot(v, thirds_ref[...]) for v in vs[: len(pairs)]] for vs in swapped]
            for t, vs in zip(work, potential):
                sums = {}
                for (i, j), v in zip(pairs, vs):
                    term = v * band(j, t).astype(F32)
                    sums[i] = sums[i] + term if i in sums else term
                for i, v in sums.items():
                    total_ref[i, t] += v
            return carry

        lax.fori_loop(0, steps // wide, first_two, 0)
        lax.fori_loop(0, half // many, middle_two, 0)
        lax.fori_loop(0, steps // wide, last_two, 0)


def solve(own, bands, start, tables, side):
    sizes = [b.shape[0] for b in bands]
    count = own.shape[0]
    groups = make_groups(count, sum(sizes))
    pitch = side + 4
    vmem = pl.BlockSpec(memory_space=pltpu.VMEM)
    operands = [own, *bands] + ([] if start is None else [start]) + list(tables)
    body = functools.partial(
        solve_body, side=side, pitch=pitch, sizes=sizes, groups=groups, has_start=start is not None
    )
    pairs = count * sum(sizes)
    return pl.pallas_call(
        body,
        in_specs=[vmem] * len(operands),
        out_specs=vmem,
        out_shape=jax.ShapeDtypeStruct(own.shape, F32),
        scratch_shapes=[pltpu.VMEM((side * pitch, HALF), F32)] * 2,
        compiler_params=pltpu.CompilerParams(vmem_limit_bytes=60 * 2**20),
        cost_estimate=pl.CostEstimate(
            flops=pairs * 12 * side**4 * 4, bytes_accessed=10 * 2**20, transcendentals=0
        ),
    )(*operands)


def make_tables(side, slab, level):
    cas = cas_table(side)
    two = np.eye(2, dtype=np.float32)
    cas2 = jnp.asarray(np.kron(two, cas.astype(np.float32)).astype(BF16))
    three = np.kron(np.eye(PACK, dtype=np.float32), cas.astype(np.float32))
    margin = LANES - three.shape[0]
    thirds = jnp.asarray(np.pad(three, ((0, margin), (0, margin))).astype(BF16))
    screen = screened_kernel(side).transpose(1, 0, 2)
    screen = padded(np.concatenate([screen] * PACK, axis=-1), LANES)
    screen = jnp.asarray(screen.reshape(side // 2, 2 * side, LANES))
    table = jnp.asarray(cas)
    moved = lax.dynamic_slice_in_dim(jnp.concatenate([table, table], 0), level * slab, side, 0)
    zero = jnp.zeros_like(moved)
    back = jnp.concatenate(
        [jnp.concatenate([moved, zero], 1), jnp.concatenate([zero, moved], 1)], 0
    )
    return screen, cas2, back.T, back, thirds


def from_level(value, ahead):
    count = lax.axis_size("grid")
    pairs = [((h + ahead) % count, h) for h in range(count)]
    return lax.ppermute(value, "grid", pairs)


def flip(value, bit):
    return lax.ppermute(value, "band", [(b, b ^ bit) for b in range(lax.axis_size("band"))])


def pick(options, index):
    result = options[0]
    for k in range(1, len(options)):
        result = jnp.where(index == k, options[k], result)
    return result


def own_bands(packed, per_device):
    levels = lax.axis_size("grid")
    level = lax.axis_index("grid")
    pieces = []
    for ahead in range(levels):
        start = (level + levels - ahead) % levels * per_device
        piece = lax.dynamic_slice_in_dim(packed, start, per_device, 0)
        pieces.append(from_level(piece, ahead) if ahead else piece)
    return jnp.concatenate(pieces, axis=1)


def whole(slab):
    levels = lax.axis_size("grid")
    pieces = [slab] + [from_level(slab, ahead) for ahead in range(1, levels)]
    return jnp.concatenate(pieces, axis=1)


def fields_small(packed, owners, own, tables, side):
    band = lax.axis_index("band")
    core, line = band % 2, band // 2
    share = packed.shape[0] // 4
    parts = []
    for k in range(4):
        part = lax.dynamic_slice_in_dim(packed, (line ^ k) * share, share, 0)
        parts.append(flip(part, 2 * k) if k else part)
    here = owners[core]
    there = owners[1 - core]
    mine = pick(parts, line ^ (here // 2))
    other = flip(pick(parts, line ^ (there // 2)), 1)
    mine = whole(jnp.where(here % 2 == core, mine, other))
    mine_x, mine_y = flip(mine, 2), flip(mine, 4)
    cut = share // 2
    corner = [flip(mine_x[:cut], 4), flip(mine_y[cut:], 2)]
    total = solve(own, [mine, flip(mine, 1)], None, tables, side)
    total = solve(own, [mine_x, mine_y, flip(mine_x, 1), flip(mine_y, 1)], total, tables, side)
    return solve(own, corner + [flip(c, 1) for c in corner], total, tables, side)


def fields_any(packed, owners, own, tables, side):
    total = None
    band = lax.axis_index("band")
    for r in range(owners.shape[0]):
        kept = jnp.where(band == owners[r], packed, jnp.zeros_like(packed))
        bands = whole(lax.psum(kept, "band"))
        total = solve(own, [bands], total, tables, side)
    return total


def body(orbitals, owners):
    band_count, slab, plane = orbitals.shape
    levels = lax.axis_size("grid")
    level = lax.axis_index("grid")
    side = slab * levels
    per_device = band_count // levels
    tables = make_tables(side, slab, level)
    packed = pack(orbitals.reshape(band_count, slab, side, side))
    own = own_bands(packed, per_device)
    small = lax.axis_size("band") == 8 and owners.shape[0] == 2 and band_count % 8 == 0
    fields = (fields_small if small else fields_any)(packed, owners, own, tables, side)
    fields = fields.astype(BF16)
    steps = slab // 6
    pieces = []
    for ahead in range(levels):
        behind = (levels - ahead) % levels
        piece = fields[:, behind * steps : (behind + 1) * steps]
        pieces.append(from_level(piece, ahead) if ahead else piece)
    ordered = jnp.concatenate(pieces + pieces, axis=0)
    ordered = lax.dynamic_slice_in_dim(ordered, (levels - level) * per_device, band_count, 0)
    return unpack(ordered, side).astype(F32).reshape(band_count, slab, plane)


def solution(mesh):
    placed = (P("band", "grid", None), P())
    return jax.shard_map(
        body, mesh=mesh, in_specs=placed, out_specs=P("band", "grid", None), check_vma=False
    )
```

time: 1110 us -> 351 us (0.32)
  matrix products: 329 us -> 0 us
  waiting for transfers between devices: 369 us -> 156 us
  local copies, waits for them, and re-layouts: 241 us -> 64.6 us
  Pallas kernels: 0 us -> 94.4 us
  blocking collectives: 72.3 us -> 0 us
  other arithmetic: 75 us -> 11 us
  starting transfers between devices: 0.04 us -> 18.5 us
    dot_general x48 -> x0, matrix products: 329 us -> none  [the longest x16 136 us: solve_whole(): return jnp.einsum('pxyc,zc->pxyz', fifth, table, preferred_element_type=f32)]
    psum x1 -> x0, waiting for transfers between devices: 256 us -> none  [broadcast(): return lax.psum(block, axis)]
    ppermute x0 -> x22, waiting for transfers between devices: none -> 156 us  [the longest x9 100 us: from_level(): return lax.ppermute(value, 'grid', pairs)]
    convert_element_type x32 -> x4, local copies, waits for them, and re-layouts: 168 us -> 27.8 us  [body(): return unpack(ordered, side).astype(F32).reshape(band_count, slab, plane)]
    all_gather x1 -> x0, waiting for transfers between devices: 113 us -> none  [body(): group_full = lax.all_gather(orbitals, 'grid', axis=1, tiled=True)]
    pallas_call x0 -> x3, Pallas kernels: none -> 94.4 us  [solve(): pl.pallas_call(body, in_specs=[vmem] * len(operands), out_specs=vmem, out...]
    all_to_all x1 -> x0, blocking collectives: 72.3 us -> none  [body(): lax.all_to_all(flat_field, 'grid', split_axis=1, concat_axis=0, tiled=True)]
    reshape x7 -> x2, local copies, waits for them, and re-layouts: 63.4 us -> 9.39 us  [pack(): joined = split.reshape(count, planes // 6, 2 * side, PACK * side)]
  transfers between devices with their start and end apart: 2 -> 22, of which waited for: 2 -> 10; matrix products, arithmetic and copies ran while one was open for 1% -> 3% of each run, Pallas kernels for 0% -> 20%
where the time goes in v1:
time: 351 us; the launch traced here: 350 us
  waiting for transfers between devices  156 us (44%)
  Pallas kernels  94.4 us (27%)
  local copies, waits for them, and re-layouts  64.6 us (18%)
  starting transfers between devices  18.5 us (5%)
  other arithmetic  11 us (3%)
  between operations  5.29 us (2%)
    ppermute x9, waiting for transfers between devices, from_level(): return lax.ppermute(value, 'grid', pairs)  100 us
    pallas_call x3, Pallas kernels, solve(): pl.pallas_call(body, in_specs=[vmem] * len(operands), out_specs=vmem, out...  94.4 us
    ppermute x13, waiting for transfers between devices, flip(): lax.ppermute(value, 'band', [(b, b ^ bit) for b in range(lax.axis_size('b...  55.7 us
    convert_element_type x4, local copies, waits for them, and re-layouts, body(): return unpack(ordered, side).astype(F32).reshape(band_count, slab, plane)  27.8 us
    another operation x2, local copies, waits for them, and re-layouts, pack(): bands.reshape(count, planes // 6, 2, PACK, side, side)  12.3 us
    ppermute x13, starting transfers between devices, flip(): lax.ppermute(value, 'band', [(b, b ^ bit) for b in range(lax.axis_size('b...  9.4 us
    reshape x2, local copies, waits for them, and re-layouts, pack(): joined = split.reshape(count, planes // 6, 2 * side, PACK * side)  9.39 us
    ppermute x9, starting transfers between devices, from_level(): return lax.ppermute(value, 'grid', pairs)  9.14 us
  transfers between devices with their start and end apart: 22, of which 10 were waited for; matrix products, arithmetic and copies ran while one was open for 3% of the time, Pallas kernels for 20%

profile of v1, /device:TPU:0, one launch (start us, length us, event | category | flops | bytes accessed | tf_op | source)
XLA Modules:
  0.0 349.9 jit_solution(11815748488744174308)
XLA Ops:
  0.0 5.3 %reshape_reshape.3 = bf16[8,3,2,3,72,72]{5,4,0,3,2,1:T(8,128)(2,1)} reshape(bf16[8,18,5184]{2,0,1:T(8,128)(2,1)} %param.6) | data formatting | bytes 2985984 | tf_op jit(solution)/shard_map/reshape;reshape | solution.py:48
  5.3 7.0 %copy.18 = bf16[8,3,2,3,72,72]{4,2,5,3,1,0:T(2,128)(2,1)} copy(bf16[8,3,2,3,72,72]{5,4,0,3,2,1:T(8,128)(2,1)} %reshape_reshape.3) | data formatting | bytes 2985984 | tf_op jit(solution)/shard_map/reshape;reshape | solution.py:48
  12.3 6.3 %reshape.11 = bf16[8,3,144,216]{2,3,1,0:T(8,128)(2,1)} reshape(bf16[8,3,2,72,3,72]{3,2,5,4,1,0:T(2,128)(2,1)} %bitcast.19) | data formatting | bytes 2985984 | tf_op jit(solution)/shard_map/reshape | solution.py:49
  18.7 3.0 copy.19
  21.7 0.0 copy-start.1
  21.7 1.1 pad_dynamic-slice_fusion
  22.9 3.9 %collective-permute-start.3 = (bf16[2,3,144,256]{3,2,1,0:T(8,128)(2,1)}, bf16[2,3,144,256]{3,2,1,0:T(8,128)(2,1)S(1)}, u32[]{:S(2)}, u32[]{:S(2)}) collective-permute-start(bf16[2,3,144,256]{3,2,1,0:T(8,128)(2,1)} %get-tuple-element.15), channel_id=1, source_target_pairs={{0,24},{4,28},{8,16},{12,20},{16,8},{20,12},{24,0},{28,4},{1,25},{... | collective-permute-start | bytes 1327112 | tf_op jit(solution)/shard_map/ppermute | solution.py:225
  26.8 0.5 collective-permute-start.4
  27.3 0.1 collective-permute-start.5
  27.3 0.6 fusion.5
  30.6 7.4 %collective-permute-done.3 = bf16[2,3,144,256]{3,2,1,0:T(8,128)(2,1)S(1)} collective-permute-done((bf16[2,3,144,256]{3,2,1,0:T(8,128)(2,1)}, bf16[2,3,144,256]{3,2,1,0:T(8,128)(2,1)S(1)}, u32[]{:S(2)}, u32[]{:S(2)}) %collective-permute-start.3) | collective-permute-done | bytes 442400 | tf_op jit(solution)/shard_map/ppermute | solution.py:225
  38.0 8.6 %collective-permute-done.4 = bf16[2,3,144,256]{3,2,1,0:T(8,128)(2,1)S(1)} collective-permute-done((bf16[2,3,144,256]{3,2,1,0:T(8,128)(2,1)}, bf16[2,3,144,256]{3,2,1,0:T(8,128)(2,1)S(1)}, u32[]{:S(2)}, u32[]{:S(2)}) %collective-permute-start.4) | collective-permute-done | bytes 442400 | tf_op jit(solution)/shard_map/ppermute | solution.py:225
  46.6 0.3 collective-permute-done.5
  46.9 0.2 select_select_fusion
  47.2 0.1 collective-permute-start.6
  49.8 2.5 select_select_fusion.1
  52.3 3.6 %collective-permute-start.7 = (bf16[2,3,144,256]{3,2,1,0:T(8,128)(2,1)S(1)}, bf16[2,3,144,256]{3,2,1,0:T(8,128)(2,1)S(1)}, u32[]{:S(2)}, u32[]{:S(2)}) collective-permute-start(bf16[2,3,144,256]{3,2,1,0:T(8,128)(2,1)S(1)} %get-tuple-element.9), channel_id=1, source_target_pairs={{1,0},{2,1},{3,2},{0,3},{5,4},{6,5},{7,6},{4,7},{9,8},{10,9},{11,1... | collective-permute-start | bytes 1327112 | tf_op jit(solution)/shard_map/ppermute | solution.py:221
  55.9 1.0 collective-permute-start.9
  56.9 9.6 %collective-permute-done.7 = bf16[2,3,144,256]{3,2,1,0:T(8,128)(2,1)S(1)} collective-permute-done((bf16[2,3,144,256]{3,2,1,0:T(8,128)(2,1)S(1)}, bf16[2,3,144,256]{3,2,1,0:T(8,128)(2,1)S(1)}, u32[]{:S(2)}, u32[]{:S(2)}) %collective-permute-start.7) | collective-permute-done | bytes 442400 | tf_op jit(solution)/shard_map/ppermute | solution.py:221
  66.5 27.9 %collective-permute-done.8 = bf16[2,3,144,256]{3,2,1,0:T(8,128)(2,1)S(1)} collective-permute-done((bf16[2,3,144,256]{3,2,1,0:T(8,128)(2,1)S(1)}, bf16[2,3,144,256]{3,2,1,0:T(8,128)(2,1)S(1)}, u32[]{:S(2)}, u32[]{:S(2)}) %collective-permute-start.8) | collective-permute-done | bytes 442400 | tf_op jit(solution)/shard_map/ppermute | solution.py:221
  94.3 0.0 collective-permute-done.9
  94.3 0.2 pad_maximum_fusion.1.refs_1_
  94.6 1.6 collective-permute-start.10
  96.1 0.7 collective-permute-start.12
  96.9 38.1 %collective-permute-done.10.refs_1_ = bf16[2,12,144,256]{3,2,1,0:T(8,128)(2,1)} collective-permute-done((bf16[2,12,144,256]{3,2,1,0:T(8,128)(2,1)S(1)}, bf16[2,12,144,256]{3,2,1,0:T(8,128)(2,1)}, u32[]{:S(2)}, u32[]{:S(2)}) %collective-permute-start.10) | collective-permute-done | bytes 1769504 | tf_op jit(solution)/shard_map/ppermute | solution.py:225
  135.0 0.0 collective-permute-start.16
  135.0 1.2 collective-permute-done.12.refs_2_
  136.2 2.5 collective-permute-start.1
  138.7 0.0 collective-permute-done
  138.7 0.7 constant_dynamic-slice_fusion
  139.4 0.7 fusion.2
  140.2 1.6 copy.20.refs_5_.refs_8_
  141.8 27.1 %collective-permute-done.1 = bf16[2,3,144,256]{3,2,1,0:T(8,128)(2,1)S(1)} collective-permute-done((bf16[2,3,144,256]{3,2,1,0:T(8,128)(2,1)}, bf16[2,3,144,256]{3,2,1,0:T(8,128)(2,1)S(1)}, u32[]{:S(2)}, u32[]{:S(2)}) %collective-permute-start.1) | collective-permute-done | bytes 442400 | tf_op jit(solution)/shard_map/ppermute | solution.py:221
  168.9 0.0 collective-permute-done.2
  168.9 1.4 pad_maximum_fusion.refs_0_
  170.3 1.2 slice.28
  171.5 0.8 collective-permute-start.11
  172.3 1.2 slice.29
  173.5 1.3 collective-permute-start.13
  174.8 24.4 %shard_map.64.refs_5_ = f32[2,12,144,256]{3,2,1,0:T(8,128)} custom-call(bf16[2,12,144,256]{3,2,1,0:T(8,128)(2,1)} %pad_maximum_fusion.refs_0_, bf16[2,12,144,256]{3,2,1,0:T(8,128)(2,1)} %copy-done, bf16[2,12,144,256]{3,2,1,0:T(8,128)(2,1)} %collective-permute-done.18.refs_2_, f32[36,144,256]{2,1,0:T(8,128)} %constant.104.clone.refs_3_.refs_6_, ...), custom_call_target="tpu_custom_call" | custom-call | flops 10319560704 | bytes 10485760 | tf_op jit(solution)/shard_map/pallas_call | solution.py:186
  199.2 0.0 collective-permute-done.11.refs_1_
  199.2 0.0 collective-permute-start.14
  199.2 0.5 collective-permute-start.15
  199.7 44.7 %shard_map.65.refs_5_ = f32[2,12,144,256]{3,2,1,0:T(8,128)} custom-call(bf16[2,12,144,256]{3,2,1,0:T(8,128)(2,1)} %pad_maximum_fusion.refs_0_, bf16[2,12,144,256]{3,2,1,0:T(8,128)(2,1)} %collective-permute-done.10.refs_1_, bf16[2,12,144,256]{3,2,1,0:T(8,128)(2,1)} %collective-permute-done.12.refs_2_, ...), custom_call_target="tpu_custom_call" | custom-call | flops 20639121408 | bytes 10485760 | tf_op jit(solution)/shard_map/pallas_call | solution.py:186
  244.5 0.9 copy-done.2
  245.4 1.0 copy-done.3
  246.4 25.3 %shard_map.66 = f32[2,12,144,256]{3,2,1,0:T(8,128)} custom-call(bf16[2,12,144,256]{3,2,1,0:T(8,128)(2,1)} %pad_maximum_fusion.refs_0_, bf16[1,12,144,256]{3,2,1,0:T(8,128)(2,1)} %collective-permute-done.11.refs_1_, bf16[1,12,144,256]{3,2,1,0:T(8,128)(2,1)} %collective-permute-done.13.refs_2_, bf16[1,12,144,256]{3,2,1,0:T(8,128)(2,1)} %copy-done.2, ...), custom_call_target="tpu_custom_call" | custom-call | flops 10319560704 | bytes 10485760 | tf_op jit(solution)/shard_map/pallas_call | solution.py:186
  271.7 2.2 convert_element_type.18
  273.8 1.1 fusion.4
  274.9 2.0 collective-permute-start.21
  277.0 11.6 %collective-permute-done.19 = bf16[2,3,144,256]{3,2,1,0:T(8,128)(2,1)S(1)} collective-permute-done((bf16[2,3,144,256]{3,2,1,0:T(8,128)(2,1)}, bf16[2,3,144,256]{3,2,1,0:T(8,128)(2,1)S(1)}, u32[]{:S(2)}, u32[]{:S(2)}) %collective-permute-start.19) | collective-permute-done | bytes 442400 | tf_op jit(solution)/shard_map/ppermute | solution.py:221
  288.6 0.8 constant_dynamic-update-slice_fusion.5
  289.3 24.3 %collective-permute-done.20 = bf16[2,3,144,256]{3,2,1,0:T(8,128)(2,1)S(1)} collective-permute-done((bf16[2,3,144,256]{3,2,1,0:T(8,128)(2,1)}, bf16[2,3,144,256]{3,2,1,0:T(8,128)(2,1)S(1)}, u32[]{:S(2)}, u32[]{:S(2)}) %collective-permute-start.20) | collective-permute-done | bytes 442400 | tf_op jit(solution)/shard_map/ppermute | solution.py:221
  313.6 0.8 constant_dynamic-update-slice_fusion.4
  314.4 0.8 constant_dynamic-update-slice_fusion.3
  315.2 0.8 slice_dynamic-update-slice_fusion.1
  316.0 0.8 constant_dynamic-update-slice_fusion.2
  316.9 0.8 constant_dynamic-update-slice_fusion.1
  317.7 0.8 constant_dynamic-update-slice_fusion
  318.4 3.7 %dynamic-slice_convert_fusion = f32[8,3,144,216]{3,2,1,0:T(8,128)} fusion(bf16[16,3,144,256]{3,2,1,0:T(8,128)(2,1)} %constant_dynamic-update-slice_fusion, s32[]{:T(128)S(6)} %select_n.151), kind=kLoop, calls=%fused_computation | loop fusion | flops 746496 | bytes 4478980 | tf_op jit(solution)/shard_map/convert_element_type | solution.py:303
  322.1 5.9 %copy.23 = f32[8,3,144,216]{2,3,1,0:T(8,128)} copy(f32[8,3,144,216]{3,2,1,0:T(8,128)} %dynamic-slice_convert_fusion) | data formatting | bytes 5971968 | tf_op jit(solution)/shard_map/convert_element_type | solution.py:303
  328.1 7.9 %reshape.13 = f32[8,3,2,72,3,72]{3,2,5,4,1,0:T(2,128)} reshape(f32[8,3,144,216]{2,3,1,0:T(8,128)} %copy.23) | data formatting | bytes 5971968 | tf_op jit(solution)/shard_map/convert_element_type | solution.py:303
  336.0 8.5 %copy.24 = f32[8,3,2,3,72,72]{5,4,0,3,2,1:T(8,128)} copy(f32[8,3,2,3,72,72]{4,2,5,3,1,0:T(2,128)} %bitcast.18) | data formatting | bytes 5971968 | tf_op jit(solution)/shard_map/convert_element_type | solution.py:303
  344.5 5.4 %reshape.12 = f32[8,18,5184]{2,0,1:T(8,128)} reshape(f32[8,3,2,3,72,72]{5,4,0,3,2,1:T(8,128)} %copy.24) | data formatting | bytes 5971968 | tf_op jit(solution)/shard_map/convert_element_type | solution.py:303
  (20 shorter events, 0.0 us)
Async XLA Ops:
  21.7 5.6 %copy-start.1 = (s32[2]{0:T(128)S(1)}, s32[2]{0:T(128)}, u32[]{:S(2)}) copy-start(s32[2]{0:T(128)} %param.7) | copy-start | bytes 28
  22.9 15.1 %collective-permute-start.3 = (bf16[2,3,144,256]{3,2,1,0:T(8,128)(2,1)}, bf16[2,3,144,256]{3,2,1,0:T(8,128)(2,1)S(1)}, u32[]{:S(2)}, u32[]{:S(2)}) collective-permute-start(bf16[2,3,144,256]{3,2,1,0:T(8,128)(2,1)} %get-tuple-element.15), channel_id=1, source_target_pairs={{0,24},{4,28},{8,16},{12,20},{16,8},{20,12},{24,0},{28,4},{1,25},{... | collective-permute-start | bytes 1327112 | tf_op jit(solution)/shard_map/ppermute | solution.py:225
  26.8 19.9 %collective-permute-start.4 = (bf16[2,3,144,256]{3,2,1,0:T(8,128)(2,1)}, bf16[2,3,144,256]{3,2,1,0:T(8,128)(2,1)S(1)}, u32[]{:S(2)}, u32[]{:S(2)}) collective-permute-start(bf16[2,3,144,256]{3,2,1,0:T(8,128)(2,1)} %get-tuple-element.16), channel_id=1, source_target_pairs={{0,16},{4,20},{8,24},{12,28},{16,0},{20,4},{24,8},{28,12},{1,17},{... | collective-permute-start | bytes 1327112 | tf_op jit(solution)/shard_map/ppermute | solution.py:225
  27.3 19.6 %collective-permute-start.5 = (bf16[2,3,144,256]{3,2,1,0:T(8,128)(2,1)S(1)}, bf16[2,3,144,256]{3,2,1,0:T(8,128)(2,1)S(1)}, u32[]{:S(2)}, u32[]{:S(2)}) collective-permute-start(bf16[2,3,144,256]{3,2,1,0:T(8,128)(2,1)S(1)} %get-tuple-element.14), channel_id=1, source_target_pairs={{0,8},{4,12},{8,0},{12,4},{16,24},{20,28},{24,16},{28,20},{1,9},{5... | collective-permute-start | bytes 1327112 | tf_op jit(solution)/shard_map/ppermute | solution.py:225
  47.2 2.7 collective-permute-start.6
  52.3 14.2 %collective-permute-start.7 = (bf16[2,3,144,256]{3,2,1,0:T(8,128)(2,1)S(1)}, bf16[2,3,144,256]{3,2,1,0:T(8,128)(2,1)S(1)}, u32[]{:S(2)}, u32[]{:S(2)}) collective-permute-start(bf16[2,3,144,256]{3,2,1,0:T(8,128)(2,1)S(1)} %get-tuple-element.9), channel_id=1, source_target_pairs={{1,0},{2,1},{3,2},{0,3},{5,4},{6,5},{7,6},{4,7},{9,8},{10,9},{11,1... | collective-permute-start | bytes 1327112 | tf_op jit(solution)/shard_map/ppermute | solution.py:221
  55.9 38.4 %collective-permute-start.8 = (bf16[2,3,144,256]{3,2,1,0:T(8,128)(2,1)S(1)}, bf16[2,3,144,256]{3,2,1,0:T(8,128)(2,1)S(1)}, u32[]{:S(2)}, u32[]{:S(2)}) collective-permute-start(bf16[2,3,144,256]{3,2,1,0:T(8,128)(2,1)S(1)} %get-tuple-element.9), channel_id=1, source_target_pairs={{2,0},{3,1},{0,2},{1,3},{6,4},{7,5},{4,6},{5,7},{10,8},{11,9},{8,1... | collective-permute-start | bytes 1327112 | tf_op jit(solution)/shard_map/ppermute | solution.py:221
  55.9 38.4 %collective-permute-start.9 = (bf16[2,3,144,256]{3,2,1,0:T(8,128)(2,1)S(1)}, bf16[2,3,144,256]{3,2,1,0:T(8,128)(2,1)S(1)}, u32[]{:S(2)}, u32[]{:S(2)}) collective-permute-start(bf16[2,3,144,256]{3,2,1,0:T(8,128)(2,1)S(1)} %get-tuple-element.9), channel_id=1, source_target_pairs={{3,0},{0,1},{1,2},{2,3},{7,4},{4,5},{5,6},{6,7},{11,8},{8,9},{9,10... | collective-permute-start | bytes 1327112 | tf_op jit(solution)/shard_map/ppermute | solution.py:221
  94.6 75.7 %copy-start = (bf16[2,12,144,256]{3,2,1,0:T(8,128)(2,1)}, bf16[2,12,144,256]{3,2,1,0:T(8,128)(2,1)S(1)}, u32[]{:S(2)}) copy-start(bf16[2,12,144,256]{3,2,1,0:T(8,128)(2,1)S(1)} %pad_maximum_fusion.1.refs_1_) | copy-start | bytes 5308420
  94.6 40.4 %collective-permute-start.10 = (bf16[2,12,144,256]{3,2,1,0:T(8,128)(2,1)S(1)}, bf16[2,12,144,256]{3,2,1,0:T(8,128)(2,1)}, u32[]{:S(2)}, u32[]{:S(2)}) collective-permute-start(bf16[2,12,144,256]{3,2,1,0:T(8,128)(2,1)S(1)} %pad_maximum_fusion.1.refs_1_), channel_id=1, source_target_pairs={{0,8},{4,12},{8,0},{12,4},{16,24},{20,28},{24,16},{28,20},{1,9},{5... | collective-permute-start | bytes 5308424 | tf_op jit(solution)/shard_map/ppermute | solution.py:225
  96.1 40.1 %collective-permute-start.12 = (bf16[2,12,144,256]{3,2,1,0:T(8,128)(2,1)S(1)}, bf16[2,12,144,256]{3,2,1,0:T(8,128)(2,1)}, u32[]{:S(2)}, u32[]{:S(2)}) collective-permute-start(bf16[2,12,144,256]{3,2,1,0:T(8,128)(2,1)S(1)} %pad_maximum_fusion.1.refs_1_), channel_id=1, source_target_pairs={{0,16},{4,20},{8,24},{12,28},{16,0},{20,4},{24,8},{28,12},{1,17},{... | collective-permute-start | bytes 5308424 | tf_op jit(solution)/shard_map/ppermute | solution.py:225
  96.9 78.0 %collective-permute-start.18 = (bf16[2,12,144,256]{3,2,1,0:T(8,128)(2,1)S(1)}, bf16[2,12,144,256]{3,2,1,0:T(8,128)(2,1)}, u32[]{:S(2)}, u32[]{:S(2)}) collective-permute-start(bf16[2,12,144,256]{3,2,1,0:T(8,128)(2,1)S(1)} %pad_maximum_fusion.1.refs_1_), channel_id=1, source_target_pairs={{0,4},{4,0},{8,12},{12,8},{16,20},{20,16},{24,28},{28,24},{1,5},{5... | collective-permute-start | bytes 5308424 | tf_op jit(solution)/shard_map/ppermute | solution.py:225
  96.9 41.8 %collective-permute-start = (bf16[2,3,144,256]{3,2,1,0:T(8,128)(2,1)S(1)}, bf16[2,3,144,256]{3,2,1,0:T(8,128)(2,1)S(1)}, u32[]{:S(2)}, u32[]{:S(2)}) collective-permute-start(bf16[2,3,144,256]{3,2,1,0:T(8,128)(2,1)S(1)} %get-tuple-element.10), channel_id=1, source_target_pairs={{1,0},{2,1},{3,2},{0,3},{5,4},{6,5},{7,6},{4,7},{9,8},{10,9},{11,1... | collective-permute-start | bytes 1327112 | tf_op jit(solution)/shard_map/ppermute | solution.py:221
  135.0 64.7 %collective-permute-start.16 = (bf16[2,12,144,256]{3,2,1,0:T(8,128)(2,1)}, bf16[2,12,144,256]{3,2,1,0:T(8,128)(2,1)}, u32[]{:S(2)}, u32[]{:S(2)}) collective-permute-start(bf16[2,12,144,256]{3,2,1,0:T(8,128)(2,1)} %collective-permute-done.10.refs_1_), channel_id=1, source_target_pairs={{0,4},{4,0},{8,12},{12,8},{16,20},{20,16},{24,28},{28,24},{1,5},{5... | collective-permute-start | bytes 5308424 | tf_op jit(solution)/shard_map/ppermute | solution.py:225
  136.2 63.5 %collective-permute-start.17 = (bf16[2,12,144,256]{3,2,1,0:T(8,128)(2,1)}, bf16[2,12,144,256]{3,2,1,0:T(8,128)(2,1)}, u32[]{:S(2)}, u32[]{:S(2)}) collective-permute-start(bf16[2,12,144,256]{3,2,1,0:T(8,128)(2,1)} %collective-permute-done.12.refs_2_), channel_id=1, source_target_pairs={{0,4},{4,0},{8,12},{12,8},{16,20},{20,16},{24,28},{28,24},{1,5},{5... | collective-permute-start | bytes 5308424 | tf_op jit(solution)/shard_map/ppermute | solution.py:225
  136.2 32.6 %collective-permute-start.1 = (bf16[2,3,144,256]{3,2,1,0:T(8,128)(2,1)}, bf16[2,3,144,256]{3,2,1,0:T(8,128)(2,1)S(1)}, u32[]{:S(2)}, u32[]{:S(2)}) collective-permute-start(bf16[2,3,144,256]{3,2,1,0:T(8,128)(2,1)} %get-tuple-element.11), channel_id=1, source_target_pairs={{2,0},{3,1},{0,2},{1,3},{6,4},{7,5},{4,6},{5,7},{10,8},{11,9},{8,1... | collective-permute-start | bytes 1327112 | tf_op jit(solution)/shard_map/ppermute | solution.py:221
  138.7 30.2 %collective-permute-start.2 = (bf16[2,3,144,256]{3,2,1,0:T(8,128)(2,1)}, bf16[2,3,144,256]{3,2,1,0:T(8,128)(2,1)S(1)}, u32[]{:S(2)}, u32[]{:S(2)}) collective-permute-start(bf16[2,3,144,256]{3,2,1,0:T(8,128)(2,1)} %get-tuple-element.12), channel_id=1, source_target_pairs={{3,0},{0,1},{1,2},{2,3},{7,4},{4,5},{5,6},{6,7},{11,8},{8,9},{9,10... | collective-permute-start | bytes 1327112 | tf_op jit(solution)/shard_map/ppermute | solution.py:221
  171.5 27.7 %collective-permute-start.11 = (bf16[1,12,144,256]{3,2,1,0:T(8,128)(2,1)S(1)}, bf16[1,12,144,256]{3,2,1,0:T(8,128)(2,1)}, u32[]{:S(2)}, u32[]{:S(2)}) collective-permute-start(bf16[1,12,144,256]{3,2,1,0:T(8,128)(2,1)S(1)} %slice.28), channel_id=1, source_target_pairs={{0,16},{4,20},{8,24},{12,28},{16,0},{20,4},{24,8},{28,12},{1,17},{... | collective-permute-start | bytes 2654216 | tf_op jit(solution)/shard_map/ppermute | solution.py:225
  173.5 25.7 %collective-permute-start.13 = (bf16[1,12,144,256]{3,2,1,0:T(8,128)(2,1)S(1)}, bf16[1,12,144,256]{3,2,1,0:T(8,128)(2,1)}, u32[]{:S(2)}, u32[]{:S(2)}) collective-permute-start(bf16[1,12,144,256]{3,2,1,0:T(8,128)(2,1)S(1)} %slice.29), channel_id=1, source_target_pairs={{0,8},{4,12},{8,0},{12,4},{16,24},{20,28},{24,16},{28,20},{1,9},{5... | collective-permute-start | bytes 2654216 | tf_op jit(solution)/shard_map/ppermute | solution.py:225
  199.2 45.3 %collective-permute-start.14 = (bf16[1,12,144,256]{3,2,1,0:T(8,128)(2,1)}, bf16[1,12,144,256]{3,2,1,0:T(8,128)(2,1)S(1)}, u32[]{:S(2)}, u32[]{:S(2)}) collective-permute-start(bf16[1,12,144,256]{3,2,1,0:T(8,128)(2,1)} %collective-permute-done.11.refs_1_), channel_id=1, source_target_pairs={{0,4},{4,0},{8,12},{12,8},{16,20},{20,16},{24,28},{28,24},{1,5},{5... | collective-permute-start | bytes 2654216 | tf_op jit(solution)/shard_map/ppermute | solution.py:225
  199.2 45.3 %collective-permute-start.15 = (bf16[1,12,144,256]{3,2,1,0:T(8,128)(2,1)}, bf16[1,12,144,256]{3,2,1,0:T(8,128)(2,1)S(1)}, u32[]{:S(2)}, u32[]{:S(2)}) collective-permute-start(bf16[1,12,144,256]{3,2,1,0:T(8,128)(2,1)} %collective-permute-done.13.refs_2_), channel_id=1, source_target_pairs={{0,4},{4,0},{8,12},{12,8},{16,20},{20,16},{24,28},{28,24},{1,5},{5... | collective-permute-start | bytes 2654216 | tf_op jit(solution)/shard_map/ppermute | solution.py:225
  244.5 0.9 copy-start.2
  245.4 1.0 copy-start.3
  274.9 13.6 %collective-permute-start.19 = (bf16[2,3,144,256]{3,2,1,0:T(8,128)(2,1)}, bf16[2,3,144,256]{3,2,1,0:T(8,128)(2,1)S(1)}, u32[]{:S(2)}, u32[]{:S(2)}) collective-permute-start(bf16[2,3,144,256]{3,2,1,0:T(8,128)(2,1)} %get-tuple-element.8), channel_id=1, source_target_pairs={{1,0},{2,1},{3,2},{0,3},{5,4},{6,5},{7,6},{4,7},{9,8},{10,9},{11,1... | collective-permute-start | bytes 1327112 | tf_op jit(solution)/shard_map/ppermute | solution.py:221
  274.9 38.7 %collective-permute-start.20 = (bf16[2,3,144,256]{3,2,1,0:T(8,128)(2,1)}, bf16[2,3,144,256]{3,2,1,0:T(8,128)(2,1)S(1)}, u32[]{:S(2)}, u32[]{:S(2)}) collective-permute-start(bf16[2,3,144,256]{3,2,1,0:T(8,128)(2,1)} %get-tuple-element.7), channel_id=1, source_target_pairs={{2,0},{3,1},{0,2},{1,3},{6,4},{7,5},{4,6},{5,7},{10,8},{11,9},{8,1... | collective-permute-start | bytes 1327112 | tf_op jit(solution)/shard_map/ppermute | solution.py:221
  274.9 39.5 %collective-permute-start.21 = (bf16[2,3,144,256]{3,2,1,0:T(8,128)(2,1)S(1)}, bf16[2,3,144,256]{3,2,1,0:T(8,128)(2,1)S(1)}, u32[]{:S(2)}, u32[]{:S(2)}) collective-permute-start(bf16[2,3,144,256]{3,2,1,0:T(8,128)(2,1)S(1)} %get-tuple-element.5), channel_id=1, source_target_pairs={{3,0},{0,1},{1,2},{2,3},{7,4},{4,5},{5,6},{6,7},{11,8},{8,9},{9,10... | collective-permute-start | bytes 1327112 | tf_op jit(solution)/shard_map/ppermute | solution.py:221

commit v2 on v1

--- a/solution.py
+++ b/solution.py
@@ -43,19 +43,67 @@
     return np.pad(array, [(0, 0)] * (array.ndim - 1) + [(0, width - array.shape[-1])])
 
 
-def pack(bands):
-    count, planes, side, _ = bands.shape
-    split = bands.reshape(count, planes // 6, 2, PACK, side, side).transpose(0, 1, 2, 4, 3, 5)
-    joined = split.reshape(count, planes // 6, 2 * side, PACK * side)
-    return jnp.pad(joined, ((0, 0), (0, 0), (0, 0), (0, LANES - PACK * side)))
-
-
-def unpack(packed, side):
-    count, steps = packed.shape[:2]
-    split = packed[..., : PACK * side].reshape(count, steps, 2, side, PACK, side)
-    return split.transpose(0, 1, 2, 4, 3, 5).reshape(count, steps * 6, side, side)
-
-
+def pack_body(in_ref, out_ref, rows, *, side):
+    slab, plane = in_ref.shape[1:]
+    pitch = rows.shape[0] // slab
+    values = in_ref[0].astype(F32)
+    for y in range(side):
+        rows[pl.ds(y, slab, stride=pitch), pl.ds(0, side)] = values[:, y * side : (y + 1) * side]
+    pad = jnp.zeros((2 * side, LANES - PACK * side), BF16)
+    for step in range(slab // 6):
+        parts = []
+        for s in range(PACK):
+            both = [rows[pl.ds((6 * step + PACK * e + s) * pitch, side), :][:, :side] for e in range(2)]
+            parts.append(jnp.concatenate(both, axis=0).astype(BF16))
+        out_ref[0, step] = jnp.concatenate(parts + [pad], axis=1)
+
+def pack(orbitals, side):
+    count, slab, plane = orbitals.shape
+    return pl.pallas_call(
+        functools.partial(pack_body, side=side),
+        grid=(count,),
+        in_specs=[pl.BlockSpec((1, slab, plane), lambda b: (b, 0, 0))],
+        out_specs=pl.BlockSpec((1, slab // 6, 2 * side, LANES), lambda b: (b, 0, 0, 0)),
+        out_shape=jax.ShapeDtypeStruct((count, slab // 6, 2 * side, LANES), BF16),
+        scratch_shapes=[pltpu.VMEM((slab * (side+4), HALF), F32)],
+        compiler_params=pltpu.CompilerParams(vmem_limit_bytes=32 * 2**20),
+    )(orbitals)
+
+def unpack_body(level_ref, *refs, side):
+    pieces, (out_ref, rows) = refs[:-2], refs[-2:]
+    slab = out_ref.shape[1]
+    pitch = rows.shape[0] // slab
+    ahead, band = pl.program_id(0), pl.program_id(1)
+    for k, piece in enumerate(pieces):
+        @pl.when(ahead == k)
+        def _():
+            for step in range(slab // 6):
+                value = piece[band, step].astype(F32)
+                for s in range(PACK):
+                    part = value[:, s * side : (s + 1) * side]
+                    for e in range(2):
+                        start = (6 * step + PACK * e + s) * pitch
+                        rows[pl.ds(start, side), pl.ds(0, side)] = part[e * side : (e + 1) * side]
+    parts = [rows[pl.ds(y, slab, stride=pitch), :][:, :side] for y in range(side)]
+    out_ref[0] = jnp.concatenate(parts, axis=1)
+
+def unpack(pieces, level, side):
+    levels = len(pieces)
+    share, steps = pieces[0].shape[:2]
+    slab = steps * 6
+    grid_spec = pltpu.PrefetchScalarGridSpec(
+        num_scalar_prefetch=1,
+        grid=(levels, share),
+        in_specs=[pl.BlockSpec(memory_space=pltpu.VMEM)] * levels,
+        out_specs=pl.BlockSpec((1, slab, side * side), lambda k, b, lv: ((lv[0] + k) % levels * share + b, 0, 0)),
+        scratch_shapes=[pltpu.VMEM((slab * (side+4), HALF), F32)],
+    )
+    return pl.pallas_call(
+        functools.partial(unpack_body, side=side),
+        grid_spec=grid_spec,
+        out_shape=jax.ShapeDtypeStruct((levels * share, slab, side * side), F32),
+        compiler_params=pltpu.CompilerParams(vmem_limit_bytes=32 * 2**20),
+    )(jnp.reshape(level, (1,)), *pieces)
 def dot(left, right):
     return lax.dot_general(left, right, (((1,), (0,)), ((), ())), preferred_element_type=F32)
 
@@ -80,13 +128,15 @@
     return groups
 
 
-def solve_body(*refs, side, pitch, sizes, groups, has_start):
+def solve_body(*refs, side, pitch, sizes, groups, has_start, cuts):
     own_ref = refs[0]
     band_refs = refs[1 : 1 + len(sizes)]
     rest = refs[1 + len(sizes) :]
     if has_start:
         start_ref, rest = rest[0], rest[1:]
-    kernel_ref, cas2_ref, ahead_ref, back_ref, thirds_ref, total_ref, low, high = rest
+    kernel_ref, cas2_ref, ahead_ref, back_ref, thirds_ref = rest[:5]
+    out_refs, (low, high, *totals) = rest[5 : 5 + cuts], rest[5 + cuts :]
+    total_ref = totals[0] if totals else out_refs[0]
     where = [(ref, k) for ref, size in zip(band_refs, sizes) for k in range(size)]
     steps = own_ref.shape[1]
     half = side // 2
@@ -170,9 +220,13 @@
         lax.fori_loop(0, steps // wide, first_two, 0)
         lax.fori_loop(0, half // many, middle_two, 0)
         lax.fori_loop(0, steps // wide, last_two, 0)
-
-
-def solve(own, bands, start, tables, side):
+    if totals:
+        for k, out_ref in enumerate(out_refs):
+            size = out_ref.shape[1]
+            out_ref[...] = total_ref[:, k * size : (k + 1) * size].astype(out_ref.dtype)
+
+
+def solve(own, bands, start, tables, side, cuts=0):
     sizes = [b.shape[0] for b in bands]
     count = own.shape[0]
     groups = make_groups(count, sum(sizes))
@@ -180,15 +234,19 @@
     vmem = pl.BlockSpec(memory_space=pltpu.VMEM)
     operands = [own, *bands] + ([] if start is None else [start]) + list(tables)
     body = functools.partial(
-        solve_body, side=side, pitch=pitch, sizes=sizes, groups=groups, has_start=start is not None
-    )
+        solve_body, side=side, pitch=pitch, sizes=sizes, groups=groups,
+        has_start=start is not None, cuts=max(cuts, 1)
+    )
+    totals = [pltpu.VMEM(own.shape, F32)] if cuts else []
+    piece = (count, own.shape[1] // max(cuts, 1)) + own.shape[2:]
+    piece = jax.ShapeDtypeStruct(piece, BF16)
     pairs = count * sum(sizes)
     return pl.pallas_call(
         body,
         in_specs=[vmem] * len(operands),
-        out_specs=vmem,
-        out_shape=jax.ShapeDtypeStruct(own.shape, F32),
-        scratch_shapes=[pltpu.VMEM((side * pitch, HALF), F32)] * 2,
+        out_specs=[vmem] * cuts if cuts else vmem,
+        out_shape=[piece] * cuts if cuts else jax.ShapeDtypeStruct(own.shape, F32),
+        scratch_shapes=[pltpu.VMEM((side * pitch, HALF), F32)] * 2 + totals,
         compiler_params=pltpu.CompilerParams(vmem_limit_bytes=60 * 2**20),
         cost_estimate=pl.CostEstimate(
             flops=pairs * 12 * side**4 * 4, bytes_accessed=10 * 2**20, transcendentals=0
@@ -240,7 +298,7 @@
         start = (level + levels - ahead) % levels * per_device
         piece = lax.dynamic_slice_in_dim(packed, start, per_device, 0)
         pieces.append(from_level(piece, ahead) if ahead else piece)
-    return jnp.concatenate(pieces, axis=1)
+    return pieces
 
 
 def whole(slab):
@@ -257,26 +315,35 @@
     for k in range(4):
         part = lax.dynamic_slice_in_dim(packed, (line ^ k) * share, share, 0)
         parts.append(flip(part, 2 * k) if k else part)
+    parts, own = lax.optimization_barrier((parts, own))
+    own = jnp.concatenate(own, axis=1)
     here = owners[core]
     there = owners[1 - core]
     mine = pick(parts, line ^ (here // 2))
     other = flip(pick(parts, line ^ (there // 2)), 1)
-    mine = whole(jnp.where(here % 2 == core, mine, other))
+    mine = jnp.where(here % 2 == core, mine, other)
+    mine = whole(mine)
     mine_x, mine_y = flip(mine, 2), flip(mine, 4)
+    total = solve(own, [mine, flip(mine, 1)], None, tables, side)
+    total, mine_x, mine_y = lax.optimization_barrier((total, mine_x, mine_y))
     cut = share // 2
     corner = [flip(mine_x[:cut], 4), flip(mine_y[cut:], 2)]
-    total = solve(own, [mine, flip(mine, 1)], None, tables, side)
     total = solve(own, [mine_x, mine_y, flip(mine_x, 1), flip(mine_y, 1)], total, tables, side)
-    return solve(own, corner + [flip(c, 1) for c in corner], total, tables, side)
+    total, *corner = lax.optimization_barrier((total, *corner))
+    levels = lax.axis_size("grid")
+    return solve(own, corner + [flip(c, 1) for c in corner], total, tables, side, levels)
 
 
 def fields_any(packed, owners, own, tables, side):
     total = None
     band = lax.axis_index("band")
+    levels = lax.axis_size("grid")
+    own = jnp.concatenate(own, axis=1)
     for r in range(owners.shape[0]):
+        cuts = levels if r == owners.shape[0] - 1 else 0
         kept = jnp.where(band == owners[r], packed, jnp.zeros_like(packed))
         bands = whole(lax.psum(kept, "band"))
-        total = solve(own, [bands], total, tables, side)
+        total = solve(own, [bands], total, tables, side, cuts)
     return total
 
 
@@ -287,20 +354,15 @@
     side = slab * levels
     per_device = band_count // levels
     tables = make_tables(side, slab, level)
-    packed = pack(orbitals.reshape(band_count, slab, side, side))
+    packed = pack(orbitals, side)
     own = own_bands(packed, per_device)
     small = lax.axis_size("band") == 8 and owners.shape[0] == 2 and band_count % 8 == 0
     fields = (fields_small if small else fields_any)(packed, owners, own, tables, side)
-    fields = fields.astype(BF16)
-    steps = slab // 6
     pieces = []
     for ahead in range(levels):
-        behind = (levels - ahead) % levels
-        piece = fields[:, behind * steps : (behind + 1) * steps]
+        piece = fields[(levels - ahead) % levels]
         pieces.append(from_level(piece, ahead) if ahead else piece)
-    ordered = jnp.concatenate(pieces + pieces, axis=0)
-    ordered = lax.dynamic_slice_in_dim(ordered, (levels - level) * per_device, band_count, 0)
-    return unpack(ordered, side).astype(F32).reshape(band_count, slab, plane)
+    return unpack(pieces, level, side)
 
 
 def solution(mesh):

time: 351 us -> 268 us (0.76)
  local copies, waits for them, and re-layouts: 64.6 us -> 15.1 us
  waiting for transfers between devices: 156 us -> 121 us
  other arithmetic: 11 us -> 1.11 us
  starting transfers between devices: 18.5 us -> 24.2 us
  Pallas kernels: 94.4 us -> 100 us
    ppermute x13, waiting for transfers between devices: 55.7 us -> 25.4 us  [flip(): lax.ppermute(value, 'band', [(b, b ^ bit) for b in range(lax.axis_size('b...]
    convert_element_type x4 -> x0, local copies, waits for them, and re-layouts: 27.8 us -> none  [body(): return unpack(ordered, side).astype(F32).reshape(band_count, slab, plane)]
    another operation x2 -> x0, local copies, waits for them, and re-layouts: 12.3 us -> none  [pack(): bands.reshape(count, planes // 6, 2, PACK, side, side)]
    reshape x2 -> x0, local copies, waits for them, and re-layouts: 9.39 us -> none  [pack(): joined = split.reshape(count, planes // 6, 2 * side, PACK * side)]
    pallas_call x3 -> x5, Pallas kernels: 94.4 us -> 100 us  [the longest x3 93.7 us: solve(): pl.pallas_call(body, in_specs=[vmem] * len(operands), out_specs=[vmem] *...]
    convert_element_type x2 -> x0, other arithmetic: 5.86 us -> none  [the longest x1 3.68 us: body(): return unpack(ordered, side).astype(F32).reshape(band_count, slab, plane)]
    ppermute x9, waiting for transfers between devices: 100 us -> 95.9 us  [from_level(): return lax.ppermute(value, 'grid', pairs)]
    ppermute x9, starting transfers between devices: 9.14 us -> 13.3 us  [from_level(): return lax.ppermute(value, 'grid', pairs)]
  transfers between devices with their start and end apart: 22 -> 22, of which waited for: 10 -> 13; matrix products, arithmetic and copies ran while one was open for 3% -> 3% of each run, Pallas kernels for 20% -> 26%
where the time goes in v2:
time: 268 us; the launch traced here: 267 us
  waiting for transfers between devices  121 us (45%)
  Pallas kernels  100 us (37%)
  starting transfers between devices  24.2 us (9%)
  local copies, waits for them, and re-layouts  15.1 us (6%)
  between operations  5.26 us (2%)
    ppermute x9, waiting for transfers between devices, from_level(): return lax.ppermute(value, 'grid', pairs)  95.9 us
    pallas_call x3, Pallas kernels, solve(): pl.pallas_call(body, in_specs=[vmem] * len(operands), out_specs=[vmem] *...  93.7 us
    ppermute x13, waiting for transfers between devices, flip(): lax.ppermute(value, 'band', [(b, b ^ bit) for b in range(lax.axis_size('b...  25.4 us
    ppermute x9, starting transfers between devices, from_level(): return lax.ppermute(value, 'grid', pairs)  13.3 us
    ppermute x13, starting transfers between devices, flip(): lax.ppermute(value, 'band', [(b, b ^ bit) for b in range(lax.axis_size('b...  10.9 us
    unnamed x24, local copies, waits for them, and re-layouts  6.9 us
  transfers between devices with their start and end apart: 22, of which 13 were waited for; matrix products, arithmetic and copies ran while one was open for 3% of the time, Pallas kernels for 26%

profile of v2, /device:TPU:0, one launch (start us, length us, event | category | flops | bytes accessed | tf_op | source)
XLA Modules:
  0.0 267.3 jit_solution(15497829776195606939)
XLA Ops:
  0.0 1.6 copy.7.in_ref
  1.6 3.0 %shard_map.64 = bf16[8,3,144,256]{3,2,1,0:T(8,128)(2,1)S(1)} custom-call(bf16[8,18,5184]{2,1,0:T(8,128)(2,1)S(1)} %copy.7.in_ref), custom_call_target="tpu_custom_call" | custom-call | tf_op jit(solution)/shard_map/pallas_call | solution.py:62
  4.7 0.0 copy-start.6
  4.7 1.2 constant_dynamic-slice_fusion.1
  5.9 2.9 %collective-permute-start = (bf16[2,3,144,256]{3,2,1,0:T(8,128)(2,1)S(1)}, bf16[2,3,144,256]{3,2,1,0:T(8,128)(2,1)S(1)}, u32[]{:S(2)}, u32[]{:S(2)}) collective-permute-start(bf16[2,3,144,256]{3,2,1,0:T(8,128)(2,1)S(1)} %get-tuple-element.47), channel_id=1, source_target_pairs={{0,8},{4,12},{8,0},{12,4},{16,24},{20,28},{24,16},{28,20},{1,9},{5... | collective-permute-start | bytes 1327112 | tf_op jit(solution)/shard_map/ppermute | solution.py:283
  8.8 1.5 collective-permute-start.1
  10.3 0.0 collective-permute-start.2
  10.3 4.1 %collective-permute-start.3 = (bf16[2,3,144,256]{3,2,1,0:T(8,128)(2,1)}, bf16[2,3,144,256]{3,2,1,0:T(8,128)(2,1)S(1)}, u32[]{:S(2)}, u32[]{:S(2)}) collective-permute-start(bf16[2,3,144,256]{3,2,1,0:T(8,128)(2,1)} %get-tuple-element.43), channel_id=1, source_target_pairs={{1,0},{2,1},{3,2},{0,3},{5,4},{6,5},{7,6},{4,7},{9,8},{10,9},{11,1... | collective-permute-start | bytes 1327112 | tf_op jit(solution)/shard_map/ppermute | solution.py:279
  14.4 0.0 collective-permute-start.4
  14.4 5.4 %collective-permute-done = bf16[2,3,144,256]{3,2,1,0:T(8,128)(2,1)S(1)} collective-permute-done((bf16[2,3,144,256]{3,2,1,0:T(8,128)(2,1)S(1)}, bf16[2,3,144,256]{3,2,1,0:T(8,128)(2,1)S(1)}, u32[]{:S(2)}, u32[]{:S(2)}) %collective-permute-start) | collective-permute-done | bytes 442400 | tf_op jit(solution)/shard_map/ppermute | solution.py:283
  19.8 2.1 collective-permute-start.5
  21.9 0.6 fusion.4
  25.1 5.0 %collective-permute-done.1 = bf16[2,3,144,256]{3,2,1,0:T(8,128)(2,1)S(1)} collective-permute-done((bf16[2,3,144,256]{3,2,1,0:T(8,128)(2,1)}, bf16[2,3,144,256]{3,2,1,0:T(8,128)(2,1)S(1)}, u32[]{:S(2)}, u32[]{:S(2)}) %collective-permute-start.1) | collective-permute-done | bytes 442400 | tf_op jit(solution)/shard_map/ppermute | solution.py:283
  30.1 0.0 collective-permute-done.2
  30.1 0.0 collective-permute-done.3
  30.1 21.5 %collective-permute-done.4 = bf16[2,3,144,256]{3,2,1,0:T(8,128)(2,1)} collective-permute-done((bf16[2,3,144,256]{3,2,1,0:T(8,128)(2,1)S(1)}, bf16[2,3,144,256]{3,2,1,0:T(8,128)(2,1)}, u32[]{:S(2)}, u32[]{:S(2)}) %collective-permute-start.4) | collective-permute-done | bytes 442400 | tf_op jit(solution)/shard_map/ppermute | solution.py:279
  51.6 0.1 select_select_fusion
  51.7 0.1 collective-permute-start.6
  54.3 0.0 collective-permute-done.6
  54.3 0.1 select_select_fusion.1
  54.4 0.0 copy-start.5
  54.5 0.1 collective-permute-start.7
  54.5 0.0 copy-start.3
  54.5 2.6 collective-permute-start.8
  57.1 1.9 collective-permute-start.9
  59.1 8.0 %collective-permute-done.7 = bf16[2,3,144,256]{3,2,1,0:T(8,128)(2,1)S(1)} collective-permute-done((bf16[2,3,144,256]{3,2,1,0:T(8,128)(2,1)S(1)}, bf16[2,3,144,256]{3,2,1,0:T(8,128)(2,1)S(1)}, u32[]{:S(2)}, u32[]{:S(2)}) %collective-permute-start.7) | collective-permute-done | bytes 442400 | tf_op jit(solution)/shard_map/ppermute | solution.py:279
  67.1 29.2 %collective-permute-done.8 = bf16[2,3,144,256]{3,2,1,0:T(8,128)(2,1)S(1)} collective-permute-done((bf16[2,3,144,256]{3,2,1,0:T(8,128)(2,1)S(1)}, bf16[2,3,144,256]{3,2,1,0:T(8,128)(2,1)S(1)}, u32[]{:S(2)}, u32[]{:S(2)}) %collective-permute-start.8) | collective-permute-done | bytes 442400 | tf_op jit(solution)/shard_map/ppermute | solution.py:279
  96.3 0.2 pad_maximum_fusion.refs_1_
  96.6 0.1 collective-permute-start.10
  96.6 1.6 collective-permute-start.11
  98.2 1.5 collective-permute-start.12
  99.7 0.7 fusion.2
  100.5 0.7 copy.8.refs_5_.refs_8_
  101.3 1.0 constant_dynamic-update-slice_fusion.1
  102.3 1.0 constant_dynamic-update-slice_fusion.refs_0_
  103.4 0.0 copy-start.4
  103.4 0.0 collective-permute-done.10.refs_2_
  103.4 1.2 copy-done.4
  104.6 24.4 %shard_map.65.refs_5_ = f32[2,12,144,256]{3,2,1,0:T(8,128)} custom-call(bf16[2,12,144,256]{3,2,1,0:T(8,128)(2,1)} %copy-done.4, bf16[2,12,144,256]{3,2,1,0:T(8,128)(2,1)} %copy-done.1, bf16[2,12,144,256]{3,2,1,0:T(8,128)(2,1)} %collective-permute-done.10.refs_2_, f32[36,144,256]{2,1,0:T(8,128)} %constant.101.clone.refs_3_.refs_6_, ...), custom_call_target="tpu_custom_call" | custom-call | flops 10319560704 | bytes 10485760 | tf_op jit(solution)/shard_map/pallas_call | solution.py:244
  128.9 8.8 %collective-permute-done.11.refs_1_ = bf16[2,12,144,256]{3,2,1,0:T(8,128)(2,1)} collective-permute-done((bf16[2,12,144,256]{3,2,1,0:T(8,128)(2,1)S(1)}, bf16[2,12,144,256]{3,2,1,0:T(8,128)(2,1)}, u32[]{:S(2)}, u32[]{:S(2)}) %collective-permute-start.11) | collective-permute-done | bytes 1769504 | tf_op jit(solution)/shard_map/ppermute | solution.py:283
  137.8 1.2 collective-permute-done.12.refs_2_
  139.0 0.0 collective-permute-start.13
  139.0 0.5 collective-permute-start.14
  139.5 1.2 slice.6
  140.7 1.2 slice.7
  142.0 1.6 collective-permute-start.15
  143.5 0.5 collective-permute-start.16
  144.1 1.3 collective-permute-done.13.refs_3_
  145.4 0.2 collective-permute-done.14.refs_4_
  145.6 1.0 copy-done.7
  146.6 44.7 %shard_map.66.refs_5_ = f32[2,12,144,256]{3,2,1,0:T(8,128)} custom-call(bf16[2,12,144,256]{3,2,1,0:T(8,128)(2,1)} %copy-done.4, bf16[2,12,144,256]{3,2,1,0:T(8,128)(2,1)} %collective-permute-done.11.refs_1_, bf16[2,12,144,256]{3,2,1,0:T(8,128)(2,1)} %collective-permute-done.12.refs_2_, bf16[2,12,144,256]{3,2,1,0:T(8,128)(2,1)} %copy-done.7, ...), custom_call_target="tpu_custom_call" | custom-call | flops 20639121408 | bytes 10485760 | tf_op jit(solution)/shard_map/pallas_call | solution.py:244
  191.3 0.2 collective-permute-start.17
  191.5 0.4 collective-permute-start.18
  191.9 2.1 collective-permute-done.17.refs_3_
  194.0 1.3 collective-permute-done.18.refs_4_
  195.3 0.9 copy-done.9
  196.2 24.6 %shard_map.67 = (bf16[2,3,144,256]{3,2,1,0:T(8,128)(2,1)}, bf16[2,3,144,256]{3,2,1,0:T(8,128)(2,1)}, bf16[2,3,144,256]{3,2,1,0:T(8,128)(2,1)}, bf16[2,3,144,256]{3,2,1,0:T(8,128)(2,1)}) custom-call(bf16[2,12,144,256]{3,2,1,0:T(8,128)(2,1)} %copy-done.4, bf16[1,12,144,256]{3,2,1,0:T(8,128)(2,1)} %collective-permute-done.15.refs_1_, ...), custom_call_target="tpu_custom_call" | custom-call | flops 10319560704 | bytes 10485760 | tf_op jit(solution)/shard_map/pallas_call | solution.py:244
  220.9 0.4 collective-permute-start.20
  221.3 2.0 collective-permute-start.21
  223.3 11.3 %collective-permute-done.19.refs_1_ = bf16[2,3,144,256]{3,2,1,0:T(8,128)(2,1)S(1)} collective-permute-done((bf16[2,3,144,256]{3,2,1,0:T(8,128)(2,1)}, bf16[2,3,144,256]{3,2,1,0:T(8,128)(2,1)S(1)}, u32[]{:S(2)}, u32[]{:S(2)}) %collective-permute-start.19) | collective-permute-done | bytes 442400 | tf_op jit(solution)/shard_map/ppermute | solution.py:279
  234.6 25.8 %collective-permute-done.20.refs_2_ = bf16[2,3,144,256]{3,2,1,0:T(8,128)(2,1)S(1)} collective-permute-done((bf16[2,3,144,256]{3,2,1,0:T(8,128)(2,1)}, bf16[2,3,144,256]{3,2,1,0:T(8,128)(2,1)S(1)}, u32[]{:S(2)}, u32[]{:S(2)}) %collective-permute-start.20) | collective-permute-done | bytes 442400 | tf_op jit(solution)/shard_map/ppermute | solution.py:279
  260.4 1.0 copy-done
  261.4 3.7 %shard_map.68 = f32[8,18,5184]{2,1,0:T(8,128)S(1)} custom-call(s32[1]{0:T(128)} %bitcast.level_ref, bf16[2,3,144,256]{3,2,1,0:T(8,128)(2,1)S(1)} %copy-done, bf16[2,3,144,256]{3,2,1,0:T(8,128)(2,1)S(1)} %collective-permute-done.19.refs_1_, bf16[2,3,144,256]{3,2,1,0:T(8,128)(2,1)S(1)} %collective-permute-done.20.refs_2_, ...), custom_call_target="tpu_custom_call" | custom-call | tf_op jit(solution)/shard_map/pallas_call | solution.py:101
  265.1 2.2 copy.11
  (21 shorter events, 0.1 us)
Async XLA Ops:
  4.7 17.3 %copy-start.6 = (s32[2]{0:T(128)S(1)}, s32[2]{0:T(128)}, u32[]{:S(2)}) copy-start(s32[2]{0:T(128)} %param.7) | copy-start | bytes 28
  5.9 13.9 %collective-permute-start = (bf16[2,3,144,256]{3,2,1,0:T(8,128)(2,1)S(1)}, bf16[2,3,144,256]{3,2,1,0:T(8,128)(2,1)S(1)}, u32[]{:S(2)}, u32[]{:S(2)}) collective-permute-start(bf16[2,3,144,256]{3,2,1,0:T(8,128)(2,1)S(1)} %get-tuple-element.47), channel_id=1, source_target_pairs={{0,8},{4,12},{8,0},{12,4},{16,24},{20,28},{24,16},{28,20},{1,9},{5... | collective-permute-start | bytes 1327112 | tf_op jit(solution)/shard_map/ppermute | solution.py:283
  8.8 21.3 %collective-permute-start.1 = (bf16[2,3,144,256]{3,2,1,0:T(8,128)(2,1)}, bf16[2,3,144,256]{3,2,1,0:T(8,128)(2,1)S(1)}, u32[]{:S(2)}, u32[]{:S(2)}) collective-permute-start(bf16[2,3,144,256]{3,2,1,0:T(8,128)(2,1)} %get-tuple-element.46), channel_id=1, source_target_pairs={{0,16},{4,20},{8,24},{12,28},{16,0},{20,4},{24,8},{28,12},{1,17},{... | collective-permute-start | bytes 1327112 | tf_op jit(solution)/shard_map/ppermute | solution.py:283
  10.3 19.8 %collective-permute-start.2 = (bf16[2,3,144,256]{3,2,1,0:T(8,128)(2,1)}, bf16[2,3,144,256]{3,2,1,0:T(8,128)(2,1)S(1)}, u32[]{:S(2)}, u32[]{:S(2)}) collective-permute-start(bf16[2,3,144,256]{3,2,1,0:T(8,128)(2,1)} %get-tuple-element.45), channel_id=1, source_target_pairs={{0,24},{4,28},{8,16},{12,20},{16,8},{20,12},{24,0},{28,4},{1,25},{... | collective-permute-start | bytes 1327112 | tf_op jit(solution)/shard_map/ppermute | solution.py:283
  10.3 19.8 %collective-permute-start.3 = (bf16[2,3,144,256]{3,2,1,0:T(8,128)(2,1)}, bf16[2,3,144,256]{3,2,1,0:T(8,128)(2,1)S(1)}, u32[]{:S(2)}, u32[]{:S(2)}) collective-permute-start(bf16[2,3,144,256]{3,2,1,0:T(8,128)(2,1)} %get-tuple-element.43), channel_id=1, source_target_pairs={{1,0},{2,1},{3,2},{0,3},{5,4},{6,5},{7,6},{4,7},{9,8},{10,9},{11,1... | collective-permute-start | bytes 1327112 | tf_op jit(solution)/shard_map/ppermute | solution.py:279
  14.4 37.2 %collective-permute-start.4 = (bf16[2,3,144,256]{3,2,1,0:T(8,128)(2,1)S(1)}, bf16[2,3,144,256]{3,2,1,0:T(8,128)(2,1)}, u32[]{:S(2)}, u32[]{:S(2)}) collective-permute-start(bf16[2,3,144,256]{3,2,1,0:T(8,128)(2,1)S(1)} %get-tuple-element.42), channel_id=1, source_target_pairs={{2,0},{3,1},{0,2},{1,3},{6,4},{7,5},{4,6},{5,7},{10,8},{11,9},{8,1... | collective-permute-start | bytes 1327112 | tf_op jit(solution)/shard_map/ppermute | solution.py:279
  19.8 31.8 %collective-permute-start.5 = (bf16[2,3,144,256]{3,2,1,0:T(8,128)(2,1)S(1)}, bf16[2,3,144,256]{3,2,1,0:T(8,128)(2,1)}, u32[]{:S(2)}, u32[]{:S(2)}) collective-permute-start(bf16[2,3,144,256]{3,2,1,0:T(8,128)(2,1)S(1)} %get-tuple-element.41), channel_id=1, source_target_pairs={{3,0},{0,1},{1,2},{2,3},{7,4},{4,5},{5,6},{6,7},{11,8},{8,9},{9,10... | collective-permute-start | bytes 1327112 | tf_op jit(solution)/shard_map/ppermute | solution.py:279
  30.1 24.3 %copy-start.2 = (bf16[2,3,144,256]{3,2,1,0:T(8,128)(2,1)}, bf16[2,3,144,256]{3,2,1,0:T(8,128)(2,1)S(1)}, u32[]{:S(2)}) copy-start(bf16[2,3,144,256]{3,2,1,0:T(8,128)(2,1)S(1)} %collective-permute-done.3) | copy-start | bytes 1327108
  51.7 2.6 collective-permute-start.6
  54.4 45.3 %copy-start.5 = (bf16[144,72]{1,0:T(8,128)(2,1)S(1)}, bf16[144,72]{1,0:T(8,128)(2,1)}, u32[]{:S(2)}) copy-start(bf16[144,72]{1,0:T(8,128)(2,1)} %constant.108) | copy-start | bytes 62212
  54.5 12.6 %collective-permute-start.7 = (bf16[2,3,144,256]{3,2,1,0:T(8,128)(2,1)S(1)}, bf16[2,3,144,256]{3,2,1,0:T(8,128)(2,1)S(1)}, u32[]{:S(2)}, u32[]{:S(2)}) collective-permute-start(bf16[2,3,144,256]{3,2,1,0:T(8,128)(2,1)S(1)} %select_select_fusion.1), channel_id=1, source_target_pairs={{1,0},{2,1},{3,2},{0,3},{5,4},{6,5},{7,6},{4,7},{9,8},{10,9},{11,1... | collective-permute-start | bytes 1327112 | tf_op jit(solution)/shard_map/ppermute | solution.py:279
  54.5 46.7 %copy-start.3 = (bf16[2,3,144,256]{3,2,1,0:T(8,128)(2,1)S(1)}, bf16[2,3,144,256]{3,2,1,0:T(8,128)(2,1)}, u32[]{:S(2)}) copy-start(bf16[2,3,144,256]{3,2,1,0:T(8,128)(2,1)} %copy-done.2) | copy-start | bytes 1327108
  54.5 41.8 %collective-permute-start.8 = (bf16[2,3,144,256]{3,2,1,0:T(8,128)(2,1)S(1)}, bf16[2,3,144,256]{3,2,1,0:T(8,128)(2,1)S(1)}, u32[]{:S(2)}, u32[]{:S(2)}) collective-permute-start(bf16[2,3,144,256]{3,2,1,0:T(8,128)(2,1)S(1)} %select_select_fusion.1), channel_id=1, source_target_pairs={{2,0},{3,1},{0,2},{1,3},{6,4},{7,5},{4,6},{5,7},{10,8},{11,9},{8,1... | collective-permute-start | bytes 1327112 | tf_op jit(solution)/shard_map/ppermute | solution.py:279
  57.1 39.2 %collective-permute-start.9 = (bf16[2,3,144,256]{3,2,1,0:T(8,128)(2,1)S(1)}, bf16[2,3,144,256]{3,2,1,0:T(8,128)(2,1)S(1)}, u32[]{:S(2)}, u32[]{:S(2)}) collective-permute-start(bf16[2,3,144,256]{3,2,1,0:T(8,128)(2,1)S(1)} %select_select_fusion.1), channel_id=1, source_target_pairs={{3,0},{0,1},{1,2},{2,3},{7,4},{4,5},{5,6},{6,7},{11,8},{8,9},{9,10... | collective-permute-start | bytes 1327112 | tf_op jit(solution)/shard_map/ppermute | solution.py:279
  96.5 6.8 %copy-start.1 = (bf16[2,12,144,256]{3,2,1,0:T(8,128)(2,1)}, bf16[2,12,144,256]{3,2,1,0:T(8,128)(2,1)S(1)}, u32[]{:S(2)}) copy-start(bf16[2,12,144,256]{3,2,1,0:T(8,128)(2,1)S(1)} %pad_maximum_fusion.refs_1_) | copy-start | bytes 5308420
  96.6 6.8 %collective-permute-start.10 = (bf16[2,12,144,256]{3,2,1,0:T(8,128)(2,1)S(1)}, bf16[2,12,144,256]{3,2,1,0:T(8,128)(2,1)}, u32[]{:S(2)}, u32[]{:S(2)}) collective-permute-start(bf16[2,12,144,256]{3,2,1,0:T(8,128)(2,1)S(1)} %pad_maximum_fusion.refs_1_), channel_id=1, source_target_pairs={{0,4},{4,0},{8,12},{12,8},{16,20},{20,16},{24,28},{28,24},{1,5},{5... | collective-permute-start | bytes 5308424 | tf_op jit(solution)/shard_map/ppermute | solution.py:283
  96.6 41.1 %collective-permute-start.11 = (bf16[2,12,144,256]{3,2,1,0:T(8,128)(2,1)S(1)}, bf16[2,12,144,256]{3,2,1,0:T(8,128)(2,1)}, u32[]{:S(2)}, u32[]{:S(2)}) collective-permute-start(bf16[2,12,144,256]{3,2,1,0:T(8,128)(2,1)S(1)} %pad_maximum_fusion.refs_1_), channel_id=1, source_target_pairs={{0,8},{4,12},{8,0},{12,4},{16,24},{20,28},{24,16},{28,20},{1,9},{5... | collective-permute-start | bytes 5308424 | tf_op jit(solution)/shard_map/ppermute | solution.py:283
  98.2 40.8 %collective-permute-start.12 = (bf16[2,12,144,256]{3,2,1,0:T(8,128)(2,1)S(1)}, bf16[2,12,144,256]{3,2,1,0:T(8,128)(2,1)}, u32[]{:S(2)}, u32[]{:S(2)}) collective-permute-start(bf16[2,12,144,256]{3,2,1,0:T(8,128)(2,1)S(1)} %pad_maximum_fusion.refs_1_), channel_id=1, source_target_pairs={{0,16},{4,20},{8,24},{12,28},{16,0},{20,4},{24,8},{28,12},{1,17},{... | collective-permute-start | bytes 5308424 | tf_op jit(solution)/shard_map/ppermute | solution.py:283
  103.4 1.2 copy-start.4
  139.0 6.4 %collective-permute-start.13 = (bf16[2,12,144,256]{3,2,1,0:T(8,128)(2,1)}, bf16[2,12,144,256]{3,2,1,0:T(8,128)(2,1)S(1)}, u32[]{:S(2)}, u32[]{:S(2)}) collective-permute-start(bf16[2,12,144,256]{3,2,1,0:T(8,128)(2,1)} %collective-permute-done.11.refs_1_), channel_id=1, source_target_pairs={{0,4},{4,0},{8,12},{12,8},{16,20},{20,16},{24,28},{28,24},{1,5},{5... | collective-permute-start | bytes 5308424 | tf_op jit(solution)/shard_map/ppermute | solution.py:283
  139.0 6.6 %collective-permute-start.14 = (bf16[2,12,144,256]{3,2,1,0:T(8,128)(2,1)}, bf16[2,12,144,256]{3,2,1,0:T(8,128)(2,1)}, u32[]{:S(2)}, u32[]{:S(2)}) collective-permute-start(bf16[2,12,144,256]{3,2,1,0:T(8,128)(2,1)} %collective-permute-done.12.refs_2_), channel_id=1, source_target_pairs={{0,4},{4,0},{8,12},{12,8},{16,20},{20,16},{24,28},{28,24},{1,5},{5... | collective-permute-start | bytes 5308424 | tf_op jit(solution)/shard_map/ppermute | solution.py:283
  142.0 49.4 %collective-permute-start.15 = (bf16[1,12,144,256]{3,2,1,0:T(8,128)(2,1)S(1)}, bf16[1,12,144,256]{3,2,1,0:T(8,128)(2,1)}, u32[]{:S(2)}, u32[]{:S(2)}) collective-permute-start(bf16[1,12,144,256]{3,2,1,0:T(8,128)(2,1)S(1)} %slice.6), channel_id=1, source_target_pairs={{0,16},{4,20},{8,24},{12,28},{16,0},{20,4},{24,8},{28,12},{1,17},{... | collective-permute-start | bytes 2654216 | tf_op jit(solution)/shard_map/ppermute | solution.py:283
  143.5 47.8 %collective-permute-start.16 = (bf16[1,12,144,256]{3,2,1,0:T(8,128)(2,1)S(1)}, bf16[1,12,144,256]{3,2,1,0:T(8,128)(2,1)}, u32[]{:S(2)}, u32[]{:S(2)}) collective-permute-start(bf16[1,12,144,256]{3,2,1,0:T(8,128)(2,1)S(1)} %slice.7), channel_id=1, source_target_pairs={{0,8},{4,12},{8,0},{12,4},{16,24},{20,28},{24,16},{28,20},{1,9},{5... | collective-permute-start | bytes 2654216 | tf_op jit(solution)/shard_map/ppermute | solution.py:283
  145.4 1.2 copy-start.7
  191.3 2.7 %collective-permute-start.17 = (bf16[1,12,144,256]{3,2,1,0:T(8,128)(2,1)}, bf16[1,12,144,256]{3,2,1,0:T(8,128)(2,1)S(1)}, u32[]{:S(2)}, u32[]{:S(2)}) collective-permute-start(bf16[1,12,144,256]{3,2,1,0:T(8,128)(2,1)} %collective-permute-done.15.refs_1_), channel_id=1, source_target_pairs={{0,4},{4,0},{8,12},{12,8},{16,20},{20,16},{24,28},{28,24},{1,5},{5... | collective-permute-start | bytes 2654216 | tf_op jit(solution)/shard_map/ppermute | solution.py:283
  191.5 3.8 %collective-permute-start.18 = (bf16[1,12,144,256]{3,2,1,0:T(8,128)(2,1)}, bf16[1,12,144,256]{3,2,1,0:T(8,128)(2,1)S(1)}, u32[]{:S(2)}, u32[]{:S(2)}) collective-permute-start(bf16[1,12,144,256]{3,2,1,0:T(8,128)(2,1)} %collective-permute-done.16.refs_2_), channel_id=1, source_target_pairs={{0,4},{4,0},{8,12},{12,8},{16,20},{20,16},{24,28},{28,24},{1,5},{5... | collective-permute-start | bytes 2654216 | tf_op jit(solution)/shard_map/ppermute | solution.py:283
  194.0 1.3 copy-start.8
  195.3 0.9 copy-start.9
  220.9 13.7 %collective-permute-start.19 = (bf16[2,3,144,256]{3,2,1,0:T(8,128)(2,1)}, bf16[2,3,144,256]{3,2,1,0:T(8,128)(2,1)S(1)}, u32[]{:S(2)}, u32[]{:S(2)}) collective-permute-start(bf16[2,3,144,256]{3,2,1,0:T(8,128)(2,1)} %get-tuple-element.38), channel_id=1, source_target_pairs={{1,0},{2,1},{3,2},{0,3},{5,4},{6,5},{7,6},{4,7},{9,8},{10,9},{11,1... | collective-permute-start | bytes 1327112 | tf_op jit(solution)/shard_map/ppermute | solution.py:279
  220.9 39.5 %collective-permute-start.20 = (bf16[2,3,144,256]{3,2,1,0:T(8,128)(2,1)}, bf16[2,3,144,256]{3,2,1,0:T(8,128)(2,1)S(1)}, u32[]{:S(2)}, u32[]{:S(2)}) collective-permute-start(bf16[2,3,144,256]{3,2,1,0:T(8,128)(2,1)} %get-tuple-element.39), channel_id=1, source_target_pairs={{2,0},{3,1},{0,2},{1,3},{6,4},{7,5},{4,6},{5,7},{10,8},{11,9},{8,1... | collective-permute-start | bytes 1327112 | tf_op jit(solution)/shard_map/ppermute | solution.py:279
  221.3 39.1 %collective-permute-start.21 = (bf16[2,3,144,256]{3,2,1,0:T(8,128)(2,1)}, bf16[2,3,144,256]{3,2,1,0:T(8,128)(2,1)S(1)}, u32[]{:S(2)}, u32[]{:S(2)}) collective-permute-start(bf16[2,3,144,256]{3,2,1,0:T(8,128)(2,1)} %get-tuple-element.40), channel_id=1, source_target_pairs={{3,0},{0,1},{1,2},{2,3},{7,4},{4,5},{5,6},{6,7},{11,8},{8,9},{9,10... | collective-permute-start | bytes 1327112 | tf_op jit(solution)/shard_map/ppermute | solution.py:279
  260.4 1.0 copy-start

commit v3 on v1

v3 whole, which is shorter than its diff:
```python
import functools
import math

import jax
import jax.numpy as jnp
import numpy as np
from jax import lax
from jax.experimental import pallas as pl
from jax.experimental.pallas import tpu as pltpu
from jax.sharding import PartitionSpec as P

box_length = 12.0
screening = 0.106
BF16 = jnp.bfloat16
F32 = jnp.float32
LANES = 256
HALF = 128
PACK = 3


def cas_table(length):
    points = np.arange(length)
    products = points[:, None] * points[None, :] % length
    phase = products.astype(np.float32) * np.float32(2.0 * math.pi / length)
    return (np.cos(phase) + np.sin(phase)).astype(BF16)


def screened_kernel(length):
    points = np.arange(length)
    folded = np.minimum(points, length - points).astype(np.float32)
    squares = folded * folded
    factor = np.float32((2.0 * math.pi / box_length) ** 2)
    wave_sq = factor * (squares[:, None, None] + squares[None, :, None] + squares[None, None, :])
    positive = np.where(wave_sq > 0.0, wave_sq, np.float32(1.0))
    screen = np.float32(4.0 * math.pi) * (
        np.float32(1.0) - np.exp(-positive / np.float32(4.0 * screening * screening))
    )
    screen = screen / positive / np.float32(length**3)
    return np.where(wave_sq > 0.0, screen, np.float32(0.0)).astype(np.float32)


def padded(array, width):
    return np.pad(array, [(0, 0)] * (array.ndim - 1) + [(0, width - array.shape[-1])])


def pack_body(in_ref, out_ref, rows, *, side):
    planes, bands = in_ref.shape[:2]
    pitch = rows.shape[0] // (planes * bands)
    for x in range(planes):
        values = in_ref[x].astype(F32)
        for y in range(side):
            part = values[:, y * side : (y + 1) * side]
            rows[pl.ds(x * bands * pitch + y, bands, stride=pitch), pl.ds(0, side)] = part
    pad = jnp.zeros((2 * side, LANES - PACK * side), BF16)
    for band in range(bands):
        parts = []
        for s in range(PACK):
            starts = [((PACK * e + s) * bands + band) * pitch for e in range(2)]
            both = [rows[pl.ds(start, side), :][:, :side] for start in starts]
            parts.append(jnp.concatenate(both, axis=0).astype(BF16))
        out_ref[band, 0] = jnp.concatenate(parts + [pad], axis=1)


def pack(orbitals, side):
    count, slab, plane = orbitals.shape
    steps = slab // (2 * PACK)
    return pl.pallas_call(
        functools.partial(pack_body, side=side),
        grid=(steps,),
        in_specs=[pl.BlockSpec((2 * PACK, count, plane), lambda m: (m, 0, 0))],
        out_specs=pl.BlockSpec((count, 1, 2 * side, LANES), lambda m: (0, m, 0, 0)),
        out_shape=jax.ShapeDtypeStruct((count, steps, 2 * side, LANES), BF16),
        scratch_shapes=[pltpu.VMEM((2 * PACK * count * (side + 4), HALF), F32)],
        compiler_params=pltpu.CompilerParams(vmem_limit_bytes=32 * 2**20),
    )(orbitals.transpose(1, 0, 2))


def unpack_body(level_ref, *refs, side, levels):
    pieces, (out_ref, rows) = refs[:-2], refs[-2:]
    planes, bands = out_ref.shape[:2]
    share = bands // levels
    pitch = rows.shape[0] // (planes * bands)
    for k, piece in enumerate(pieces):
        band = (level_ref[0] + k % levels) % levels * share + k // levels
        value = piece[0, 0].astype(F32)
        for s in range(PACK):
            part = value[:, s * side : (s + 1) * side]
            for e in range(2):
                start = ((PACK * e + s) * bands + band) * pitch
                rows[pl.ds(start, side), pl.ds(0, side)] = part[e * side : (e + 1) * side]
    for x in range(planes):
        parts = [rows[pl.ds(x * bands * pitch + y, bands, stride=pitch), :] for y in range(side)]
        out_ref[x] = jnp.concatenate([v[:, :side] for v in parts], axis=1)


def unpack(pieces, level, side, share):
    levels = len(pieces) // share
    bands = len(pieces)
    steps = pieces[0].shape[1]
    grid_spec = pltpu.PrefetchScalarGridSpec(
        num_scalar_prefetch=1,
        grid=(steps,),
        in_specs=[pl.BlockSpec((1, 1, 2 * side, LANES), lambda m, first: (0, m, 0, 0))] * bands,
        out_specs=pl.BlockSpec((2 * PACK, bands, side * side), lambda m, first: (m, 0, 0)),
        scratch_shapes=[pltpu.VMEM((2 * PACK * bands * (side + 4), HALF), F32)],
    )
    field = pl.pallas_call(
        functools.partial(unpack_body, side=side, levels=levels),
        grid_spec=grid_spec,
        out_shape=jax.ShapeDtypeStruct((2 * PACK * steps, bands, side * side), F32),
        compiler_params=pltpu.CompilerParams(vmem_limit_bytes=32 * 2**20),
    )(jnp.reshape(level, (1,)), *pieces)
    return field.transpose(1, 0, 2)


def dot(left, right):
    return lax.dot_general(left, right, (((1,), (0,)), ((), ())), preferred_element_type=F32)


def swap_thirds(values, side):
    pad = jnp.zeros((values[0].shape[0], LANES - PACK * side), values[0].dtype)
    return [
        jnp.concatenate([v[:, side * s : side * s + side] for v in values] + [pad], axis=1)
        for s in range(PACK)
    ]


def solve_body(*refs, side, pitch, places, pieces, count, has_start, cuts):
    own_pieces, rest = refs[:pieces], refs[pieces:]
    arrays = rest[: max(a for a, _ in places) + 1]
    rest = rest[len(arrays) :]
    if has_start:
        start_hbm, rest = rest[0], rest[1:]
    kernel_hbm, cas2_ref, ahead_ref, back_ref, thirds_ref = rest[:5]
    out_refs = rest[5 : 5 + max(cuts, 1)]
    own_ref, bands, kernel_ref, low, high, own_sem, band_sem, wide_sem, *totals = rest[5 + len(out_refs) :]
    total_ref = totals[0] if totals else out_refs[0]
    steps = own_ref.shape[0]
    half = side // 2
    part = steps // pieces

    own_copies = [
        pltpu.make_async_copy(ref.at[0], own_ref.at[pl.ds(k * part, part)], own_sem.at[k])
        for k, ref in enumerate(own_pieces)
    ]
    band_copies = [
        pltpu.make_async_copy(arrays[a].at[k], bands.at[j], band_sem.at[j])
        for j, (a, k) in enumerate(places)
    ]
    kernel_copy = pltpu.make_async_copy(kernel_hbm, kernel_ref, wide_sem.at[0])
    for copy in own_copies + band_copies[:PACK]:
        copy.start()
    if not has_start:
        total_ref[...] = jnp.zeros_like(total_ref)
    for j in range(len(places), bands.shape[0]):
        bands[j] = jnp.zeros_like(bands[j])

    def put(plane, value):
        low[pl.ds(plane * pitch, side), :] = value[:, :HALF]
        high[pl.ds(plane * pitch, side), :] = value[:, HALF:]

    def get(plane):
        parts = [r[pl.ds(plane * pitch, side), :] for r in (low, high)]
        return jnp.concatenate(parts, axis=1)

    def put_across(row, value):
        low[pl.ds(row, side, stride=pitch), :] = value[:, :HALF]
        high[pl.ds(row, side, stride=pitch), :] = value[:, HALF:]

    def get_across(row):
        parts = [r[pl.ds(row, side, stride=pitch), :] for r in (low, high)]
        return jnp.concatenate(parts, axis=1)

    def first_two(base, work):
        sources = []
        for step in work:
            density = [own_ref[step] * bands[base + k, step] for k in range(PACK)]
            sources += [(6 * step + s, v) for s, v in enumerate(swap_thirds(density, side))]
        along_z = [dot(v, thirds_ref[...]).astype(BF16) for _, v in sources]
        along_y = [dot(cas2_ref[...], v) for v in along_z]
        for (plane, _), v in zip(sources, along_y):
            put(plane, v[:side])
            put(plane + PACK, v[side:])

    def middle_two(rows):
        planes = [
            jnp.concatenate([get_across(2 * r), get_across(2 * r + 1)], axis=0).astype(BF16)
            for r in rows
        ]
        waves = [dot(ahead_ref[...], v) for v in planes]
        waves = [(v * kernel_ref[r]).astype(BF16) for r, v in zip(rows, waves)]
        planes = [dot(back_ref[...], v) for v in waves]
        for r, v in zip(rows, planes):
            put_across(2 * r, v[:side])
            put_across(2 * r + 1, v[side:])

    def last_two(base, work):
        halves = [
            [
                jnp.concatenate([get(6 * t + s), get(6 * t + PACK + s)], axis=0).astype(BF16)
                for s in range(PACK)
            ]
            for t in work
        ]
        along_y = [[dot(cas2_ref[...], v).astype(BF16) for v in vs] for vs in halves]
        swapped = [swap_thirds(vs, side) for vs in along_y]
        potential = [[dot(v, thirds_ref[...]) for v in vs] for vs in swapped]
        for t, vs in zip(work, potential):
            terms = [v * bands[base + k, t].astype(F32) for k, v in enumerate(vs)]
            total_ref[t] += terms[0] + terms[1] + terms[2]

    def loop(count, at_once, run):
        if at_once >= count:
            run(list(range(count)))
        else:
            lax.fori_loop(
                0, count // at_once, lambda q, c: run([q * at_once + w for w in range(at_once)]) or c, 0
            )

    for copy in own_copies + band_copies[:PACK]:
        copy.wait()
    kernel_copy.start()
    if has_start:
        start_copy = pltpu.make_async_copy(start_hbm, total_ref, wide_sem.at[1])
        start_copy.start()
    for copy in band_copies[PACK:]:
        copy.start()

    def group(g, carry):
        base = g * PACK
        for k in range(PACK):

            @pl.when((g > 0) & (base + k < len(places)))
            def _(k=k):
                pltpu.make_async_copy(
                    arrays[0].at[0], bands.at[base + k], band_sem.at[base + k]
                ).wait()
        loop(steps, at_once[0] or steps, lambda work: first_two(base, work))

        @pl.when(g == 0)
        def _():
            kernel_copy.wait()
            if has_start:
                start_copy.wait()

        loop(half, at_once[1] or half, middle_two)
        loop(steps, at_once[2] or steps, lambda work: last_two(base, work))
        return carry

    lax.fori_loop(0, count, group, 0)
    if totals:
        for k, out_ref in enumerate(out_refs):
            size = out_ref.shape[1]
            out_ref[0] = total_ref[k * size : (k + 1) * size].astype(out_ref.dtype)


at_once = (0, 0, 0)


def solve(own, bands, start, tables, side, cuts=0):
    places = [(a, k) for a, array in enumerate(bands) for k in range(array.shape[0])]
    part = own[0].shape[1]
    shape = (part * len(own),) + own[0].shape[2:]
    pitch = side + 4
    count = -(-len(places) // PACK)
    vmem = pl.BlockSpec(memory_space=pltpu.VMEM)
    hbm = pl.BlockSpec(memory_space=pl.ANY)
    first = [*own, *bands] + ([] if start is None else [start]) + [tables[0]]
    body = functools.partial(
        solve_body, side=side, pitch=pitch, places=places, pieces=len(own), count=count,
        has_start=start is not None, cuts=cuts
    )
    scratch = [
        pltpu.VMEM(shape, BF16),
        pltpu.VMEM((count * PACK,) + shape, BF16),
        pltpu.VMEM(tables[0].shape, F32),
        pltpu.VMEM((side * pitch, HALF), F32),
        pltpu.VMEM((side * pitch, HALF), F32),
        pltpu.SemaphoreType.DMA((len(own),)),
        pltpu.SemaphoreType.DMA((count * PACK,)),
        pltpu.SemaphoreType.DMA((2,)),
    ]
    piece = jax.ShapeDtypeStruct((1, shape[0] // max(cuts, 1)) + shape[1:], BF16)
    return pl.pallas_call(
        body,
        in_specs=[hbm] * len(first) + [vmem] * 4,
        out_specs=[vmem] * cuts if cuts else vmem,
        out_shape=[piece] * cuts if cuts else jax.ShapeDtypeStruct(shape, F32),
        scratch_shapes=scratch + ([pltpu.VMEM(shape, F32)] if cuts else []),
        compiler_params=pltpu.CompilerParams(vmem_limit_bytes=60 * 2**20),
        cost_estimate=pl.CostEstimate(
            flops=len(places) * 96 * side**4, bytes_accessed=10 * 2**20, transcendentals=0
        ),
    )(*first, *tables[1:])


def make_tables(side, slab, level):
    cas = cas_table(side)
    two = np.eye(2, dtype=np.float32)
    cas2 = jnp.asarray(np.kron(two, cas.astype(np.float32)).astype(BF16))
    three = np.kron(np.eye(PACK, dtype=np.float32), cas.astype(np.float32))
    margin = LANES - three.shape[0]
    thirds = jnp.asarray(np.pad(three, ((0, margin), (0, margin))).astype(BF16))
    screen = screened_kernel(side).transpose(1, 0, 2)
    screen = padded(np.concatenate([screen] * PACK, axis=-1), LANES)
    screen = jnp.asarray(screen.reshape(side // 2, 2 * side, LANES))
    table = jnp.asarray(cas)
    moved = lax.dynamic_slice_in_dim(jnp.concatenate([table, table], 0), level * slab, side, 0)
    zero = jnp.zeros_like(moved)
    back = jnp.concatenate(
        [jnp.concatenate([moved, zero], 1), jnp.concatenate([zero, moved], 1)], 0
    )
    return screen, cas2, back.T, back, thirds


def from_level(value, ahead):
    count = lax.axis_size("grid")
    pairs = [((h + ahead) % count, h) for h in range(count)]
    return lax.ppermute(value, "grid", pairs)


def flip(value, bit):
    return lax.ppermute(value, "band", [(b, b ^ bit) for b in range(lax.axis_size("band"))])


def pick(options, index):
    result = options[0]
    for k in range(1, len(options)):
        result = jnp.where(index == k, options[k], result)
    return result


def own_slabs(packed, per_device, which):
    levels = lax.axis_size("grid")
    level = lax.axis_index("grid")
    pieces = []
    for ahead in range(levels):
        start = (level + levels - ahead) % levels * per_device + which
        piece = lax.dynamic_slice_in_dim(packed, start, 1, 0)
        pieces.append(from_level(piece, ahead) if ahead else piece)
    return pieces


def whole(slab):
    levels = lax.axis_size("grid")
    pieces = [slab] + [from_level(slab, ahead) for ahead in range(1, levels)]
    return jnp.concatenate(pieces, axis=1)


def after(value, *others):
    return lax.optimization_barrier((value, others))[0]


def share_out(packed, owners, which):
    band = lax.axis_index("band")
    core, line = band % 2, band // 2
    share = packed.shape[0] // 4
    parts = []
    for k in range(4):
        part = lax.dynamic_slice_in_dim(packed, (line ^ k) * share + which, 1, 0)
        parts.append(flip(part, 2 * k) if k else part)
    here, there = owners[core], owners[1 - core]
    mine = pick(parts, line ^ (here // 2))
    other = flip(pick(parts, line ^ (there // 2)), 1)
    return jnp.where(here % 2 == core, mine, other), parts


def fields_small(packed, owners, tables, side):
    levels = lax.axis_size("grid")
    own0 = own_slabs(packed, 2, 0)
    slab0, parts = share_out(packed, owners, 0)
    slab1, _ = share_out(after(packed, parts), owners, 1)
    slab0, own0 = lax.optimization_barrier((slab0, own0))
    mine0 = whole(slab0)
    x0, y0 = flip(mine0, 2), flip(mine0, 4)
    mine1 = whole(after(slab1, mine0))
    own1 = own_slabs(after(packed, mine1), 2, 1)
    late = after(mine1, x0, y0)
    x1, y1 = flip(late, 2), flip(late, 4)
    near = [mine0, mine1, x0, y0]
    near = near + [flip(v, 1) for v in near]
    total0 = solve(own0, near, None, tables, side)
    x1, y1, total0 = lax.optimization_barrier((x1, y1, total0))
    corner = [flip(after(x0, x1, y1), 4), flip(y1, 2)]
    far = [x1, y1, flip(x1, 1), flip(y1, 1)]
    total1 = solve(own1, near, None, tables, side)
    corner, total1 = lax.optimization_barrier((corner, total1))
    far = far + corner + [flip(v, 1) for v in corner]
    field0 = solve(own0, far, total0, tables, side, levels)
    field1 = solve(own1, far, total1, tables, side, levels)
    return [field0, field1]


def fields_any(packed, owners, tables, side):
    band = lax.axis_index("band")
    levels = lax.axis_size("grid")
    per_device = packed.shape[0] // levels
    own = [own_slabs(packed, per_device, i) for i in range(per_device)]
    totals = [None] * per_device
    for r in range(owners.shape[0]):
        kept = jnp.where(band == owners[r], packed, jnp.zeros_like(packed))
        bands = whole(lax.psum(kept, "band"))
        cuts = levels if r == owners.shape[0] - 1 else 0
        totals = [solve(o, [bands], t, tables, side, cuts) for o, t in zip(own, totals)]
    return totals


def body(orbitals, owners):
    band_count, slab, plane = orbitals.shape
    levels = lax.axis_size("grid")
    level = lax.axis_index("grid")
    side = slab * levels
    tables = make_tables(side, slab, level)
    packed = pack(orbitals, side)
    small = (lax.axis_size("band"), owners.shape[0], band_count, levels) == (8, 2, 8, 4)
    fields = (fields_small if small else fields_any)(packed, owners, tables, side)
    pieces = []
    for field in fields:
        for ahead in range(levels):
            piece = field[(levels - ahead) % levels]
            pieces.append(from_level(piece, ahead) if ahead else piece)
    return unpack(pieces, level, side, len(fields))


def solution(mesh):
    placed = (P("band", "grid", None), P())
    return jax.shard_map(
        body, mesh=mesh, in_specs=placed, out_specs=P("band", "grid", None), check_vma=False
    )
```

time: 351 us -> 221 us (0.63)
  waiting for transfers between devices: 156 us -> 74.9 us
  local copies, waits for them, and re-layouts: 64.6 us -> 9.11 us
  starting transfers between devices: 18.5 us -> 38.7 us
  other arithmetic: 11 us -> 2.63 us
  Pallas kernels: 94.4 us -> 90.1 us
    ppermute x13 -> x22, waiting for transfers between devices: 55.7 us -> 10.9 us  [flip(): lax.ppermute(value, 'band', [(b, b ^ bit) for b in range(lax.axis_size('b...]
    ppermute x9 -> x18, waiting for transfers between devices: 100 us -> 64 us  [from_level(): return lax.ppermute(value, 'grid', pairs)]
    convert_element_type x4 -> x0, local copies, waits for them, and re-layouts: 27.8 us -> none  [body(): return unpack(ordered, side).astype(F32).reshape(band_count, slab, plane)]
    ppermute x9 -> x18, starting transfers between devices: 9.14 us -> 22.5 us  [from_level(): return lax.ppermute(value, 'grid', pairs)]
    another operation x2 -> x0, local copies, waits for them, and re-layouts: 12.3 us -> none  [pack(): bands.reshape(count, planes // 6, 2, PACK, side, side)]
    reshape x2 -> x0, local copies, waits for them, and re-layouts: 9.39 us -> none  [pack(): joined = split.reshape(count, planes // 6, 2 * side, PACK * side)]
    ppermute x13 -> x22, starting transfers between devices: 9.4 us -> 16.2 us  [flip(): lax.ppermute(value, 'band', [(b, b ^ bit) for b in range(lax.axis_size('b...]
    convert_element_type x2 -> x0, other arithmetic: 5.86 us -> none  [the longest x1 3.68 us: body(): return unpack(ordered, side).astype(F32).reshape(band_count, slab, plane)]
  transfers between devices with their start and end apart: 22 -> 40, of which waited for: 10 -> 13; matrix products, arithmetic and copies ran while one was open for 3% -> 3% of each run, Pallas kernels for 20% -> 29%
where the time goes in v3:
time: 221 us
  Pallas kernels  90.1 us (41%)
  waiting for transfers between devices  74.9 us (34%)
  starting transfers between devices  38.7 us (18%)
  local copies, waits for them, and re-layouts  9.11 us (4%)
  between operations  5.27 us (2%)
  other arithmetic  2.63 us (1%)
    pallas_call x4, Pallas kernels, solve(): pl.pallas_call(body, in_specs=[hbm] * len(first) + [vmem] * 4, out_specs=...  84.6 us
    ppermute x18, waiting for transfers between devices, from_level(): return lax.ppermute(value, 'grid', pairs)  64 us
    ppermute x18, starting transfers between devices, from_level(): return lax.ppermute(value, 'grid', pairs)  22.5 us
    ppermute x22, starting transfers between devices, flip(): lax.ppermute(value, 'band', [(b, b ^ bit) for b in range(lax.axis_size('b...  16.2 us
    ppermute x22, waiting for transfers between devices, flip(): lax.ppermute(value, 'band', [(b, b ^ bit) for b in range(lax.axis_size('b...  10.9 us
    unnamed x34, local copies, waits for them, and re-layouts  6.23 us
  transfers between devices with their start and end apart: 40, of which 13 were waited for; matrix products, arithmetic and copies ran while one was open for 3% of the time, Pallas kernels for 29%

profile of v3, /device:TPU:0, one launch (start us, length us, event | category | flops | bytes accessed | tf_op | source)
XLA Modules:
  0.0 220.7 jit_solution(6375917494673920954)
XLA Ops:
  0.0 1.4 copy-done
  1.4 2.0 shard_map.64
  3.5 4.0 %collective-permute-start = (bf16[1,3,144,256]{3,2,1,0:T(8,128)(2,1)S(1)}, bf16[1,3,144,256]{3,2,1,0:T(8,128)(2,1)S(1)}, u32[]{:S(2)}, u32[]{:S(2)}) collective-permute-start(bf16[1,3,144,256]{3,2,1,0:T(8,128)(2,1)S(1)} %get-tuple-element.70), channel_id=1, source_target_pairs={{0,24},{4,28},{8,16},{12,20},{16,8},{20,12},{24,0},{28,4},{1,25},{... | collective-permute-start | bytes 663560 | tf_op jit(solution)/shard_map/ppermute | solution.py:323
  7.4 0.5 collective-permute-start.1
  7.9 0.1 collective-permute-start.2
  8.1 0.6 fusion.4
  11.0 2.7 %collective-permute-done = bf16[1,3,144,256]{3,2,1,0:T(8,128)(2,1)S(1)} collective-permute-done((bf16[1,3,144,256]{3,2,1,0:T(8,128)(2,1)S(1)}, bf16[1,3,144,256]{3,2,1,0:T(8,128)(2,1)S(1)}, u32[]{:S(2)}, u32[]{:S(2)}) %collective-permute-start) | collective-permute-done | bytes 221216 | tf_op jit(solution)/shard_map/ppermute | solution.py:323
  13.7 3.9 %collective-permute-done.1 = bf16[1,3,144,256]{3,2,1,0:T(8,128)(2,1)S(1)} collective-permute-done((bf16[1,3,144,256]{3,2,1,0:T(8,128)(2,1)S(1)}, bf16[1,3,144,256]{3,2,1,0:T(8,128)(2,1)S(1)}, u32[]{:S(2)}, u32[]{:S(2)}) %collective-permute-start.1) | collective-permute-done | bytes 221216 | tf_op jit(solution)/shard_map/ppermute | solution.py:323
  17.6 0.3 collective-permute-done.2
  17.9 0.8 constant_dynamic-slice_fusion.8
  18.7 3.6 %collective-permute-start.4 = (bf16[1,3,144,256]{3,2,1,0:T(8,128)(2,1)S(1)}, bf16[1,3,144,256]{3,2,1,0:T(8,128)(2,1)}, u32[]{:S(2)}, u32[]{:S(2)}) collective-permute-start(bf16[1,3,144,256]{3,2,1,0:T(8,128)(2,1)S(1)} %get-tuple-element.64), channel_id=1, source_target_pairs={{1,0},{2,1},{3,2},{0,3},{5,4},{6,5},{7,6},{4,7},{9,8},{10,9},{11,1... | collective-permute-start | bytes 663560 | tf_op jit(solution)/shard_map/ppermute | solution.py:319
  25.0 1.0 collective-permute-start.6
  26.1 1.7 collective-permute-start.7
  27.8 1.3 collective-permute-start.8
  29.1 0.5 collective-permute-start.9
  29.6 1.0 select_select_fusion.3
  30.6 12.0 %collective-permute-done.5.refs_2_ = bf16[1,3,144,256]{3,2,1,0:T(8,128)(2,1)S(1)} collective-permute-done((bf16[1,3,144,256]{3,2,1,0:T(8,128)(2,1)S(1)}, bf16[1,3,144,256]{3,2,1,0:T(8,128)(2,1)S(1)}, u32[]{:S(2)}, u32[]{:S(2)}) %collective-permute-start.5) | collective-permute-done | bytes 221216 | tf_op jit(solution)/shard_map/ppermute | solution.py:319
  42.7 0.7 copy-done.10
  43.4 2.5 %collective-permute-start.12 = (bf16[1,3,144,256]{3,2,1,0:T(8,128)(2,1)S(1)}, bf16[1,3,144,256]{3,2,1,0:T(8,128)(2,1)S(1)}, u32[]{:S(2)}, u32[]{:S(2)}) collective-permute-start(bf16[1,3,144,256]{3,2,1,0:T(8,128)(2,1)S(1)} %select_select_fusion.3), channel_id=1, source_target_pairs={{2,0},{3,1},{0,2},{1,3},{6,4},{7,5},{4,6},{5,7},{10,8},{11,9},{8,1... | collective-permute-start | bytes 663560 | tf_op jit(solution)/shard_map/ppermute | solution.py:319
  45.9 2.0 collective-permute-start.13
  48.1 0.7 constant_dynamic-update-slice_fusion.3
  48.8 1.9 collective-permute-done.11
  50.7 0.7 constant_dynamic-update-slice_fusion.2
  51.4 14.4 %collective-permute-done.12 = bf16[1,3,144,256]{3,2,1,0:T(8,128)(2,1)S(1)} collective-permute-done((bf16[1,3,144,256]{3,2,1,0:T(8,128)(2,1)S(1)}, bf16[1,3,144,256]{3,2,1,0:T(8,128)(2,1)S(1)}, u32[]{:S(2)}, u32[]{:S(2)}) %collective-permute-start.12) | collective-permute-done | bytes 221216 | tf_op jit(solution)/shard_map/ppermute | solution.py:319
  65.8 0.7 constant_dynamic-update-slice_fusion.1
  66.5 0.7 constant_dynamic-update-slice_fusion.refs_4_
  67.2 1.5 collective-permute-start.17
  68.7 0.7 collective-permute-start.18
  69.4 0.1 select_select_fusion.1
  69.6 0.1 collective-permute-start.15
  69.6 1.9 collective-permute-start.16
  71.6 5.5 %collective-permute-done.14 = bf16[1,3,144,256]{3,2,1,0:T(8,128)(2,1)S(1)} collective-permute-done((bf16[1,3,144,256]{3,2,1,0:T(8,128)(2,1)S(1)}, bf16[1,3,144,256]{3,2,1,0:T(8,128)(2,1)S(1)}, u32[]{:S(2)}, u32[]{:S(2)}) %collective-permute-start.14) | collective-permute-done | bytes 221216 | tf_op jit(solution)/shard_map/ppermute | solution.py:319
  77.1 11.3 %collective-permute-done.15 = bf16[1,3,144,256]{3,2,1,0:T(8,128)(2,1)S(1)} collective-permute-done((bf16[1,3,144,256]{3,2,1,0:T(8,128)(2,1)S(1)}, bf16[1,3,144,256]{3,2,1,0:T(8,128)(2,1)S(1)}, u32[]{:S(2)}, u32[]{:S(2)}) %collective-permute-start.15) | collective-permute-done | bytes 221216 | tf_op jit(solution)/shard_map/ppermute | solution.py:319
  88.5 0.1 collective-permute-start.22
  88.6 0.5 collective-permute-start.23
  89.1 0.7 collective-permute-done.18.refs_7_
  89.8 0.7 fusion.2
  90.5 0.7 copy.7.refs_14_.refs_15_
  91.2 0.7 constant_dynamic-slice_fusion
  92.0 2.1 collective-permute-start.30
  94.1 2.0 collective-permute-start.31
  96.2 1.2 collective-permute-start.19
  97.4 0.6 collective-permute-start.20
  98.0 21.0 %shard_map.65.refs_12_ = f32[12,144,256]{2,1,0:T(8,128)} custom-call(bf16[1,3,144,256]{3,2,1,0:T(8,128)(2,1)} %get-tuple-element.29.refs_0_, bf16[1,3,144,256]{3,2,1,0:T(8,128)(2,1)} %collective-permute-done.4.refs_1_, bf16[1,3,144,256]{3,2,1,0:T(8,128)(2,1)} %copy-done.9, bf16[1,3,144,256]{3,2,1,0:T(8,128)(2,1)} %copy-done.10, ...), custom_call_target="tpu_custom_call" | custom-call | flops 20639121408 | bytes 10485760 | tf_op jit(solution)/shard_map/pallas_call | solution.py:284
  119.1 1.6 collective-permute-start.28
  120.7 0.5 collective-permute-start.26
  121.2 0.7 collective-permute-start.27
  121.9 0.7 copy-done.13
  122.6 21.1 %shard_map.66.refs_12_ = f32[12,144,256]{2,1,0:T(8,128)} custom-call(bf16[1,3,144,256]{3,2,1,0:T(8,128)(2,1)} %get-tuple-element.58.refs_0_, bf16[1,3,144,256]{3,2,1,0:T(8,128)(2,1)} %copy-done.11, bf16[1,3,144,256]{3,2,1,0:T(8,128)(2,1)} %copy-done.12, bf16[1,3,144,256]{3,2,1,0:T(8,128)(2,1)} %copy-done.13, ...), custom_call_target="tpu_custom_call" | custom-call | flops 20639121408 | bytes 10485760 | tf_op jit(solution)/shard_map/pallas_call | solution.py:284
  143.8 0.5 collective-permute-start.33
  144.3 2.6 %collective-permute-done.32.refs_10_ = bf16[1,12,144,256]{3,2,1,0:T(8,128)(2,1)S(1)} collective-permute-done((bf16[1,12,144,256]{3,2,1,0:T(8,128)(2,1)}, bf16[1,12,144,256]{3,2,1,0:T(8,128)(2,1)S(1)}, u32[]{:S(2)}, u32[]{:S(2)}) %collective-permute-start.32) | collective-permute-done | bytes 884768 | tf_op jit(solution)/shard_map/ppermute | solution.py:323
  146.9 0.7 collective-permute-done.33.refs_11_
  147.6 0.3 copy-done.8
  147.9 21.3 %shard_map.68 = (bf16[1,3,144,256]{3,2,1,0:T(8,128)(2,1)}, bf16[1,3,144,256]{3,2,1,0:T(8,128)(2,1)}, bf16[1,3,144,256]{3,2,1,0:T(8,128)(2,1)}, bf16[1,3,144,256]{3,2,1,0:T(8,128)(2,1)}) custom-call(bf16[1,3,144,256]{3,2,1,0:T(8,128)(2,1)} %get-tuple-element.58.refs_0_, bf16[1,3,144,256]{3,2,1,0:T(8,128)(2,1)} %copy-done.11, ...), custom_call_target="tpu_custom_call" | custom-call | flops 20639121408 | bytes 10485760 | tf_op jit(solution)/shard_map/pallas_call | solution.py:284
  169.2 1.9 collective-permute-start.37
  171.0 1.0 collective-permute-start.39
  172.0 21.2 %shard_map.67 = (bf16[1,3,144,256]{3,2,1,0:T(8,128)(2,1)}, bf16[1,3,144,256]{3,2,1,0:T(8,128)(2,1)}, bf16[1,3,144,256]{3,2,1,0:T(8,128)(2,1)}, bf16[1,3,144,256]{3,2,1,0:T(8,128)(2,1)}) custom-call(bf16[1,3,144,256]{3,2,1,0:T(8,128)(2,1)} %get-tuple-element.29.refs_0_, bf16[1,3,144,256]{3,2,1,0:T(8,128)(2,1)} %collective-permute-done.4.refs_1_, ...), custom_call_target="tpu_custom_call" | custom-call | flops 20639121408 | bytes 10485760 | tf_op jit(solution)/shard_map/pallas_call | solution.py:284
  193.3 2.9 %collective-permute-start.34 = (bf16[1,3,144,256]{3,2,1,0:T(8,128)(2,1)}, bf16[1,3,144,256]{3,2,1,0:T(8,128)(2,1)S(1)}, u32[]{:S(2)}, u32[]{:S(2)}) collective-permute-start(bf16[1,3,144,256]{3,2,1,0:T(8,128)(2,1)} %get-tuple-element.45), channel_id=1, source_target_pairs={{1,0},{2,1},{3,2},{0,3},{5,4},{6,5},{7,6},{4,7},{9,8},{10,9},{11,1... | collective-permute-start | bytes 663560 | tf_op jit(solution)/shard_map/ppermute | solution.py:319
  196.1 1.1 collective-permute-start.35
  197.3 0.2 collective-permute-start.36
  197.5 4.9 %collective-permute-done.34.refs_1_ = bf16[1,3,144,256]{3,2,1,0:T(8,128)(2,1)S(1)} collective-permute-done((bf16[1,3,144,256]{3,2,1,0:T(8,128)(2,1)}, bf16[1,3,144,256]{3,2,1,0:T(8,128)(2,1)S(1)}, u32[]{:S(2)}, u32[]{:S(2)}) %collective-permute-start.34) | collective-permute-done | bytes 221216 | tf_op jit(solution)/shard_map/ppermute | solution.py:319
  202.4 13.9 %collective-permute-done.35.refs_2_ = bf16[1,3,144,256]{3,2,1,0:T(8,128)(2,1)S(1)} collective-permute-done((bf16[1,3,144,256]{3,2,1,0:T(8,128)(2,1)}, bf16[1,3,144,256]{3,2,1,0:T(8,128)(2,1)S(1)}, u32[]{:S(2)}, u32[]{:S(2)}) %collective-permute-start.35) | collective-permute-done | bytes 221216 | tf_op jit(solution)/shard_map/ppermute | solution.py:319
  216.3 0.9 copy-done.2
  217.2 3.5 %shard_map.69 = f32[18,8,5184]{2,1,0:T(8,128)} custom-call(s32[1]{0:T(128)} %bitcast.level_ref, bf16[1,3,144,256]{3,2,1,0:T(8,128)(2,1)S(1)} %copy-done.2, bf16[1,3,144,256]{3,2,1,0:T(8,128)(2,1)S(1)} %collective-permute-done.34.refs_1_, bf16[1,3,144,256]{3,2,1,0:T(8,128)(2,1)S(1)} %collective-permute-done.35.refs_2_, ...), custom_call_target="tpu_custom_call" | custom-call | tf_op jit(solution)/shard_map/pallas_call | solution.py:107
  (69 shorter events, 0.7 us)
Async XLA Ops:
  0.0 1.4 copy-start
  1.4 6.7 %copy-start.5 = (s32[2]{0:T(128)S(1)}, s32[2]{0:T(128)}, u32[]{:S(2)}) copy-start(s32[2]{0:T(128)} %param.7) | copy-start | bytes 28
  3.5 10.3 %collective-permute-start = (bf16[1,3,144,256]{3,2,1,0:T(8,128)(2,1)S(1)}, bf16[1,3,144,256]{3,2,1,0:T(8,128)(2,1)S(1)}, u32[]{:S(2)}, u32[]{:S(2)}) collective-permute-start(bf16[1,3,144,256]{3,2,1,0:T(8,128)(2,1)S(1)} %get-tuple-element.70), channel_id=1, source_target_pairs={{0,24},{4,28},{8,16},{12,20},{16,8},{20,12},{24,0},{28,4},{1,25},{... | collective-permute-start | bytes 663560 | tf_op jit(solution)/shard_map/ppermute | solution.py:323
  7.4 10.2 %collective-permute-start.1 = (bf16[1,3,144,256]{3,2,1,0:T(8,128)(2,1)S(1)}, bf16[1,3,144,256]{3,2,1,0:T(8,128)(2,1)S(1)}, u32[]{:S(2)}, u32[]{:S(2)}) collective-permute-start(bf16[1,3,144,256]{3,2,1,0:T(8,128)(2,1)S(1)} %get-tuple-element.69), channel_id=1, source_target_pairs={{0,16},{4,20},{8,24},{12,28},{16,0},{20,4},{24,8},{28,12},{1,17},{... | collective-permute-start | bytes 663560 | tf_op jit(solution)/shard_map/ppermute | solution.py:323
  7.9 10.0 %collective-permute-start.2 = (bf16[1,3,144,256]{3,2,1,0:T(8,128)(2,1)S(1)}, bf16[1,3,144,256]{3,2,1,0:T(8,128)(2,1)S(1)}, u32[]{:S(2)}, u32[]{:S(2)}) collective-permute-start(bf16[1,3,144,256]{3,2,1,0:T(8,128)(2,1)S(1)} %get-tuple-element.68), channel_id=1, source_target_pairs={{0,8},{4,12},{8,0},{12,4},{16,24},{20,28},{24,16},{28,20},{1,9},{5... | collective-permute-start | bytes 663560 | tf_op jit(solution)/shard_map/ppermute | solution.py:323
  18.7 9.1 %collective-permute-start.3 = (bf16[1,3,144,256]{3,2,1,0:T(8,128)(2,1)S(1)}, bf16[1,3,144,256]{3,2,1,0:T(8,128)(2,1)}, u32[]{:S(2)}, u32[]{:S(2)}) collective-permute-start(bf16[1,3,144,256]{3,2,1,0:T(8,128)(2,1)S(1)} %get-tuple-element.66), channel_id=1, source_target_pairs={{0,4},{4,0},{8,12},{12,8},{16,20},{20,16},{24,28},{28,24},{1,5},{5... | collective-permute-start | bytes 663560 | tf_op jit(solution)/shard_map/ppermute | solution.py:323
  18.7 10.4 %collective-permute-start.4 = (bf16[1,3,144,256]{3,2,1,0:T(8,128)(2,1)S(1)}, bf16[1,3,144,256]{3,2,1,0:T(8,128)(2,1)}, u32[]{:S(2)}, u32[]{:S(2)}) collective-permute-start(bf16[1,3,144,256]{3,2,1,0:T(8,128)(2,1)S(1)} %get-tuple-element.64), channel_id=1, source_target_pairs={{1,0},{2,1},{3,2},{0,3},{5,4},{6,5},{7,6},{4,7},{9,8},{10,9},{11,1... | collective-permute-start | bytes 663560 | tf_op jit(solution)/shard_map/ppermute | solution.py:319
  24.9 17.7 %collective-permute-start.5 = (bf16[1,3,144,256]{3,2,1,0:T(8,128)(2,1)S(1)}, bf16[1,3,144,256]{3,2,1,0:T(8,128)(2,1)S(1)}, u32[]{:S(2)}, u32[]{:S(2)}) collective-permute-start(bf16[1,3,144,256]{3,2,1,0:T(8,128)(2,1)S(1)} %get-tuple-element.63), channel_id=1, source_target_pairs={{2,0},{3,1},{0,2},{1,3},{6,4},{7,5},{4,6},{5,7},{10,8},{11,9},{8,1... | collective-permute-start | bytes 663560 | tf_op jit(solution)/shard_map/ppermute | solution.py:319
  25.0 17.6 %collective-permute-start.6 = (bf16[1,3,144,256]{3,2,1,0:T(8,128)(2,1)S(1)}, bf16[1,3,144,256]{3,2,1,0:T(8,128)(2,1)S(1)}, u32[]{:S(2)}, u32[]{:S(2)}) collective-permute-start(bf16[1,3,144,256]{3,2,1,0:T(8,128)(2,1)S(1)} %get-tuple-element.62), channel_id=1, source_target_pairs={{3,0},{0,1},{1,2},{2,3},{7,4},{4,5},{5,6},{6,7},{11,8},{8,9},{9,10... | collective-permute-start | bytes 663560 | tf_op jit(solution)/shard_map/ppermute | solution.py:319
  26.1 19.9 %collective-permute-start.7 = (bf16[1,3,144,256]{3,2,1,0:T(8,128)(2,1)S(1)}, bf16[1,3,144,256]{3,2,1,0:T(8,128)(2,1)S(1)}, u32[]{:S(2)}, u32[]{:S(2)}) collective-permute-start(bf16[1,3,144,256]{3,2,1,0:T(8,128)(2,1)S(1)} %get-tuple-element.61), channel_id=1, source_target_pairs={{0,24},{4,28},{8,16},{12,20},{16,8},{20,12},{24,0},{28,4},{1,25},{... | collective-permute-start | bytes 663560 | tf_op jit(solution)/shard_map/ppermute | solution.py:323
  27.8 20.2 %collective-permute-start.8 = (bf16[1,3,144,256]{3,2,1,0:T(8,128)(2,1)S(1)}, bf16[1,3,144,256]{3,2,1,0:T(8,128)(2,1)S(1)}, u32[]{:S(2)}, u32[]{:S(2)}) collective-permute-start(bf16[1,3,144,256]{3,2,1,0:T(8,128)(2,1)S(1)} %get-tuple-element.60), channel_id=1, source_target_pairs={{0,16},{4,20},{8,24},{12,28},{16,0},{20,4},{24,8},{28,12},{1,17},{... | collective-permute-start | bytes 663560 | tf_op jit(solution)/shard_map/ppermute | solution.py:323
  29.1 18.9 %collective-permute-start.9 = (bf16[1,3,144,256]{3,2,1,0:T(8,128)(2,1)S(1)}, bf16[1,3,144,256]{3,2,1,0:T(8,128)(2,1)S(1)}, u32[]{:S(2)}, u32[]{:S(2)}) collective-permute-start(bf16[1,3,144,256]{3,2,1,0:T(8,128)(2,1)S(1)} %get-tuple-element.59), channel_id=1, source_target_pairs={{0,8},{4,12},{8,0},{12,4},{16,24},{20,28},{24,16},{28,20},{1,9},{5... | collective-permute-start | bytes 663560 | tf_op jit(solution)/shard_map/ppermute | solution.py:323
  42.7 0.8 copy-start.9
  42.7 0.7 copy-start.10
  43.4 7.2 %collective-permute-start.11 = (bf16[1,3,144,256]{3,2,1,0:T(8,128)(2,1)S(1)}, bf16[1,3,144,256]{3,2,1,0:T(8,128)(2,1)S(1)}, u32[]{:S(2)}, u32[]{:S(2)}) collective-permute-start(bf16[1,3,144,256]{3,2,1,0:T(8,128)(2,1)S(1)} %select_select_fusion.3), channel_id=1, source_target_pairs={{1,0},{2,1},{3,2},{0,3},{5,4},{6,5},{7,6},{4,7},{9,8},{10,9},{11,1... | collective-permute-start | bytes 663560 | tf_op jit(solution)/shard_map/ppermute | solution.py:319
  43.4 22.4 %collective-permute-start.12 = (bf16[1,3,144,256]{3,2,1,0:T(8,128)(2,1)S(1)}, bf16[1,3,144,256]{3,2,1,0:T(8,128)(2,1)S(1)}, u32[]{:S(2)}, u32[]{:S(2)}) collective-permute-start(bf16[1,3,144,256]{3,2,1,0:T(8,128)(2,1)S(1)} %select_select_fusion.3), channel_id=1, source_target_pairs={{2,0},{3,1},{0,2},{1,3},{6,4},{7,5},{4,6},{5,7},{10,8},{11,9},{8,1... | collective-permute-start | bytes 663560 | tf_op jit(solution)/shard_map/ppermute | solution.py:319
  45.9 20.6 %collective-permute-start.13 = (bf16[1,3,144,256]{3,2,1,0:T(8,128)(2,1)S(1)}, bf16[1,3,144,256]{3,2,1,0:T(8,128)(2,1)S(1)}, u32[]{:S(2)}, u32[]{:S(2)}) collective-permute-start(bf16[1,3,144,256]{3,2,1,0:T(8,128)(2,1)S(1)} %select_select_fusion.3), channel_id=1, source_target_pairs={{3,0},{0,1},{1,2},{2,3},{7,4},{4,5},{5,6},{6,7},{11,8},{8,9},{9,10... | collective-permute-start | bytes 663560 | tf_op jit(solution)/shard_map/ppermute | solution.py:319
  48.0 21.4 %collective-permute-start.10 = (bf16[1,3,144,256]{3,2,1,0:T(8,128)(2,1)S(1)}, bf16[1,3,144,256]{3,2,1,0:T(8,128)(2,1)S(1)}, u32[]{:S(2)}, u32[]{:S(2)}) collective-permute-start(bf16[1,3,144,256]{3,2,1,0:T(8,128)(2,1)S(1)} %select_select_fusion), channel_id=1, source_target_pairs={{0,4},{4,0},{8,12},{12,8},{16,20},{20,16},{24,28},{28,24},{1,5},{5... | collective-permute-start | bytes 663560 | tf_op jit(solution)/shard_map/ppermute | solution.py:323
  66.5 23.3 %copy-start.4 = (bf16[144,72]{1,0:T(8,128)(2,1)S(1)}, bf16[144,72]{1,0:T(8,128)(2,1)}, u32[]{:S(2)}) copy-start(bf16[144,72]{1,0:T(8,128)(2,1)} %constant.135) | copy-start | bytes 62212
  67.2 21.4 %collective-permute-start.17 = (bf16[1,12,144,256]{3,2,1,0:T(8,128)(2,1)}, bf16[1,12,144,256]{3,2,1,0:T(8,128)(2,1)}, u32[]{:S(2)}, u32[]{:S(2)}) collective-permute-start(bf16[1,12,144,256]{3,2,1,0:T(8,128)(2,1)} %constant_dynamic-update-slice_fusion.refs_4_), channel_id=1, source_target_pairs={{0,8},{4,12},{8,0},{12,4},{16,24},{20,28},{24,16},{28,20},{1,9},{5... | collective-permute-start | bytes 2654216 | tf_op jit(solution)/shard_map/ppermute | solution.py:323
  68.7 21.1 %collective-permute-start.18 = (bf16[1,12,144,256]{3,2,1,0:T(8,128)(2,1)}, bf16[1,12,144,256]{3,2,1,0:T(8,128)(2,1)}, u32[]{:S(2)}, u32[]{:S(2)}) collective-permute-start(bf16[1,12,144,256]{3,2,1,0:T(8,128)(2,1)} %constant_dynamic-update-slice_fusion.refs_4_), channel_id=1, source_target_pairs={{0,16},{4,20},{8,24},{12,28},{16,0},{20,4},{24,8},{28,12},{1,17},{... | collective-permute-start | bytes 2654216 | tf_op jit(solution)/shard_map/ppermute | solution.py:323
  69.5 7.6 %collective-permute-start.14 = (bf16[1,3,144,256]{3,2,1,0:T(8,128)(2,1)S(1)}, bf16[1,3,144,256]{3,2,1,0:T(8,128)(2,1)S(1)}, u32[]{:S(2)}, u32[]{:S(2)}) collective-permute-start(bf16[1,3,144,256]{3,2,1,0:T(8,128)(2,1)S(1)} %select_select_fusion.1), channel_id=1, source_target_pairs={{1,0},{2,1},{3,2},{0,3},{5,4},{6,5},{7,6},{4,7},{9,8},{10,9},{11,1... | collective-permute-start | bytes 663560 | tf_op jit(solution)/shard_map/ppermute | solution.py:319
  69.6 18.9 %collective-permute-start.15 = (bf16[1,3,144,256]{3,2,1,0:T(8,128)(2,1)S(1)}, bf16[1,3,144,256]{3,2,1,0:T(8,128)(2,1)S(1)}, u32[]{:S(2)}, u32[]{:S(2)}) collective-permute-start(bf16[1,3,144,256]{3,2,1,0:T(8,128)(2,1)S(1)} %select_select_fusion.1), channel_id=1, source_target_pairs={{2,0},{3,1},{0,2},{1,3},{6,4},{7,5},{4,6},{5,7},{10,8},{11,9},{8,1... | collective-permute-start | bytes 663560 | tf_op jit(solution)/shard_map/ppermute | solution.py:319
  69.6 18.8 %collective-permute-start.16 = (bf16[1,3,144,256]{3,2,1,0:T(8,128)(2,1)S(1)}, bf16[1,3,144,256]{3,2,1,0:T(8,128)(2,1)S(1)}, u32[]{:S(2)}, u32[]{:S(2)}) collective-permute-start(bf16[1,3,144,256]{3,2,1,0:T(8,128)(2,1)S(1)} %select_select_fusion.1), channel_id=1, source_target_pairs={{3,0},{0,1},{1,2},{2,3},{7,4},{4,5},{5,6},{6,7},{11,8},{8,9},{9,10... | collective-permute-start | bytes 663560 | tf_op jit(solution)/shard_map/ppermute | solution.py:319
  77.1 14.9 %collective-permute-start.21 = (bf16[1,12,144,256]{3,2,1,0:T(8,128)(2,1)}, bf16[1,12,144,256]{3,2,1,0:T(8,128)(2,1)}, u32[]{:S(2)}, u32[]{:S(2)}) collective-permute-start(bf16[1,12,144,256]{3,2,1,0:T(8,128)(2,1)} %constant_dynamic-update-slice_fusion.refs_4_), channel_id=1, source_target_pairs={{0,4},{4,0},{8,12},{12,8},{16,20},{20,16},{24,28},{28,24},{1,5},{5... | collective-permute-start | bytes 2654216 | tf_op jit(solution)/shard_map/ppermute | solution.py:323
  88.5 9.5 %copy-start.3 = (bf16[1,12,144,256]{3,2,1,0:T(8,128)(2,1)}, bf16[1,12,144,256]{3,2,1,0:T(8,128)(2,1)S(1)}, u32[]{:S(2)}) copy-start(bf16[1,12,144,256]{3,2,1,0:T(8,128)(2,1)S(1)} %constant_dynamic-update-slice_fusion.4.refs_5_) | copy-start | bytes 2654212
  88.5 5.6 %collective-permute-start.22 = (bf16[1,12,144,256]{3,2,1,0:T(8,128)(2,1)S(1)}, bf16[1,12,144,256]{3,2,1,0:T(8,128)(2,1)}, u32[]{:S(2)}, u32[]{:S(2)}) collective-permute-start(bf16[1,12,144,256]{3,2,1,0:T(8,128)(2,1)S(1)} %constant_dynamic-update-slice_fusion.4.refs_5_), channel_id=1, source_target_pairs={{0,4},{4,0},{8,12},{12,8},{16,20},{20,16},{24,28},{28,24},{1,5},{5... | collective-permute-start | bytes 2654216 | tf_op jit(solution)/shard_map/ppermute | solution.py:323
  88.6 7.6 %collective-permute-start.23 = (bf16[1,12,144,256]{3,2,1,0:T(8,128)(2,1)}, bf16[1,12,144,256]{3,2,1,0:T(8,128)(2,1)}, u32[]{:S(2)}, u32[]{:S(2)}) collective-permute-start(bf16[1,12,144,256]{3,2,1,0:T(8,128)(2,1)} %collective-permute-done.17.refs_6_), channel_id=1, source_target_pairs={{0,4},{4,0},{8,12},{12,8},{16,20},{20,16},{24,28},{28,24},{1,5},{5... | collective-permute-start | bytes 2654216 | tf_op jit(solution)/shard_map/ppermute | solution.py:323
  89.8 7.6 %collective-permute-start.24 = (bf16[1,12,144,256]{3,2,1,0:T(8,128)(2,1)}, bf16[1,12,144,256]{3,2,1,0:T(8,128)(2,1)}, u32[]{:S(2)}, u32[]{:S(2)}) collective-permute-start(bf16[1,12,144,256]{3,2,1,0:T(8,128)(2,1)} %collective-permute-done.18.refs_7_), channel_id=1, source_target_pairs={{0,4},{4,0},{8,12},{12,8},{16,20},{20,16},{24,28},{28,24},{1,5},{5... | collective-permute-start | bytes 2654216 | tf_op jit(solution)/shard_map/ppermute | solution.py:323
  92.0 28.7 %collective-permute-start.29 = (bf16[1,3,144,256]{3,2,1,0:T(8,128)(2,1)S(1)}, bf16[1,3,144,256]{3,2,1,0:T(8,128)(2,1)S(1)}, u32[]{:S(2)}, u32[]{:S(2)}) collective-permute-start(bf16[1,3,144,256]{3,2,1,0:T(8,128)(2,1)S(1)} %get-tuple-element.57), channel_id=1, source_target_pairs={{1,0},{2,1},{3,2},{0,3},{5,4},{6,5},{7,6},{4,7},{9,8},{10,9},{11,1... | collective-permute-start | bytes 663560 | tf_op jit(solution)/shard_map/ppermute | solution.py:319
  92.0 29.2 %collective-permute-start.30 = (bf16[1,3,144,256]{3,2,1,0:T(8,128)(2,1)S(1)}, bf16[1,3,144,256]{3,2,1,0:T(8,128)(2,1)S(1)}, u32[]{:S(2)}, u32[]{:S(2)}) collective-permute-start(bf16[1,3,144,256]{3,2,1,0:T(8,128)(2,1)S(1)} %get-tuple-element.56), channel_id=1, source_target_pairs={{2,0},{3,1},{0,2},{1,3},{6,4},{7,5},{4,6},{5,7},{10,8},{11,9},{8,1... | collective-permute-start | bytes 663560 | tf_op jit(solution)/shard_map/ppermute | solution.py:319
  94.1 27.8 %collective-permute-start.31 = (bf16[1,3,144,256]{3,2,1,0:T(8,128)(2,1)S(1)}, bf16[1,3,144,256]{3,2,1,0:T(8,128)(2,1)S(1)}, u32[]{:S(2)}, u32[]{:S(2)}) collective-permute-start(bf16[1,3,144,256]{3,2,1,0:T(8,128)(2,1)S(1)} %get-tuple-element.55), channel_id=1, source_target_pairs={{3,0},{0,1},{1,2},{2,3},{7,4},{4,5},{5,6},{6,7},{11,8},{8,9},{9,10... | collective-permute-start | bytes 663560 | tf_op jit(solution)/shard_map/ppermute | solution.py:319
  96.2 22.9 %collective-permute-start.19 = (bf16[1,12,144,256]{3,2,1,0:T(8,128)(2,1)S(1)}, bf16[1,12,144,256]{3,2,1,0:T(8,128)(2,1)S(1)}, u32[]{:S(2)}, u32[]{:S(2)}) collective-permute-start(bf16[1,12,144,256]{3,2,1,0:T(8,128)(2,1)S(1)} %constant_dynamic-update-slice_fusion.4.refs_5_), channel_id=1, source_target_pairs={{0,8},{4,12},{8,0},{12,4},{16,24},{20,28},{24,16},{28,20},{1,9},{5... | collective-permute-start | bytes 2654216 | tf_op jit(solution)/shard_map/ppermute | solution.py:323
  97.4 21.7 %collective-permute-start.20 = (bf16[1,12,144,256]{3,2,1,0:T(8,128)(2,1)S(1)}, bf16[1,12,144,256]{3,2,1,0:T(8,128)(2,1)}, u32[]{:S(2)}, u32[]{:S(2)}) collective-permute-start(bf16[1,12,144,256]{3,2,1,0:T(8,128)(2,1)S(1)} %constant_dynamic-update-slice_fusion.4.refs_5_), channel_id=1, source_target_pairs={{0,16},{4,20},{8,24},{12,28},{16,0},{20,4},{24,8},{28,12},{1,17},{... | collective-permute-start | bytes 2654216 | tf_op jit(solution)/shard_map/ppermute | solution.py:323
  119.1 24.6 %copy-start.6 = (bf16[1,12,144,256]{3,2,1,0:T(8,128)(2,1)}, bf16[1,12,144,256]{3,2,1,0:T(8,128)(2,1)S(1)}, u32[]{:S(2)}) copy-start(bf16[1,12,144,256]{3,2,1,0:T(8,128)(2,1)S(1)} %collective-permute-done.19.refs_4_) | copy-start | bytes 2654212
  119.1 24.6 %collective-permute-start.28 = (bf16[1,12,144,256]{3,2,1,0:T(8,128)(2,1)}, bf16[1,12,144,256]{3,2,1,0:T(8,128)(2,1)S(1)}, u32[]{:S(2)}, u32[]{:S(2)}) collective-permute-start(bf16[1,12,144,256]{3,2,1,0:T(8,128)(2,1)} %collective-permute-done.20.refs_5_), channel_id=1, source_target_pairs={{0,8},{4,12},{8,0},{12,4},{16,24},{20,28},{24,16},{28,20},{1,9},{5... | collective-permute-start | bytes 2654216 | tf_op jit(solution)/shard_map/ppermute | solution.py:323
  120.6 23.6 %collective-permute-start.25 = (bf16[1,12,144,256]{3,2,1,0:T(8,128)(2,1)S(1)}, bf16[1,12,144,256]{3,2,1,0:T(8,128)(2,1)}, u32[]{:S(2)}, u32[]{:S(2)}) collective-permute-start(bf16[1,12,144,256]{3,2,1,0:T(8,128)(2,1)S(1)} %collective-permute-done.19.refs_4_), channel_id=1, source_target_pairs={{0,4},{4,0},{8,12},{12,8},{16,20},{20,16},{24,28},{28,24},{1,5},{5... | collective-permute-start | bytes 2654216 | tf_op jit(solution)/shard_map/ppermute | solution.py:323
  120.7 1.2 copy-start.11
  120.7 23.6 %collective-permute-start.26 = (bf16[1,12,144,256]{3,2,1,0:T(8,128)(2,1)}, bf16[1,12,144,256]{3,2,1,0:T(8,128)(2,1)}, u32[]{:S(2)}, u32[]{:S(2)}) collective-permute-start(bf16[1,12,144,256]{3,2,1,0:T(8,128)(2,1)} %collective-permute-done.20.refs_5_), channel_id=1, source_target_pairs={{0,4},{4,0},{8,12},{12,8},{16,20},{20,16},{24,28},{28,24},{1,5},{5... | collective-permute-start | bytes 2654216 | tf_op jit(solution)/shard_map/ppermute | solution.py:323
  121.2 0.7 copy-start.12
  121.2 22.5 %collective-permute-start.27 = (bf16[1,12,144,256]{3,2,1,0:T(8,128)(2,1)}, bf16[1,12,144,256]{3,2,1,0:T(8,128)(2,1)}, u32[]{:S(2)}, u32[]{:S(2)}) collective-permute-start(bf16[1,12,144,256]{3,2,1,0:T(8,128)(2,1)} %collective-permute-done.17.refs_6_), channel_id=1, source_target_pairs={{0,16},{4,20},{8,24},{12,28},{16,0},{20,4},{24,8},{28,12},{1,17},{... | collective-permute-start | bytes 2654216 | tf_op jit(solution)/shard_map/ppermute | solution.py:323
  121.9 0.7 copy-start.13
  143.7 3.9 %copy-start.7 = (bf16[1,12,144,256]{3,2,1,0:T(8,128)(2,1)}, bf16[1,12,144,256]{3,2,1,0:T(8,128)(2,1)S(1)}, u32[]{:S(2)}) copy-start(bf16[1,12,144,256]{3,2,1,0:T(8,128)(2,1)S(1)} %collective-permute-done.28.refs_9_) | copy-start | bytes 2654212
  143.7 3.2 %collective-permute-start.32 = (bf16[1,12,144,256]{3,2,1,0:T(8,128)(2,1)}, bf16[1,12,144,256]{3,2,1,0:T(8,128)(2,1)S(1)}, u32[]{:S(2)}, u32[]{:S(2)}) collective-permute-start(bf16[1,12,144,256]{3,2,1,0:T(8,128)(2,1)} %collective-permute-done.27.refs_8_), channel_id=1, source_target_pairs={{0,4},{4,0},{8,12},{12,8},{16,20},{20,16},{24,28},{28,24},{1,5},{5... | collective-permute-start | bytes 2654216 | tf_op jit(solution)/shard_map/ppermute | solution.py:323
  143.8 3.8 %collective-permute-start.33 = (bf16[1,12,144,256]{3,2,1,0:T(8,128)(2,1)S(1)}, bf16[1,12,144,256]{3,2,1,0:T(8,128)(2,1)}, u32[]{:S(2)}, u32[]{:S(2)}) collective-permute-start(bf16[1,12,144,256]{3,2,1,0:T(8,128)(2,1)S(1)} %collective-permute-done.28.refs_9_), channel_id=1, source_target_pairs={{0,4},{4,0},{8,12},{12,8},{16,20},{20,16},{24,28},{28,24},{1,5},{5... | collective-permute-start | bytes 2654216 | tf_op jit(solution)/shard_map/ppermute | solution.py:323
  146.9 1.0 copy-start.8
  169.2 28.1 %collective-permute-start.37 = (bf16[1,3,144,256]{3,2,1,0:T(8,128)(2,1)}, bf16[1,3,144,256]{3,2,1,0:T(8,128)(2,1)S(1)}, u32[]{:S(2)}, u32[]{:S(2)}) collective-permute-start(bf16[1,3,144,256]{3,2,1,0:T(8,128)(2,1)} %get-tuple-element.50), channel_id=1, source_target_pairs={{1,0},{2,1},{3,2},{0,3},{5,4},{6,5},{7,6},{4,7},{9,8},{10,9},{11,1... | collective-permute-start | bytes 663560 | tf_op jit(solution)/shard_map/ppermute | solution.py:319
  171.0 26.5 %collective-permute-start.38 = (bf16[1,3,144,256]{3,2,1,0:T(8,128)(2,1)}, bf16[1,3,144,256]{3,2,1,0:T(8,128)(2,1)S(1)}, u32[]{:S(2)}, u32[]{:S(2)}) collective-permute-start(bf16[1,3,144,256]{3,2,1,0:T(8,128)(2,1)} %get-tuple-element.51), channel_id=1, source_target_pairs={{2,0},{3,1},{0,2},{1,3},{6,4},{7,5},{4,6},{5,7},{10,8},{11,9},{8,1... | collective-permute-start | bytes 663560 | tf_op jit(solution)/shard_map/ppermute | solution.py:319
  171.0 45.3 %copy-start.1 = (bf16[1,3,144,256]{3,2,1,0:T(8,128)(2,1)S(1)}, bf16[1,3,144,256]{3,2,1,0:T(8,128)(2,1)}, u32[]{:S(2)}) copy-start(bf16[1,3,144,256]{3,2,1,0:T(8,128)(2,1)} %get-tuple-element.49.refs_4_) | copy-start | bytes 663556
  171.0 26.5 %collective-permute-start.39 = (bf16[1,3,144,256]{3,2,1,0:T(8,128)(2,1)}, bf16[1,3,144,256]{3,2,1,0:T(8,128)(2,1)S(1)}, u32[]{:S(2)}, u32[]{:S(2)}) collective-permute-start(bf16[1,3,144,256]{3,2,1,0:T(8,128)(2,1)} %get-tuple-element.52), channel_id=1, source_target_pairs={{3,0},{0,1},{1,2},{2,3},{7,4},{4,5},{5,6},{6,7},{11,8},{8,9},{9,10... | collective-permute-start | bytes 663560 | tf_op jit(solution)/shard_map/ppermute | solution.py:319
  193.3 9.1 %collective-permute-start.34 = (bf16[1,3,144,256]{3,2,1,0:T(8,128)(2,1)}, bf16[1,3,144,256]{3,2,1,0:T(8,128)(2,1)S(1)}, u32[]{:S(2)}, u32[]{:S(2)}) collective-permute-start(bf16[1,3,144,256]{3,2,1,0:T(8,128)(2,1)} %get-tuple-element.45), channel_id=1, source_target_pairs={{1,0},{2,1},{3,2},{0,3},{5,4},{6,5},{7,6},{4,7},{9,8},{10,9},{11,1... | collective-permute-start | bytes 663560 | tf_op jit(solution)/shard_map/ppermute | solution.py:319
  196.1 20.1 %collective-permute-start.35 = (bf16[1,3,144,256]{3,2,1,0:T(8,128)(2,1)}, bf16[1,3,144,256]{3,2,1,0:T(8,128)(2,1)S(1)}, u32[]{:S(2)}, u32[]{:S(2)}) collective-permute-start(bf16[1,3,144,256]{3,2,1,0:T(8,128)(2,1)} %get-tuple-element.46), channel_id=1, source_target_pairs={{2,0},{3,1},{0,2},{1,3},{6,4},{7,5},{4,6},{5,7},{10,8},{11,9},{8,1... | collective-permute-start | bytes 663560 | tf_op jit(solution)/shard_map/ppermute | solution.py:319
  197.3 19.0 %collective-permute-start.36 = (bf16[1,3,144,256]{3,2,1,0:T(8,128)(2,1)}, bf16[1,3,144,256]{3,2,1,0:T(8,128)(2,1)S(1)}, u32[]{:S(2)}, u32[]{:S(2)}) collective-permute-start(bf16[1,3,144,256]{3,2,1,0:T(8,128)(2,1)} %get-tuple-element.47), channel_id=1, source_target_pairs={{3,0},{0,1},{1,2},{2,3},{7,4},{4,5},{5,6},{6,7},{11,8},{8,9},{9,10... | collective-permute-start | bytes 663560 | tf_op jit(solution)/shard_map/ppermute | solution.py:319
  216.3 0.9 copy-start.2

commit v4 on v3

--- a/solution.py
+++ b/solution.py
@@ -182,13 +182,17 @@
             put(plane, v[:side])
             put(plane + PACK, v[side:])
 
+    def screen(r):
+        both = [kernel_ref[min(b, side - b)] for b in (2 * r, 2 * r + 1)]
+        return jnp.concatenate(both, axis=0)
+
     def middle_two(rows):
         planes = [
             jnp.concatenate([get_across(2 * r), get_across(2 * r + 1)], axis=0).astype(BF16)
             for r in rows
         ]
         waves = [dot(ahead_ref[...], v) for v in planes]
-        waves = [(v * kernel_ref[r]).astype(BF16) for r, v in zip(rows, waves)]
+        waves = [(v * screen(r)).astype(BF16) for r, v in zip(rows, waves)]
         planes = [dot(back_ref[...], v) for v in waves]
         for r, v in zip(rows, planes):
             put_across(2 * r, v[:side])
@@ -209,14 +213,6 @@
             terms = [v * bands[base + k, t].astype(F32) for k, v in enumerate(vs)]
             total_ref[t] += terms[0] + terms[1] + terms[2]
 
-    def loop(count, at_once, run):
-        if at_once >= count:
-            run(list(range(count)))
-        else:
-            lax.fori_loop(
-                0, count // at_once, lambda q, c: run([q * at_once + w for w in range(at_once)]) or c, 0
-            )
-
     for copy in own_copies + band_copies[:PACK]:
         copy.wait()
     kernel_copy.start()
@@ -235,7 +231,7 @@
                 pltpu.make_async_copy(
                     arrays[0].at[0], bands.at[base + k], band_sem.at[base + k]
                 ).wait()
-        loop(steps, at_once[0] or steps, lambda work: first_two(base, work))
+        first_two(base, list(range(steps)))
 
         @pl.when(g == 0)
         def _():
@@ -243,8 +239,8 @@
             if has_start:
                 start_copy.wait()
 
-        loop(half, at_once[1] or half, middle_two)
-        loop(steps, at_once[2] or steps, lambda work: last_two(base, work))
+        middle_two(list(range(half)))
+        last_two(base, list(range(steps)))
         return carry
 
     lax.fori_loop(0, count, group, 0)
@@ -252,9 +248,6 @@
         for k, out_ref in enumerate(out_refs):
             size = out_ref.shape[1]
             out_ref[0] = total_ref[k * size : (k + 1) * size].astype(out_ref.dtype)
-
-
-at_once = (0, 0, 0)
 
 
 def solve(own, bands, start, tables, side, cuts=0):
@@ -301,9 +294,9 @@
     three = np.kron(np.eye(PACK, dtype=np.float32), cas.astype(np.float32))
     margin = LANES - three.shape[0]
     thirds = jnp.asarray(np.pad(three, ((0, margin), (0, margin))).astype(BF16))
-    screen = screened_kernel(side).transpose(1, 0, 2)
+    screen = screened_kernel(side)[: side // 2 + 1]
     screen = padded(np.concatenate([screen] * PACK, axis=-1), LANES)
-    screen = jnp.asarray(screen.reshape(side // 2, 2 * side, LANES))
+    screen = jnp.asarray(screen)
     table = jnp.asarray(cas)
     moved = lax.dynamic_slice_in_dim(jnp.concatenate([table, table], 0), level * slab, side, 0)
     zero = jnp.zeros_like(moved)
@@ -351,26 +344,32 @@
     return lax.optimization_barrier((value, others))[0]
 
 
-def share_out(packed, owners, which):
-    band = lax.axis_index("band")
-    core, line = band % 2, band // 2
+def hand_out(packed, which):
+    line = lax.axis_index("band") // 2
     share = packed.shape[0] // 4
     parts = []
     for k in range(4):
         part = lax.dynamic_slice_in_dim(packed, (line ^ k) * share + which, 1, 0)
         parts.append(flip(part, 2 * k) if k else part)
+    return parts
+
+
+def keep(parts, owners):
+    band = lax.axis_index("band")
+    core, line = band % 2, band // 2
     here, there = owners[core], owners[1 - core]
     mine = pick(parts, line ^ (here // 2))
     other = flip(pick(parts, line ^ (there // 2)), 1)
-    return jnp.where(here % 2 == core, mine, other), parts
+    return jnp.where(here % 2 == core, mine, other)
 
 
 def fields_small(packed, owners, tables, side):
     levels = lax.axis_size("grid")
     own0 = own_slabs(packed, 2, 0)
-    slab0, parts = share_out(packed, owners, 0)
-    slab1, _ = share_out(after(packed, parts), owners, 1)
-    slab0, own0 = lax.optimization_barrier((slab0, own0))
+    parts0, own0 = lax.optimization_barrier((hand_out(packed, 0), own0))
+    slab0 = keep(parts0, owners)
+    slab1 = keep(hand_out(after(packed, parts0), 1), owners)
+    slab0, tables = lax.optimization_barrier((slab0, tables))
     mine0 = whole(slab0)
     x0, y0 = flip(mine0, 2), flip(mine0, 4)
     mine1 = whole(after(slab1, mine0))

time: 221 us -> 210 us (0.950)
  waiting for transfers between devices: 74.9 us -> 64 us
  local copies, waits for them, and re-layouts: 9.11 us -> 12.5 us
  Pallas kernels: 90.1 us -> 87.3 us
    ppermute x18, waiting for transfers between devices: 64 us -> 53.3 us  [from_level(): return lax.ppermute(value, 'grid', pairs)]
    pallas_call x4, Pallas kernels: 84.6 us -> 81.8 us  [solve(): pl.pallas_call(body, in_specs=[hbm] * len(first) + [vmem] * 4, out_specs=...]
    unnamed x34 -> x26, local copies, waits for them, and re-layouts: 6.23 us -> 7.25 us
  transfers between devices with their start and end apart: 40 -> 40, of which waited for: 13 -> 13; matrix products, arithmetic and copies ran while one was open for 3% -> 5% of each run, Pallas kernels for 29% -> 29%
where the time goes in v4:
time: 210 us
  Pallas kernels  87.3 us (42%)
  waiting for transfers between devices  64 us (30%)
  starting transfers between devices  39.5 us (19%)
  local copies, waits for them, and re-layouts  12.5 us (6%)
  between operations  5.65 us (3%)
    pallas_call x4, Pallas kernels, solve(): pl.pallas_call(body, in_specs=[hbm] * len(first) + [vmem] * 4, out_specs=...  81.8 us
    ppermute x18, waiting for transfers between devices, from_level(): return lax.ppermute(value, 'grid', pairs)  53.3 us
    ppermute x18, starting transfers between devices, from_level(): return lax.ppermute(value, 'grid', pairs)  22.8 us
    ppermute x22, starting transfers between devices, flip(): lax.ppermute(value, 'band', [(b, b ^ bit) for b in range(lax.axis_size('b...  16.7 us
    ppermute x22, waiting for transfers between devices, flip(): lax.ppermute(value, 'band', [(b, b ^ bit) for b in range(lax.axis_size('b...  10.6 us
    unnamed x26, local copies, waits for them, and re-layouts  7.25 us
  transfers between devices with their start and end apart: 40, of which 13 were waited for; matrix products, arithmetic and copies ran while one was open for 5% of the time, Pallas kernels for 29%

profile of v4, /device:TPU:0, one launch (start us, length us, event | category | flops | bytes accessed | tf_op | source)
XLA Modules:
  0.0 209.8 jit_solution(10681764140955893070)
XLA Ops:
  0.0 1.4 copy-done
  1.4 2.0 shard_map.64
  3.4 0.9 constant_dynamic-slice_fusion.8
  4.3 2.9 %collective-permute-start = (bf16[1,3,144,256]{3,2,1,0:T(8,128)(2,1)S(1)}, bf16[1,3,144,256]{3,2,1,0:T(8,128)(2,1)S(1)}, u32[]{:S(2)}, u32[]{:S(2)}) collective-permute-start(bf16[1,3,144,256]{3,2,1,0:T(8,128)(2,1)S(1)} %get-tuple-element.84), channel_id=1, source_target_pairs={{0,8},{4,12},{8,0},{12,4},{16,24},{20,28},{24,16},{28,20},{1,9},{5... | collective-permute-start | bytes 663560 | tf_op jit(solution)/shard_map/ppermute | solution.py:316
  7.3 1.5 collective-permute-start.1
  8.8 4.1 %collective-permute-start.3 = (bf16[1,3,144,256]{3,2,1,0:T(8,128)(2,1)S(1)}, bf16[1,3,144,256]{3,2,1,0:T(8,128)(2,1)}, u32[]{:S(2)}, u32[]{:S(2)}) collective-permute-start(bf16[1,3,144,256]{3,2,1,0:T(8,128)(2,1)S(1)} %get-tuple-element.80), channel_id=1, source_target_pairs={{1,0},{2,1},{3,2},{0,3},{5,4},{6,5},{7,6},{4,7},{9,8},{10,9},{11,1... | collective-permute-start | bytes 663560 | tf_op jit(solution)/shard_map/ppermute | solution.py:312
  12.9 0.6 collective-permute-done
  13.5 2.1 %collective-permute-start.5 = (bf16[1,3,144,256]{3,2,1,0:T(8,128)(2,1)S(1)}, bf16[1,3,144,256]{3,2,1,0:T(8,128)(2,1)}, u32[]{:S(2)}, u32[]{:S(2)}) collective-permute-start(bf16[1,3,144,256]{3,2,1,0:T(8,128)(2,1)S(1)} %get-tuple-element.78), channel_id=1, source_target_pairs={{3,0},{0,1},{1,2},{2,3},{7,4},{4,5},{5,6},{6,7},{11,8},{8,9},{9,10... | collective-permute-start | bytes 663560 | tf_op jit(solution)/shard_map/ppermute | solution.py:312
  15.7 0.7 fusion.4
  21.7 0.7 constant_dynamic-slice_fusion.4
  22.5 8.4 %collective-permute-done.4.refs_2_ = bf16[1,3,144,256]{3,2,1,0:T(8,128)(2,1)} collective-permute-done((bf16[1,3,144,256]{3,2,1,0:T(8,128)(2,1)S(1)}, bf16[1,3,144,256]{3,2,1,0:T(8,128)(2,1)}, u32[]{:S(2)}, u32[]{:S(2)}) %collective-permute-start.4) | collective-permute-done | bytes 221216 | tf_op jit(solution)/shard_map/ppermute | solution.py:312
  31.1 0.7 fusion.2
  31.8 2.5 %collective-permute-start.6 = (bf16[1,3,144,256]{3,2,1,0:T(8,128)(2,1)S(1)}, bf16[1,3,144,256]{3,2,1,0:T(8,128)(2,1)S(1)}, u32[]{:S(2)}, u32[]{:S(2)}) collective-permute-start(bf16[1,3,144,256]{3,2,1,0:T(8,128)(2,1)S(1)} %get-tuple-element.77), channel_id=1, source_target_pairs={{0,24},{4,28},{8,16},{12,20},{16,8},{20,12},{24,0},{28,4},{1,25},{... | collective-permute-start | bytes 663560 | tf_op jit(solution)/shard_map/ppermute | solution.py:316
  34.4 0.5 collective-permute-start.7
  34.9 0.5 collective-permute-start.8
  35.4 0.1 select_select_fusion.1
  35.5 2.8 %collective-permute-start.12 = (bf16[1,3,144,256]{3,2,1,0:T(8,128)(2,1)S(1)}, bf16[1,3,144,256]{3,2,1,0:T(8,128)(2,1)S(1)}, u32[]{:S(2)}, u32[]{:S(2)}) collective-permute-start(bf16[1,3,144,256]{3,2,1,0:T(8,128)(2,1)S(1)} %select_select_fusion.1), channel_id=1, source_target_pairs={{2,0},{3,1},{0,2},{1,3},{6,4},{7,5},{4,6},{5,7},{10,8},{11,9},{8,1... | collective-permute-start | bytes 663560 | tf_op jit(solution)/shard_map/ppermute | solution.py:312
  38.4 2.7 %collective-permute-done.6 = bf16[1,3,144,256]{3,2,1,0:T(8,128)(2,1)S(1)} collective-permute-done((bf16[1,3,144,256]{3,2,1,0:T(8,128)(2,1)S(1)}, bf16[1,3,144,256]{3,2,1,0:T(8,128)(2,1)S(1)}, u32[]{:S(2)}, u32[]{:S(2)}) %collective-permute-start.6) | collective-permute-done | bytes 221216 | tf_op jit(solution)/shard_map/ppermute | solution.py:316
  41.1 0.7 collective-permute-start.13
  41.8 3.6 %collective-permute-done.7 = bf16[1,3,144,256]{3,2,1,0:T(8,128)(2,1)S(1)} collective-permute-done((bf16[1,3,144,256]{3,2,1,0:T(8,128)(2,1)S(1)}, bf16[1,3,144,256]{3,2,1,0:T(8,128)(2,1)S(1)}, u32[]{:S(2)}, u32[]{:S(2)}) %collective-permute-start.7) | collective-permute-done | bytes 221216 | tf_op jit(solution)/shard_map/ppermute | solution.py:316
  45.4 0.1 collective-permute-done.8
  45.6 0.7 constant_dynamic-update-slice_fusion.3
  46.3 0.7 constant_dynamic-update-slice_fusion.2
  47.0 10.7 %collective-permute-done.12 = bf16[1,3,144,256]{3,2,1,0:T(8,128)(2,1)S(1)} collective-permute-done((bf16[1,3,144,256]{3,2,1,0:T(8,128)(2,1)S(1)}, bf16[1,3,144,256]{3,2,1,0:T(8,128)(2,1)S(1)}, u32[]{:S(2)}, u32[]{:S(2)}) %collective-permute-start.12) | collective-permute-done | bytes 221216 | tf_op jit(solution)/shard_map/ppermute | solution.py:312
  57.8 0.7 constant_dynamic-update-slice_fusion.1
  58.5 0.7 constant_dynamic-update-slice_fusion.refs_4_
  59.2 1.5 collective-permute-start.17
  60.6 1.5 collective-permute-start.18
  62.4 1.9 collective-permute-start.16
  64.3 0.7 constant_dynamic-update-slice_fusion.7
  65.0 4.3 %collective-permute-done.14 = bf16[1,3,144,256]{3,2,1,0:T(8,128)(2,1)S(1)} collective-permute-done((bf16[1,3,144,256]{3,2,1,0:T(8,128)(2,1)S(1)}, bf16[1,3,144,256]{3,2,1,0:T(8,128)(2,1)S(1)}, u32[]{:S(2)}, u32[]{:S(2)}) %collective-permute-start.14) | collective-permute-done | bytes 221216 | tf_op jit(solution)/shard_map/ppermute | solution.py:312
  69.3 0.7 constant_dynamic-update-slice_fusion.6
  70.0 11.1 %collective-permute-done.15 = bf16[1,3,144,256]{3,2,1,0:T(8,128)(2,1)S(1)} collective-permute-done((bf16[1,3,144,256]{3,2,1,0:T(8,128)(2,1)S(1)}, bf16[1,3,144,256]{3,2,1,0:T(8,128)(2,1)S(1)}, u32[]{:S(2)}, u32[]{:S(2)}) %collective-permute-start.15) | collective-permute-done | bytes 221216 | tf_op jit(solution)/shard_map/ppermute | solution.py:312
  81.1 0.7 constant_dynamic-update-slice_fusion.5
  81.8 0.7 constant_dynamic-update-slice_fusion.4.refs_5_
  82.5 0.5 collective-permute-start.23
  83.1 0.7 copy.7.refs_14_.refs_15_
  83.8 0.8 constant_dynamic-slice_fusion
  84.6 1.8 collective-permute-start.30
  86.3 2.0 collective-permute-start.31
  88.4 0.5 collective-permute-start.19
  88.9 0.5 collective-permute-start.20
  89.4 20.3 %shard_map.65.refs_12_ = f32[12,144,256]{2,1,0:T(8,128)} custom-call(bf16[1,3,144,256]{3,2,1,0:T(8,128)(2,1)} %get-tuple-element.38.refs_0_, bf16[1,3,144,256]{3,2,1,0:T(8,128)(2,1)} %collective-permute-done.3.refs_1_, bf16[1,3,144,256]{3,2,1,0:T(8,128)(2,1)} %collective-permute-done.4.refs_2_, bf16[1,3,144,256]{3,2,1,0:T(8,128)(2,1)} %collective-permute-done.5.refs_3_, ...), custom_call_target="tpu_custom_call" | custom-call | flops 20639121408 | bytes 10485760 | tf_op jit(solution)/shard_map/pallas_call | solution.py:277
  109.7 0.3 collective-permute-done.20.refs_5_
  110.0 1.5 collective-permute-start.28
  111.5 0.5 collective-permute-start.26
  112.0 1.4 collective-permute-start.27
  113.4 0.7 copy-done.9
  114.0 20.3 %shard_map.66.refs_12_ = f32[12,144,256]{2,1,0:T(8,128)} custom-call(bf16[1,3,144,256]{3,2,1,0:T(8,128)(2,1)} %get-tuple-element.74.refs_0_, bf16[1,3,144,256]{3,2,1,0:T(8,128)(2,1)} %copy-done.7, bf16[1,3,144,256]{3,2,1,0:T(8,128)(2,1)} %copy-done.8, bf16[1,3,144,256]{3,2,1,0:T(8,128)(2,1)} %copy-done.9, ...), custom_call_target="tpu_custom_call" | custom-call | flops 20639121408 | bytes 10485760 | tf_op jit(solution)/shard_map/pallas_call | solution.py:277
  134.4 0.1 collective-permute-start.32
  134.5 0.5 collective-permute-start.33
  135.0 2.7 %collective-permute-done.32.refs_10_ = bf16[1,12,144,256]{3,2,1,0:T(8,128)(2,1)} collective-permute-done((bf16[1,12,144,256]{3,2,1,0:T(8,128)(2,1)}, bf16[1,12,144,256]{3,2,1,0:T(8,128)(2,1)}, u32[]{:S(2)}, u32[]{:S(2)}) %collective-permute-start.32) | collective-permute-done | bytes 884768 | tf_op jit(solution)/shard_map/ppermute | solution.py:316
  137.7 0.6 collective-permute-done.33.refs_11_
  138.3 20.6 %shard_map.68 = (bf16[1,3,144,256]{3,2,1,0:T(8,128)(2,1)}, bf16[1,3,144,256]{3,2,1,0:T(8,128)(2,1)}, bf16[1,3,144,256]{3,2,1,0:T(8,128)(2,1)}, bf16[1,3,144,256]{3,2,1,0:T(8,128)(2,1)}) custom-call(bf16[1,3,144,256]{3,2,1,0:T(8,128)(2,1)} %get-tuple-element.74.refs_0_, bf16[1,3,144,256]{3,2,1,0:T(8,128)(2,1)} %copy-done.7, ...), custom_call_target="tpu_custom_call" | custom-call | flops 20639121408 | bytes 10485760 | tf_op jit(solution)/shard_map/pallas_call | solution.py:277
  158.9 1.8 collective-permute-start.37
  160.8 1.4 collective-permute-start.39
  162.2 20.6 %shard_map.67 = (bf16[1,3,144,256]{3,2,1,0:T(8,128)(2,1)}, bf16[1,3,144,256]{3,2,1,0:T(8,128)(2,1)}, bf16[1,3,144,256]{3,2,1,0:T(8,128)(2,1)}, bf16[1,3,144,256]{3,2,1,0:T(8,128)(2,1)}) custom-call(bf16[1,3,144,256]{3,2,1,0:T(8,128)(2,1)} %get-tuple-element.38.refs_0_, bf16[1,3,144,256]{3,2,1,0:T(8,128)(2,1)} %collective-permute-done.3.refs_1_, ...), custom_call_target="tpu_custom_call" | custom-call | flops 20639121408 | bytes 10485760 | tf_op jit(solution)/shard_map/pallas_call | solution.py:277
  182.8 2.5 %collective-permute-start.34 = (bf16[1,3,144,256]{3,2,1,0:T(8,128)(2,1)}, bf16[1,3,144,256]{3,2,1,0:T(8,128)(2,1)S(1)}, u32[]{:S(2)}, u32[]{:S(2)}) collective-permute-start(bf16[1,3,144,256]{3,2,1,0:T(8,128)(2,1)} %get-tuple-element.63), channel_id=1, source_target_pairs={{1,0},{2,1},{3,2},{0,3},{5,4},{6,5},{7,6},{4,7},{9,8},{10,9},{11,1... | collective-permute-start | bytes 663560 | tf_op jit(solution)/shard_map/ppermute | solution.py:312
  185.3 1.1 collective-permute-start.35
  186.4 0.2 collective-permute-start.36
  186.6 4.9 %collective-permute-done.34.refs_1_ = bf16[1,3,144,256]{3,2,1,0:T(8,128)(2,1)S(1)} collective-permute-done((bf16[1,3,144,256]{3,2,1,0:T(8,128)(2,1)}, bf16[1,3,144,256]{3,2,1,0:T(8,128)(2,1)S(1)}, u32[]{:S(2)}, u32[]{:S(2)}) %collective-permute-start.34) | collective-permute-done | bytes 221216 | tf_op jit(solution)/shard_map/ppermute | solution.py:312
  191.5 13.9 %collective-permute-done.35.refs_2_ = bf16[1,3,144,256]{3,2,1,0:T(8,128)(2,1)S(1)} collective-permute-done((bf16[1,3,144,256]{3,2,1,0:T(8,128)(2,1)}, bf16[1,3,144,256]{3,2,1,0:T(8,128)(2,1)S(1)}, u32[]{:S(2)}, u32[]{:S(2)}) %collective-permute-start.35) | collective-permute-done | bytes 221216 | tf_op jit(solution)/shard_map/ppermute | solution.py:312
  205.4 0.9 copy-done.2
  206.4 3.5 %shard_map.69 = f32[18,8,5184]{2,1,0:T(8,128)} custom-call(s32[1]{0:T(128)} %bitcast.level_ref, bf16[1,3,144,256]{3,2,1,0:T(8,128)(2,1)S(1)} %copy-done.2, bf16[1,3,144,256]{3,2,1,0:T(8,128)(2,1)S(1)} %collective-permute-done.34.refs_1_, bf16[1,3,144,256]{3,2,1,0:T(8,128)(2,1)S(1)} %collective-permute-done.35.refs_2_, ...), custom_call_target="tpu_custom_call" | custom-call | tf_op jit(solution)/shard_map/pallas_call | solution.py:107
  (61 shorter events, 0.8 us)
Async XLA Ops:
  0.0 1.4 copy-start
  3.4 12.2 %copy-start.3 = (s32[2]{0:T(128)S(1)}, s32[2]{0:T(128)}, u32[]{:S(2)}) copy-start(s32[2]{0:T(128)} %param.7) | copy-start | bytes 28
  4.3 9.2 %collective-permute-start = (bf16[1,3,144,256]{3,2,1,0:T(8,128)(2,1)S(1)}, bf16[1,3,144,256]{3,2,1,0:T(8,128)(2,1)S(1)}, u32[]{:S(2)}, u32[]{:S(2)}) collective-permute-start(bf16[1,3,144,256]{3,2,1,0:T(8,128)(2,1)S(1)} %get-tuple-element.84), channel_id=1, source_target_pairs={{0,8},{4,12},{8,0},{12,4},{16,24},{20,28},{24,16},{28,20},{1,9},{5... | collective-permute-start | bytes 663560 | tf_op jit(solution)/shard_map/ppermute | solution.py:316
  7.3 15.2 %collective-permute-start.1 = (bf16[1,3,144,256]{3,2,1,0:T(8,128)(2,1)}, bf16[1,3,144,256]{3,2,1,0:T(8,128)(2,1)S(1)}, u32[]{:S(2)}, u32[]{:S(2)}) collective-permute-start(bf16[1,3,144,256]{3,2,1,0:T(8,128)(2,1)} %get-tuple-element.83), channel_id=1, source_target_pairs={{0,16},{4,20},{8,24},{12,28},{16,0},{20,4},{24,8},{28,12},{1,17},{... | collective-permute-start | bytes 663560 | tf_op jit(solution)/shard_map/ppermute | solution.py:316
  8.8 13.7 %collective-permute-start.2 = (bf16[1,3,144,256]{3,2,1,0:T(8,128)(2,1)S(1)}, bf16[1,3,144,256]{3,2,1,0:T(8,128)(2,1)S(1)}, u32[]{:S(2)}, u32[]{:S(2)}) collective-permute-start(bf16[1,3,144,256]{3,2,1,0:T(8,128)(2,1)S(1)} %get-tuple-element.82), channel_id=1, source_target_pairs={{0,24},{4,28},{8,16},{12,20},{16,8},{20,12},{24,0},{28,4},{1,25},{... | collective-permute-start | bytes 663560 | tf_op jit(solution)/shard_map/ppermute | solution.py:316
  8.8 13.7 %collective-permute-start.3 = (bf16[1,3,144,256]{3,2,1,0:T(8,128)(2,1)S(1)}, bf16[1,3,144,256]{3,2,1,0:T(8,128)(2,1)}, u32[]{:S(2)}, u32[]{:S(2)}) collective-permute-start(bf16[1,3,144,256]{3,2,1,0:T(8,128)(2,1)S(1)} %get-tuple-element.80), channel_id=1, source_target_pairs={{1,0},{2,1},{3,2},{0,3},{5,4},{6,5},{7,6},{4,7},{9,8},{10,9},{11,1... | collective-permute-start | bytes 663560 | tf_op jit(solution)/shard_map/ppermute | solution.py:312
  12.9 18.1 %collective-permute-start.4 = (bf16[1,3,144,256]{3,2,1,0:T(8,128)(2,1)S(1)}, bf16[1,3,144,256]{3,2,1,0:T(8,128)(2,1)}, u32[]{:S(2)}, u32[]{:S(2)}) collective-permute-start(bf16[1,3,144,256]{3,2,1,0:T(8,128)(2,1)S(1)} %get-tuple-element.79), channel_id=1, source_target_pairs={{2,0},{3,1},{0,2},{1,3},{6,4},{7,5},{4,6},{5,7},{10,8},{11,9},{8,1... | collective-permute-start | bytes 663560 | tf_op jit(solution)/shard_map/ppermute | solution.py:312
  13.5 17.4 %collective-permute-start.5 = (bf16[1,3,144,256]{3,2,1,0:T(8,128)(2,1)S(1)}, bf16[1,3,144,256]{3,2,1,0:T(8,128)(2,1)}, u32[]{:S(2)}, u32[]{:S(2)}) collective-permute-start(bf16[1,3,144,256]{3,2,1,0:T(8,128)(2,1)S(1)} %get-tuple-element.78), channel_id=1, source_target_pairs={{3,0},{0,1},{1,2},{2,3},{7,4},{4,5},{5,6},{6,7},{11,8},{8,9},{9,10... | collective-permute-start | bytes 663560 | tf_op jit(solution)/shard_map/ppermute | solution.py:312
  31.0 4.4 %collective-permute-start.10 = (bf16[1,3,144,256]{3,2,1,0:T(8,128)(2,1)S(1)}, bf16[1,3,144,256]{3,2,1,0:T(8,128)(2,1)S(1)}, u32[]{:S(2)}, u32[]{:S(2)}) collective-permute-start(bf16[1,3,144,256]{3,2,1,0:T(8,128)(2,1)S(1)} %select_select_fusion), channel_id=1, source_target_pairs={{0,4},{4,0},{8,12},{12,8},{16,20},{20,16},{24,28},{28,24},{1,5},{5... | collective-permute-start | bytes 663560 | tf_op jit(solution)/shard_map/ppermute | solution.py:316
  31.8 9.2 %collective-permute-start.6 = (bf16[1,3,144,256]{3,2,1,0:T(8,128)(2,1)S(1)}, bf16[1,3,144,256]{3,2,1,0:T(8,128)(2,1)S(1)}, u32[]{:S(2)}, u32[]{:S(2)}) collective-permute-start(bf16[1,3,144,256]{3,2,1,0:T(8,128)(2,1)S(1)} %get-tuple-element.77), channel_id=1, source_target_pairs={{0,24},{4,28},{8,16},{12,20},{16,8},{20,12},{24,0},{28,4},{1,25},{... | collective-permute-start | bytes 663560 | tf_op jit(solution)/shard_map/ppermute | solution.py:316
  34.4 11.0 %collective-permute-start.7 = (bf16[1,3,144,256]{3,2,1,0:T(8,128)(2,1)S(1)}, bf16[1,3,144,256]{3,2,1,0:T(8,128)(2,1)S(1)}, u32[]{:S(2)}, u32[]{:S(2)}) collective-permute-start(bf16[1,3,144,256]{3,2,1,0:T(8,128)(2,1)S(1)} %get-tuple-element.76), channel_id=1, source_target_pairs={{0,16},{4,20},{8,24},{12,28},{16,0},{20,4},{24,8},{28,12},{1,17},{... | collective-permute-start | bytes 663560 | tf_op jit(solution)/shard_map/ppermute | solution.py:316
  34.9 10.6 %collective-permute-start.8 = (bf16[1,3,144,256]{3,2,1,0:T(8,128)(2,1)S(1)}, bf16[1,3,144,256]{3,2,1,0:T(8,128)(2,1)S(1)}, u32[]{:S(2)}, u32[]{:S(2)}) collective-permute-start(bf16[1,3,144,256]{3,2,1,0:T(8,128)(2,1)S(1)} %get-tuple-element.75), channel_id=1, source_target_pairs={{0,8},{4,12},{8,0},{12,4},{16,24},{20,28},{24,16},{28,20},{1,9},{5... | collective-permute-start | bytes 663560 | tf_op jit(solution)/shard_map/ppermute | solution.py:316
  35.5 10.8 %collective-permute-start.11 = (bf16[1,3,144,256]{3,2,1,0:T(8,128)(2,1)S(1)}, bf16[1,3,144,256]{3,2,1,0:T(8,128)(2,1)S(1)}, u32[]{:S(2)}, u32[]{:S(2)}) collective-permute-start(bf16[1,3,144,256]{3,2,1,0:T(8,128)(2,1)S(1)} %select_select_fusion.1), channel_id=1, source_target_pairs={{1,0},{2,1},{3,2},{0,3},{5,4},{6,5},{7,6},{4,7},{9,8},{10,9},{11,1... | collective-permute-start | bytes 663560 | tf_op jit(solution)/shard_map/ppermute | solution.py:312
  35.5 22.2 %collective-permute-start.12 = (bf16[1,3,144,256]{3,2,1,0:T(8,128)(2,1)S(1)}, bf16[1,3,144,256]{3,2,1,0:T(8,128)(2,1)S(1)}, u32[]{:S(2)}, u32[]{:S(2)}) collective-permute-start(bf16[1,3,144,256]{3,2,1,0:T(8,128)(2,1)S(1)} %select_select_fusion.1), channel_id=1, source_target_pairs={{2,0},{3,1},{0,2},{1,3},{6,4},{7,5},{4,6},{5,7},{10,8},{11,9},{8,1... | collective-permute-start | bytes 663560 | tf_op jit(solution)/shard_map/ppermute | solution.py:312
  41.1 17.4 %collective-permute-start.13 = (bf16[1,3,144,256]{3,2,1,0:T(8,128)(2,1)S(1)}, bf16[1,3,144,256]{3,2,1,0:T(8,128)(2,1)S(1)}, u32[]{:S(2)}, u32[]{:S(2)}) collective-permute-start(bf16[1,3,144,256]{3,2,1,0:T(8,128)(2,1)S(1)} %select_select_fusion.1), channel_id=1, source_target_pairs={{3,0},{0,1},{1,2},{2,3},{7,4},{4,5},{5,6},{6,7},{11,8},{8,9},{9,10... | collective-permute-start | bytes 663560 | tf_op jit(solution)/shard_map/ppermute | solution.py:312
  45.5 16.6 %collective-permute-start.9 = (bf16[1,3,144,256]{3,2,1,0:T(8,128)(2,1)S(1)}, bf16[1,3,144,256]{3,2,1,0:T(8,128)(2,1)S(1)}, u32[]{:S(2)}, u32[]{:S(2)}) collective-permute-start(bf16[1,3,144,256]{3,2,1,0:T(8,128)(2,1)S(1)} %select_select_fusion.2), channel_id=1, source_target_pairs={{0,4},{4,0},{8,12},{12,8},{16,20},{20,16},{24,28},{28,24},{1,5},{5... | collective-permute-start | bytes 663560 | tf_op jit(solution)/shard_map/ppermute | solution.py:316
  59.2 23.3 %collective-permute-start.17 = (bf16[1,12,144,256]{3,2,1,0:T(8,128)(2,1)}, bf16[1,12,144,256]{3,2,1,0:T(8,128)(2,1)}, u32[]{:S(2)}, u32[]{:S(2)}) collective-permute-start(bf16[1,12,144,256]{3,2,1,0:T(8,128)(2,1)} %constant_dynamic-update-slice_fusion.refs_4_), channel_id=1, source_target_pairs={{0,8},{4,12},{8,0},{12,4},{16,24},{20,28},{24,16},{28,20},{1,9},{5... | collective-permute-start | bytes 2654216 | tf_op jit(solution)/shard_map/ppermute | solution.py:316
  60.6 22.4 %collective-permute-start.18 = (bf16[1,12,144,256]{3,2,1,0:T(8,128)(2,1)}, bf16[1,12,144,256]{3,2,1,0:T(8,128)(2,1)}, u32[]{:S(2)}, u32[]{:S(2)}) collective-permute-start(bf16[1,12,144,256]{3,2,1,0:T(8,128)(2,1)} %constant_dynamic-update-slice_fusion.refs_4_), channel_id=1, source_target_pairs={{0,16},{4,20},{8,24},{12,28},{16,0},{20,4},{24,8},{28,12},{1,17},{... | collective-permute-start | bytes 2654216 | tf_op jit(solution)/shard_map/ppermute | solution.py:316
  62.2 7.1 %collective-permute-start.14 = (bf16[1,3,144,256]{3,2,1,0:T(8,128)(2,1)S(1)}, bf16[1,3,144,256]{3,2,1,0:T(8,128)(2,1)S(1)}, u32[]{:S(2)}, u32[]{:S(2)}) collective-permute-start(bf16[1,3,144,256]{3,2,1,0:T(8,128)(2,1)S(1)} %select_select_fusion.3), channel_id=1, source_target_pairs={{1,0},{2,1},{3,2},{0,3},{5,4},{6,5},{7,6},{4,7},{9,8},{10,9},{11,1... | collective-permute-start | bytes 663560 | tf_op jit(solution)/shard_map/ppermute | solution.py:312
  62.3 18.8 %collective-permute-start.15 = (bf16[1,3,144,256]{3,2,1,0:T(8,128)(2,1)S(1)}, bf16[1,3,144,256]{3,2,1,0:T(8,128)(2,1)S(1)}, u32[]{:S(2)}, u32[]{:S(2)}) collective-permute-start(bf16[1,3,144,256]{3,2,1,0:T(8,128)(2,1)S(1)} %select_select_fusion.3), channel_id=1, source_target_pairs={{2,0},{3,1},{0,2},{1,3},{6,4},{7,5},{4,6},{5,7},{10,8},{11,9},{8,1... | collective-permute-start | bytes 663560 | tf_op jit(solution)/shard_map/ppermute | solution.py:312
  62.4 19.4 %collective-permute-start.16 = (bf16[1,3,144,256]{3,2,1,0:T(8,128)(2,1)S(1)}, bf16[1,3,144,256]{3,2,1,0:T(8,128)(2,1)S(1)}, u32[]{:S(2)}, u32[]{:S(2)}) collective-permute-start(bf16[1,3,144,256]{3,2,1,0:T(8,128)(2,1)S(1)} %select_select_fusion.3), channel_id=1, source_target_pairs={{3,0},{0,1},{1,2},{2,3},{7,4},{4,5},{5,6},{6,7},{11,8},{8,9},{9,10... | collective-permute-start | bytes 663560 | tf_op jit(solution)/shard_map/ppermute | solution.py:312
  69.3 15.3 %collective-permute-start.21 = (bf16[1,12,144,256]{3,2,1,0:T(8,128)(2,1)}, bf16[1,12,144,256]{3,2,1,0:T(8,128)(2,1)}, u32[]{:S(2)}, u32[]{:S(2)}) collective-permute-start(bf16[1,12,144,256]{3,2,1,0:T(8,128)(2,1)} %constant_dynamic-update-slice_fusion.refs_4_), channel_id=1, source_target_pairs={{0,4},{4,0},{8,12},{12,8},{16,20},{20,16},{24,28},{28,24},{1,5},{5... | collective-permute-start | bytes 2654216 | tf_op jit(solution)/shard_map/ppermute | solution.py:316
  82.5 3.8 %collective-permute-start.22 = (bf16[1,12,144,256]{3,2,1,0:T(8,128)(2,1)}, bf16[1,12,144,256]{3,2,1,0:T(8,128)(2,1)}, u32[]{:S(2)}, u32[]{:S(2)}) collective-permute-start(bf16[1,12,144,256]{3,2,1,0:T(8,128)(2,1)} %constant_dynamic-update-slice_fusion.4.refs_5_), channel_id=1, source_target_pairs={{0,4},{4,0},{8,12},{12,8},{16,20},{20,16},{24,28},{28,24},{1,5},{5... | collective-permute-start | bytes 2654216 | tf_op jit(solution)/shard_map/ppermute | solution.py:316
  82.5 5.9 %collective-permute-start.23 = (bf16[1,12,144,256]{3,2,1,0:T(8,128)(2,1)}, bf16[1,12,144,256]{3,2,1,0:T(8,128)(2,1)}, u32[]{:S(2)}, u32[]{:S(2)}) collective-permute-start(bf16[1,12,144,256]{3,2,1,0:T(8,128)(2,1)} %collective-permute-done.17.refs_6_), channel_id=1, source_target_pairs={{0,4},{4,0},{8,12},{12,8},{16,20},{20,16},{24,28},{28,24},{1,5},{5... | collective-permute-start | bytes 2654216 | tf_op jit(solution)/shard_map/ppermute | solution.py:316
  83.0 5.9 %collective-permute-start.24 = (bf16[1,12,144,256]{3,2,1,0:T(8,128)(2,1)}, bf16[1,12,144,256]{3,2,1,0:T(8,128)(2,1)}, u32[]{:S(2)}, u32[]{:S(2)}) collective-permute-start(bf16[1,12,144,256]{3,2,1,0:T(8,128)(2,1)} %collective-permute-done.18.refs_7_), channel_id=1, source_target_pairs={{0,4},{4,0},{8,12},{12,8},{16,20},{20,16},{24,28},{28,24},{1,5},{5... | collective-permute-start | bytes 2654216 | tf_op jit(solution)/shard_map/ppermute | solution.py:316
  84.6 26.9 %collective-permute-start.29 = (bf16[1,3,144,256]{3,2,1,0:T(8,128)(2,1)S(1)}, bf16[1,3,144,256]{3,2,1,0:T(8,128)(2,1)S(1)}, u32[]{:S(2)}, u32[]{:S(2)}) collective-permute-start(bf16[1,3,144,256]{3,2,1,0:T(8,128)(2,1)S(1)} %get-tuple-element.73), channel_id=1, source_target_pairs={{1,0},{2,1},{3,2},{0,3},{5,4},{6,5},{7,6},{4,7},{9,8},{10,9},{11,1... | collective-permute-start | bytes 663560 | tf_op jit(solution)/shard_map/ppermute | solution.py:312
  84.6 27.4 %collective-permute-start.30 = (bf16[1,3,144,256]{3,2,1,0:T(8,128)(2,1)S(1)}, bf16[1,3,144,256]{3,2,1,0:T(8,128)(2,1)S(1)}, u32[]{:S(2)}, u32[]{:S(2)}) collective-permute-start(bf16[1,3,144,256]{3,2,1,0:T(8,128)(2,1)S(1)} %get-tuple-element.72), channel_id=1, source_target_pairs={{2,0},{3,1},{0,2},{1,3},{6,4},{7,5},{4,6},{5,7},{10,8},{11,9},{8,1... | collective-permute-start | bytes 663560 | tf_op jit(solution)/shard_map/ppermute | solution.py:312
  86.3 27.0 %collective-permute-start.31 = (bf16[1,3,144,256]{3,2,1,0:T(8,128)(2,1)S(1)}, bf16[1,3,144,256]{3,2,1,0:T(8,128)(2,1)S(1)}, u32[]{:S(2)}, u32[]{:S(2)}) collective-permute-start(bf16[1,3,144,256]{3,2,1,0:T(8,128)(2,1)S(1)} %get-tuple-element.71), channel_id=1, source_target_pairs={{3,0},{0,1},{1,2},{2,3},{7,4},{4,5},{5,6},{6,7},{11,8},{8,9},{9,10... | collective-permute-start | bytes 663560 | tf_op jit(solution)/shard_map/ppermute | solution.py:312
  88.4 21.4 %collective-permute-start.19 = (bf16[1,12,144,256]{3,2,1,0:T(8,128)(2,1)}, bf16[1,12,144,256]{3,2,1,0:T(8,128)(2,1)S(1)}, u32[]{:S(2)}, u32[]{:S(2)}) collective-permute-start(bf16[1,12,144,256]{3,2,1,0:T(8,128)(2,1)} %constant_dynamic-update-slice_fusion.4.refs_5_), channel_id=1, source_target_pairs={{0,8},{4,12},{8,0},{12,4},{16,24},{20,28},{24,16},{28,20},{1,9},{5... | collective-permute-start | bytes 2654216 | tf_op jit(solution)/shard_map/ppermute | solution.py:316
  88.9 21.1 %collective-permute-start.20 = (bf16[1,12,144,256]{3,2,1,0:T(8,128)(2,1)}, bf16[1,12,144,256]{3,2,1,0:T(8,128)(2,1)S(1)}, u32[]{:S(2)}, u32[]{:S(2)}) collective-permute-start(bf16[1,12,144,256]{3,2,1,0:T(8,128)(2,1)} %constant_dynamic-update-slice_fusion.4.refs_5_), channel_id=1, source_target_pairs={{0,16},{4,20},{8,24},{12,28},{16,0},{20,4},{24,8},{28,12},{1,17},{... | collective-permute-start | bytes 2654216 | tf_op jit(solution)/shard_map/ppermute | solution.py:316
  109.7 24.7 %copy-start.4 = (bf16[1,12,144,256]{3,2,1,0:T(8,128)(2,1)}, bf16[1,12,144,256]{3,2,1,0:T(8,128)(2,1)S(1)}, u32[]{:S(2)}) copy-start(bf16[1,12,144,256]{3,2,1,0:T(8,128)(2,1)S(1)} %collective-permute-done.19.refs_4_) | copy-start | bytes 2654212
  110.0 24.4 %copy-start.5 = (bf16[1,12,144,256]{3,2,1,0:T(8,128)(2,1)}, bf16[1,12,144,256]{3,2,1,0:T(8,128)(2,1)S(1)}, u32[]{:S(2)}) copy-start(bf16[1,12,144,256]{3,2,1,0:T(8,128)(2,1)S(1)} %collective-permute-done.20.refs_5_) | copy-start | bytes 2654212
  110.0 24.5 %collective-permute-start.28 = (bf16[1,12,144,256]{3,2,1,0:T(8,128)(2,1)S(1)}, bf16[1,12,144,256]{3,2,1,0:T(8,128)(2,1)S(1)}, u32[]{:S(2)}, u32[]{:S(2)}) collective-permute-start(bf16[1,12,144,256]{3,2,1,0:T(8,128)(2,1)S(1)} %collective-permute-done.20.refs_5_), channel_id=1, source_target_pairs={{0,8},{4,12},{8,0},{12,4},{16,24},{20,28},{24,16},{28,20},{1,9},{5... | collective-permute-start | bytes 2654216 | tf_op jit(solution)/shard_map/ppermute | solution.py:316
  111.5 23.6 %collective-permute-start.25 = (bf16[1,12,144,256]{3,2,1,0:T(8,128)(2,1)S(1)}, bf16[1,12,144,256]{3,2,1,0:T(8,128)(2,1)}, u32[]{:S(2)}, u32[]{:S(2)}) collective-permute-start(bf16[1,12,144,256]{3,2,1,0:T(8,128)(2,1)S(1)} %collective-permute-done.19.refs_4_), channel_id=1, source_target_pairs={{0,4},{4,0},{8,12},{12,8},{16,20},{20,16},{24,28},{28,24},{1,5},{5... | collective-permute-start | bytes 2654216 | tf_op jit(solution)/shard_map/ppermute | solution.py:316
  111.5 1.9 copy-start.7
  111.5 23.5 %collective-permute-start.26 = (bf16[1,12,144,256]{3,2,1,0:T(8,128)(2,1)S(1)}, bf16[1,12,144,256]{3,2,1,0:T(8,128)(2,1)}, u32[]{:S(2)}, u32[]{:S(2)}) collective-permute-start(bf16[1,12,144,256]{3,2,1,0:T(8,128)(2,1)S(1)} %collective-permute-done.20.refs_5_), channel_id=1, source_target_pairs={{0,4},{4,0},{8,12},{12,8},{16,20},{20,16},{24,28},{28,24},{1,5},{5... | collective-permute-start | bytes 2654216 | tf_op jit(solution)/shard_map/ppermute | solution.py:316
  112.0 1.4 copy-start.8
  112.0 22.4 %collective-permute-start.27 = (bf16[1,12,144,256]{3,2,1,0:T(8,128)(2,1)}, bf16[1,12,144,256]{3,2,1,0:T(8,128)(2,1)}, u32[]{:S(2)}, u32[]{:S(2)}) collective-permute-start(bf16[1,12,144,256]{3,2,1,0:T(8,128)(2,1)} %collective-permute-done.17.refs_6_), channel_id=1, source_target_pairs={{0,16},{4,20},{8,24},{12,28},{16,0},{20,4},{24,8},{28,12},{1,17},{... | collective-permute-start | bytes 2654216 | tf_op jit(solution)/shard_map/ppermute | solution.py:316
  113.4 0.7 copy-start.9
  134.4 3.9 %copy-start.6 = (bf16[1,12,144,256]{3,2,1,0:T(8,128)(2,1)}, bf16[1,12,144,256]{3,2,1,0:T(8,128)(2,1)S(1)}, u32[]{:S(2)}) copy-start(bf16[1,12,144,256]{3,2,1,0:T(8,128)(2,1)S(1)} %collective-permute-done.28.refs_9_) | copy-start | bytes 2654212
  134.4 3.3 %collective-permute-start.32 = (bf16[1,12,144,256]{3,2,1,0:T(8,128)(2,1)}, bf16[1,12,144,256]{3,2,1,0:T(8,128)(2,1)}, u32[]{:S(2)}, u32[]{:S(2)}) collective-permute-start(bf16[1,12,144,256]{3,2,1,0:T(8,128)(2,1)} %collective-permute-done.27.refs_8_), channel_id=1, source_target_pairs={{0,4},{4,0},{8,12},{12,8},{16,20},{20,16},{24,28},{28,24},{1,5},{5... | collective-permute-start | bytes 2654216 | tf_op jit(solution)/shard_map/ppermute | solution.py:316
  134.5 3.8 %collective-permute-start.33 = (bf16[1,12,144,256]{3,2,1,0:T(8,128)(2,1)S(1)}, bf16[1,12,144,256]{3,2,1,0:T(8,128)(2,1)}, u32[]{:S(2)}, u32[]{:S(2)}) collective-permute-start(bf16[1,12,144,256]{3,2,1,0:T(8,128)(2,1)S(1)} %collective-permute-done.28.refs_9_), channel_id=1, source_target_pairs={{0,4},{4,0},{8,12},{12,8},{16,20},{20,16},{24,28},{28,24},{1,5},{5... | collective-permute-start | bytes 2654216 | tf_op jit(solution)/shard_map/ppermute | solution.py:316
  158.9 27.5 %collective-permute-start.37 = (bf16[1,3,144,256]{3,2,1,0:T(8,128)(2,1)}, bf16[1,3,144,256]{3,2,1,0:T(8,128)(2,1)S(1)}, u32[]{:S(2)}, u32[]{:S(2)}) collective-permute-start(bf16[1,3,144,256]{3,2,1,0:T(8,128)(2,1)} %get-tuple-element.68), channel_id=1, source_target_pairs={{1,0},{2,1},{3,2},{0,3},{5,4},{6,5},{7,6},{4,7},{9,8},{10,9},{11,1... | collective-permute-start | bytes 663560 | tf_op jit(solution)/shard_map/ppermute | solution.py:312
  160.8 25.9 %collective-permute-start.38 = (bf16[1,3,144,256]{3,2,1,0:T(8,128)(2,1)}, bf16[1,3,144,256]{3,2,1,0:T(8,128)(2,1)S(1)}, u32[]{:S(2)}, u32[]{:S(2)}) collective-permute-start(bf16[1,3,144,256]{3,2,1,0:T(8,128)(2,1)} %get-tuple-element.69), channel_id=1, source_target_pairs={{2,0},{3,1},{0,2},{1,3},{6,4},{7,5},{4,6},{5,7},{10,8},{11,9},{8,1... | collective-permute-start | bytes 663560 | tf_op jit(solution)/shard_map/ppermute | solution.py:312
  160.8 44.7 %copy-start.1 = (bf16[1,3,144,256]{3,2,1,0:T(8,128)(2,1)S(1)}, bf16[1,3,144,256]{3,2,1,0:T(8,128)(2,1)}, u32[]{:S(2)}) copy-start(bf16[1,3,144,256]{3,2,1,0:T(8,128)(2,1)} %get-tuple-element.67.refs_4_) | copy-start | bytes 663556
  160.8 25.9 %collective-permute-start.39 = (bf16[1,3,144,256]{3,2,1,0:T(8,128)(2,1)}, bf16[1,3,144,256]{3,2,1,0:T(8,128)(2,1)S(1)}, u32[]{:S(2)}, u32[]{:S(2)}) collective-permute-start(bf16[1,3,144,256]{3,2,1,0:T(8,128)(2,1)} %get-tuple-element.70), channel_id=1, source_target_pairs={{3,0},{0,1},{1,2},{2,3},{7,4},{4,5},{5,6},{6,7},{11,8},{8,9},{9,10... | collective-permute-start | bytes 663560 | tf_op jit(solution)/shard_map/ppermute | solution.py:312
  182.8 8.7 %collective-permute-start.34 = (bf16[1,3,144,256]{3,2,1,0:T(8,128)(2,1)}, bf16[1,3,144,256]{3,2,1,0:T(8,128)(2,1)S(1)}, u32[]{:S(2)}, u32[]{:S(2)}) collective-permute-start(bf16[1,3,144,256]{3,2,1,0:T(8,128)(2,1)} %get-tuple-element.63), channel_id=1, source_target_pairs={{1,0},{2,1},{3,2},{0,3},{5,4},{6,5},{7,6},{4,7},{9,8},{10,9},{11,1... | collective-permute-start | bytes 663560 | tf_op jit(solution)/shard_map/ppermute | solution.py:312
  185.3 20.2 %collective-permute-start.35 = (bf16[1,3,144,256]{3,2,1,0:T(8,128)(2,1)}, bf16[1,3,144,256]{3,2,1,0:T(8,128)(2,1)S(1)}, u32[]{:S(2)}, u32[]{:S(2)}) collective-permute-start(bf16[1,3,144,256]{3,2,1,0:T(8,128)(2,1)} %get-tuple-element.64), channel_id=1, source_target_pairs={{2,0},{3,1},{0,2},{1,3},{6,4},{7,5},{4,6},{5,7},{10,8},{11,9},{8,1... | collective-permute-start | bytes 663560 | tf_op jit(solution)/shard_map/ppermute | solution.py:312
  186.4 19.0 %collective-permute-start.36 = (bf16[1,3,144,256]{3,2,1,0:T(8,128)(2,1)}, bf16[1,3,144,256]{3,2,1,0:T(8,128)(2,1)S(1)}, u32[]{:S(2)}, u32[]{:S(2)}) collective-permute-start(bf16[1,3,144,256]{3,2,1,0:T(8,128)(2,1)} %get-tuple-element.65), channel_id=1, source_target_pairs={{3,0},{0,1},{1,2},{2,3},{7,4},{4,5},{5,6},{6,7},{11,8},{8,9},{9,10... | collective-permute-start | bytes 663560 | tf_op jit(solution)/shard_map/ppermute | solution.py:312
  205.4 0.9 copy-start.2

commit v5 on v4

--- a/solution.py
+++ b/solution.py
@@ -125,22 +125,23 @@
     ]
 
 
-def solve_body(*refs, side, pitch, places, pieces, count, has_start, cuts):
-    own_pieces, rest = refs[:pieces], refs[pieces:]
+def solve_body(*refs, side, pitch, places, pieces, owns, count, has_start, cuts):
+    own_pieces, rest = refs[: pieces * owns], refs[pieces * owns :]
     arrays = rest[: max(a for a, _ in places) + 1]
     rest = rest[len(arrays) :]
-    if has_start:
-        start_hbm, rest = rest[0], rest[1:]
+    starts, rest = rest[: owns * has_start], rest[owns * has_start :]
     kernel_hbm, cas2_ref, ahead_ref, back_ref, thirds_ref = rest[:5]
-    out_refs = rest[5 : 5 + max(cuts, 1)]
+    out_refs = rest[5 : 4 + max(cuts, 1) + owns]
     own_ref, bands, kernel_ref, low, high, own_sem, band_sem, wide_sem, *totals = rest[5 + len(out_refs) :]
     total_ref = totals[0] if totals else out_refs[0]
-    steps = own_ref.shape[0]
+    steps = own_ref.shape[1]
     half = side // 2
     part = steps // pieces
 
     own_copies = [
-        pltpu.make_async_copy(ref.at[0], own_ref.at[pl.ds(k * part, part)], own_sem.at[k])
+        pltpu.make_async_copy(
+            ref.at[0], own_ref.at[k // pieces, pl.ds(k % pieces * part, part)], own_sem.at[k]
+        )
         for k, ref in enumerate(own_pieces)
     ]
     band_copies = [
@@ -171,10 +172,16 @@
         parts = [r[pl.ds(row, side, stride=pitch), :] for r in (low, high)]
         return jnp.concatenate(parts, axis=1)
 
-    def first_two(base, work):
+    def owner(g):
+        return jnp.where(g == count - 1, 1, 0) if owns == 2 else 0
+
+    def first_two(base, which, work):
         sources = []
         for step in work:
-            density = [own_ref[step] * bands[base + k, step] for k in range(PACK)]
+            density = [
+                own_ref[which if k == PACK - 1 else 0, step] * bands[base + k, step]
+                for k in range(PACK)
+            ]
             sources += [(6 * step + s, v) for s, v in enumerate(swap_thirds(density, side))]
         along_z = [dot(v, thirds_ref[...]).astype(BF16) for _, v in sources]
         along_y = [dot(cas2_ref[...], v) for v in along_z]
@@ -198,7 +205,7 @@
             put_across(2 * r, v[:side])
             put_across(2 * r + 1, v[side:])
 
-    def last_two(base, work):
+    def last_two(base, which, work):
         halves = [
             [
                 jnp.concatenate([get(6 * t + s), get(6 * t + PACK + s)], axis=0).astype(BF16)
@@ -211,14 +218,20 @@
         potential = [[dot(v, thirds_ref[...]) for v in vs] for vs in swapped]
         for t, vs in zip(work, potential):
             terms = [v * bands[base + k, t].astype(F32) for k, v in enumerate(vs)]
-            total_ref[t] += terms[0] + terms[1] + terms[2]
+            if owns == 1:
+                total_ref[0, t] += terms[0] + terms[1] + terms[2]
+            else:
+                total_ref[0, t] += terms[0] + terms[1]
+                total_ref[which, t] += terms[2]
 
     for copy in own_copies + band_copies[:PACK]:
         copy.wait()
     kernel_copy.start()
-    if has_start:
-        start_copy = pltpu.make_async_copy(start_hbm, total_ref, wide_sem.at[1])
-        start_copy.start()
+    start_copies = [
+        pltpu.make_async_copy(ref, total_ref.at[i], wide_sem.at[1 + i]) for i, ref in enumerate(starts)
+    ]
+    for copy in start_copies:
+        copy.start()
     for copy in band_copies[PACK:]:
         copy.start()
 
@@ -231,60 +244,69 @@
                 pltpu.make_async_copy(
                     arrays[0].at[0], bands.at[base + k], band_sem.at[base + k]
                 ).wait()
-        first_two(base, list(range(steps)))
+        first_two(base, owner(g), list(range(steps)))
 
         @pl.when(g == 0)
         def _():
             kernel_copy.wait()
-            if has_start:
-                start_copy.wait()
+            for copy in start_copies:
+                copy.wait()
 
         middle_two(list(range(half)))
-        last_two(base, list(range(steps)))
+        last_two(base, owner(g), list(range(steps)))
         return carry
 
     lax.fori_loop(0, count, group, 0)
     if totals:
-        for k, out_ref in enumerate(out_refs):
+        for k, out_ref in enumerate(out_refs[:cuts]):
             size = out_ref.shape[1]
-            out_ref[0] = total_ref[k * size : (k + 1) * size].astype(out_ref.dtype)
-
-
-def solve(own, bands, start, tables, side, cuts=0):
+            out_ref[0] = total_ref[0, k * size : (k + 1) * size].astype(out_ref.dtype)
+        for out_ref in out_refs[cuts:]:
+            out_ref[...] = total_ref[1]
+
+
+def solve(own, bands, start, tables, side, cuts=0, second=None):
+    owns = 1 if second is None else 2
+    levels = len(own)
+    starts = [] if start is None else [start]
+    if second is not None:
+        own, starts = own + second[0], starts + [second[1]]
     places = [(a, k) for a, array in enumerate(bands) for k in range(array.shape[0])]
-    part = own[0].shape[1]
-    shape = (part * len(own),) + own[0].shape[2:]
+    shape = (own[0].shape[1] * levels,) + own[0].shape[2:]
     pitch = side + 4
     count = -(-len(places) // PACK)
     vmem = pl.BlockSpec(memory_space=pltpu.VMEM)
     hbm = pl.BlockSpec(memory_space=pl.ANY)
-    first = [*own, *bands] + ([] if start is None else [start]) + [tables[0]]
+    first = [*own, *bands, *starts, tables[0]]
     body = functools.partial(
-        solve_body, side=side, pitch=pitch, places=places, pieces=len(own), count=count,
-        has_start=start is not None, cuts=cuts
+        solve_body, side=side, pitch=pitch, places=places, pieces=levels, owns=owns,
+        count=count, has_start=start is not None, cuts=cuts
     )
     scratch = [
-        pltpu.VMEM(shape, BF16),
+        pltpu.VMEM((owns,) + shape, BF16),
         pltpu.VMEM((count * PACK,) + shape, BF16),
         pltpu.VMEM(tables[0].shape, F32),
         pltpu.VMEM((side * pitch, HALF), F32),
         pltpu.VMEM((side * pitch, HALF), F32),
         pltpu.SemaphoreType.DMA((len(own),)),
         pltpu.SemaphoreType.DMA((count * PACK,)),
-        pltpu.SemaphoreType.DMA((2,)),
+        pltpu.SemaphoreType.DMA((3,)),
     ]
+    total = jax.ShapeDtypeStruct(shape, F32)
     piece = jax.ShapeDtypeStruct((1, shape[0] // max(cuts, 1)) + shape[1:], BF16)
-    return pl.pallas_call(
+    outs = [piece] * cuts + [total] * (owns - 1) if cuts else [jax.ShapeDtypeStruct((1,) + shape, F32)]
+    result = pl.pallas_call(
         body,
         in_specs=[hbm] * len(first) + [vmem] * 4,
-        out_specs=[vmem] * cuts if cuts else vmem,
-        out_shape=[piece] * cuts if cuts else jax.ShapeDtypeStruct(shape, F32),
-        scratch_shapes=scratch + ([pltpu.VMEM(shape, F32)] if cuts else []),
+        out_specs=[vmem] * len(outs),
+        out_shape=outs,
+        scratch_shapes=scratch + ([pltpu.VMEM((owns,) + shape, F32)] if cuts else []),
         compiler_params=pltpu.CompilerParams(vmem_limit_bytes=60 * 2**20),
         cost_estimate=pl.CostEstimate(
             flops=len(places) * 96 * side**4, bytes_accessed=10 * 2**20, transcendentals=0
         ),
     )(*first, *tables[1:])
+    return result if cuts else result[0].reshape(shape)
 
 
 def make_tables(side, slab, level):
@@ -334,10 +356,13 @@
     return pieces
 
 
+def spread(slab):
+    levels = lax.axis_size("grid")
+    return [slab] + [from_level(slab, ahead) for ahead in range(1, levels)]
+
+
 def whole(slab):
-    levels = lax.axis_size("grid")
-    pieces = [slab] + [from_level(slab, ahead) for ahead in range(1, levels)]
-    return jnp.concatenate(pieces, axis=1)
+    return jnp.concatenate(spread(slab), axis=1)
 
 
 def after(value, *others):
@@ -372,21 +397,25 @@
     slab0, tables = lax.optimization_barrier((slab0, tables))
     mine0 = whole(slab0)
     x0, y0 = flip(mine0, 2), flip(mine0, 4)
-    mine1 = whole(after(slab1, mine0))
+    other0 = flip(mine0, 1)
+    slabs1 = spread(after(slab1, mine0))
+    total0 = solve(own0, [mine0, other0], None, tables, side)
+    slabs1[0], total0 = lax.optimization_barrier((slabs1[0], total0))
+    mine1 = jnp.concatenate(slabs1, axis=1)
     own1 = own_slabs(after(packed, mine1), 2, 1)
     late = after(mine1, x0, y0)
     x1, y1 = flip(late, 2), flip(late, 4)
-    near = [mine0, mine1, x0, y0]
+    near = [mine1, x0, y0]
     near = near + [flip(v, 1) for v in near]
-    total0 = solve(own0, near, None, tables, side)
+    total0 = solve(own0, near, total0, tables, side)
     x1, y1, total0 = lax.optimization_barrier((x1, y1, total0))
     corner = [flip(after(x0, x1, y1), 4), flip(y1, 2)]
     far = [x1, y1, flip(x1, 1), flip(y1, 1)]
-    total1 = solve(own1, near, None, tables, side)
+    total1 = solve(own1, [mine0, other0] + near + [x1], None, tables, side)
     corner, total1 = lax.optimization_barrier((corner, total1))
     far = far + corner + [flip(v, 1) for v in corner]
-    field0 = solve(own0, far, total0, tables, side, levels)
-    field1 = solve(own1, far, total1, tables, side, levels)
+    *field0, total1 = solve(own0, far + far[1:2], total0, tables, side, levels, (own1, total1))
+    field1 = solve(own1, far[2:], total1, tables, side, levels)
     return [field0, field1]
 
 

time: 210 us -> 203 us (0.967)
  waiting for transfers between devices: 64 us -> 44.8 us
  starting transfers between devices: 39.5 us -> 51.6 us
    ppermute x18, waiting for transfers between devices: 53.3 us -> 34.8 us  [from_level(): return lax.ppermute(value, 'grid', pairs)]
    ppermute x18, starting transfers between devices: 22.8 us -> 35.6 us  [from_level(): return lax.ppermute(value, 'grid', pairs)]
    pallas_call x4 -> x5, Pallas kernels: 81.8 us -> 83.8 us  [solve(): pl.pallas_call(body, in_specs=[hbm] * len(first) + [vmem] * 4, out_specs=...]
    unnamed x26 -> x30, local copies, waits for them, and re-layouts: 7.25 us -> 6.65 us
  transfers between devices with their start and end apart: 40 -> 40, of which waited for: 13 -> 10; matrix products, arithmetic and copies ran while one was open for 5% -> 3% of each run, Pallas kernels for 29% -> 30%
where the time goes in v5:
time: 203 us
  Pallas kernels  89.2 us (44%)
  starting transfers between devices  51.6 us (25%)
  waiting for transfers between devices  44.8 us (22%)
  local copies, waits for them, and re-layouts  11.1 us (5%)
  between operations  4.83 us (2%)
    pallas_call x5, Pallas kernels, solve(): pl.pallas_call(body, in_specs=[hbm] * len(first) + [vmem] * 4, out_specs=...  83.8 us
    ppermute x18, starting transfers between devices, from_level(): return lax.ppermute(value, 'grid', pairs)  35.6 us
    ppermute x18, waiting for transfers between devices, from_level(): return lax.ppermute(value, 'grid', pairs)  34.8 us
    ppermute x22, starting transfers between devices, flip(): lax.ppermute(value, 'band', [(b, b ^ bit) for b in range(lax.axis_size('b...  16 us
    ppermute x22, waiting for transfers between devices, flip(): lax.ppermute(value, 'band', [(b, b ^ bit) for b in range(lax.axis_size('b...  10.1 us
    unnamed x30, local copies, waits for them, and re-layouts  6.65 us
  transfers between devices with their start and end apart: 40, of which 10 were waited for; matrix products, arithmetic and copies ran while one was open for 3% of the time, Pallas kernels for 30%

profile of v5, /device:TPU:0, one launch (start us, length us, event | category | flops | bytes accessed | tf_op | source)
XLA Modules:
  0.0 202.6 jit_solution(5960519386278623919)
XLA Ops:
  0.0 1.4 copy-done
  1.4 2.0 shard_map.64
  3.4 0.9 constant_dynamic-slice_fusion.8
  4.3 3.0 %collective-permute-start.5 = (bf16[1,3,144,256]{3,2,1,0:T(8,128)(2,1)S(1)}, bf16[1,3,144,256]{3,2,1,0:T(8,128)(2,1)S(1)}, u32[]{:S(2)}, u32[]{:S(2)}) collective-permute-start(bf16[1,3,144,256]{3,2,1,0:T(8,128)(2,1)S(1)} %get-tuple-element.84), channel_id=1, source_target_pairs={{3,0},{0,1},{1,2},{2,3},{7,4},{4,5},{5,6},{6,7},{11,8},{8,9},{9,10... | collective-permute-start | bytes 663560 | tf_op jit(solution)/shard_map/ppermute | solution.py:334
  7.4 2.6 %collective-permute-start.4 = (bf16[1,3,144,256]{3,2,1,0:T(8,128)(2,1)}, bf16[1,3,144,256]{3,2,1,0:T(8,128)(2,1)}, u32[]{:S(2)}, u32[]{:S(2)}) collective-permute-start(bf16[1,3,144,256]{3,2,1,0:T(8,128)(2,1)} %get-tuple-element.85), channel_id=1, source_target_pairs={{2,0},{3,1},{0,2},{1,3},{6,4},{7,5},{4,6},{5,7},{10,8},{11,9},{8,1... | collective-permute-start | bytes 663560 | tf_op jit(solution)/shard_map/ppermute | solution.py:334
  9.9 1.3 collective-permute-start.3
  11.3 2.4 %collective-permute-start.2 = (bf16[1,3,144,256]{3,2,1,0:T(8,128)(2,1)S(1)}, bf16[1,3,144,256]{3,2,1,0:T(8,128)(2,1)S(1)}, u32[]{:S(2)}, u32[]{:S(2)}) collective-permute-start(bf16[1,3,144,256]{3,2,1,0:T(8,128)(2,1)S(1)} %get-tuple-element.88), channel_id=1, source_target_pairs={{0,24},{4,28},{8,16},{12,20},{16,8},{20,12},{24,0},{28,4},{1,25},{... | collective-permute-start | bytes 663560 | tf_op jit(solution)/shard_map/ppermute | solution.py:338
  13.7 0.5 collective-permute-start.1
  14.2 1.5 collective-permute-done.5.refs_3_
  15.8 0.7 copy-done.10
  16.5 1.7 collective-permute-start
  18.2 0.6 fusion.4
  23.3 1.2 collective-permute-done.4.refs_2_
  24.7 0.7 constant_dynamic-slice_fusion.4
  25.4 0.7 fusion.2
  26.2 0.1 select_select_fusion.1
  26.2 6.3 %collective-permute-start.11 = (bf16[1,3,144,256]{3,2,1,0:T(8,128)(2,1)S(1)}, bf16[1,3,144,256]{3,2,1,0:T(8,128)(2,1)S(1)}, u32[]{:S(2)}, u32[]{:S(2)}) collective-permute-start(bf16[1,3,144,256]{3,2,1,0:T(8,128)(2,1)S(1)} %select_select_fusion.1), channel_id=1, source_target_pairs={{1,0},{2,1},{3,2},{0,3},{5,4},{6,5},{7,6},{4,7},{9,8},{10,9},{11,1... | collective-permute-start | bytes 663560 | tf_op jit(solution)/shard_map/ppermute | solution.py:334
  32.6 1.6 collective-permute-start.8
  34.1 1.5 collective-permute-start.7
  35.6 0.5 collective-permute-start.6
  36.1 2.7 %collective-permute-start.12 = (bf16[1,3,144,256]{3,2,1,0:T(8,128)(2,1)S(1)}, bf16[1,3,144,256]{3,2,1,0:T(8,128)(2,1)S(1)}, u32[]{:S(2)}, u32[]{:S(2)}) collective-permute-start(bf16[1,3,144,256]{3,2,1,0:T(8,128)(2,1)S(1)} %select_select_fusion.1), channel_id=1, source_target_pairs={{2,0},{3,1},{0,2},{1,3},{6,4},{7,5},{4,6},{5,7},{10,8},{11,9},{8,1... | collective-permute-start | bytes 663560 | tf_op jit(solution)/shard_map/ppermute | solution.py:334
  38.9 0.7 constant_dynamic-update-slice_fusion.3
  39.6 2.5 %collective-permute-start.13 = (bf16[1,3,144,256]{3,2,1,0:T(8,128)(2,1)S(1)}, bf16[1,3,144,256]{3,2,1,0:T(8,128)(2,1)S(1)}, u32[]{:S(2)}, u32[]{:S(2)}) collective-permute-start(bf16[1,3,144,256]{3,2,1,0:T(8,128)(2,1)S(1)} %select_select_fusion.1), channel_id=1, source_target_pairs={{3,0},{0,1},{1,2},{2,3},{7,4},{4,5},{5,6},{6,7},{11,8},{8,9},{9,10... | collective-permute-start | bytes 663560 | tf_op jit(solution)/shard_map/ppermute | solution.py:334
  42.1 0.7 constant_dynamic-update-slice_fusion.2
  42.8 12.8 %collective-permute-done.12 = bf16[1,3,144,256]{3,2,1,0:T(8,128)(2,1)S(1)} collective-permute-done((bf16[1,3,144,256]{3,2,1,0:T(8,128)(2,1)S(1)}, bf16[1,3,144,256]{3,2,1,0:T(8,128)(2,1)S(1)}, u32[]{:S(2)}, u32[]{:S(2)}) %collective-permute-start.12) | collective-permute-done | bytes 221216 | tf_op jit(solution)/shard_map/ppermute | solution.py:334
  55.5 0.7 constant_dynamic-update-slice_fusion.1
  56.2 0.7 constant_dynamic-update-slice_fusion.refs_4_
  57.0 0.6 collective-permute-start.9
  57.6 1.5 collective-permute-start.22
  59.1 0.8 collective-permute-start.21
  59.9 0.7 copy.7.refs_8_.refs_13_.refs_15_.refs_21_
  60.7 0.1 collective-permute-start.16
  60.8 3.7 %collective-permute-start.15 = (bf16[1,3,144,256]{3,2,1,0:T(8,128)(2,1)S(1)}, bf16[1,3,144,256]{3,2,1,0:T(8,128)(2,1)S(1)}, u32[]{:S(2)}, u32[]{:S(2)}) collective-permute-start(bf16[1,3,144,256]{3,2,1,0:T(8,128)(2,1)S(1)} %select_select_fusion.3), channel_id=1, source_target_pairs={{1,0},{2,1},{3,2},{0,3},{5,4},{6,5},{7,6},{4,7},{9,8},{10,9},{11,1... | collective-permute-start | bytes 663560 | tf_op jit(solution)/shard_map/ppermute | solution.py:334
  64.6 9.0 %shard_map.65 = f32[1,12,144,256]{3,2,1,0:T(8,128)} custom-call(bf16[1,3,144,256]{3,2,1,0:T(8,128)(2,1)} %get-tuple-element.41.refs_0_, bf16[1,3,144,256]{3,2,1,0:T(8,128)(2,1)} %collective-permute-done.3.refs_1_, bf16[1,3,144,256]{3,2,1,0:T(8,128)(2,1)} %collective-permute-done.4.refs_2_, bf16[1,3,144,256]{3,2,1,0:T(8,128)(2,1)} %copy-done.10, ...), custom_call_target="tpu_custom_call" | custom-call | flops 5159780352 | bytes 10485760 | tf_op jit(solution)/shard_map/pallas_call | solution.py:298
  73.6 5.9 %collective-permute-done.22.refs_6_.refs_8_ = bf16[1,12,144,256]{3,2,1,0:T(8,128)(2,1)} collective-permute-done((bf16[1,12,144,256]{3,2,1,0:T(8,128)(2,1)}, bf16[1,12,144,256]{3,2,1,0:T(8,128)(2,1)}, u32[]{:S(2)}, u32[]{:S(2)}) %collective-permute-start.22) | collective-permute-done | bytes 884768 | tf_op jit(solution)/shard_map/ppermute | solution.py:338
  79.5 1.2 collective-permute-done.21.refs_5_.refs_7_
  80.9 0.6 collective-permute-start.25
  81.5 0.5 collective-permute-start.24
  82.0 0.8 collective-permute-start.23
  82.8 0.8 constant_dynamic-slice_fusion
  83.5 2.9 %collective-permute-start.20 = (bf16[1,3,144,256]{3,2,1,0:T(8,128)(2,1)S(1)}, bf16[1,3,144,256]{3,2,1,0:T(8,128)(2,1)S(1)}, u32[]{:S(2)}, u32[]{:S(2)}) collective-permute-start(bf16[1,3,144,256]{3,2,1,0:T(8,128)(2,1)S(1)} %get-tuple-element.77), channel_id=1, source_target_pairs={{3,0},{0,1},{1,2},{2,3},{7,4},{4,5},{5,6},{6,7},{11,8},{8,9},{9,10... | collective-permute-start | bytes 663560 | tf_op jit(solution)/shard_map/ppermute | solution.py:334
  86.4 2.4 %collective-permute-start.18 = (bf16[1,3,144,256]{3,2,1,0:T(8,128)(2,1)S(1)}, bf16[1,3,144,256]{3,2,1,0:T(8,128)(2,1)}, u32[]{:S(2)}, u32[]{:S(2)}) collective-permute-start(bf16[1,3,144,256]{3,2,1,0:T(8,128)(2,1)S(1)} %get-tuple-element.79), channel_id=1, source_target_pairs={{1,0},{2,1},{3,2},{0,3},{5,4},{6,5},{7,6},{4,7},{9,8},{10,9},{11,1... | collective-permute-start | bytes 663560 | tf_op jit(solution)/shard_map/ppermute | solution.py:334
  88.9 15.4 %shard_map.66 = f32[1,12,144,256]{3,2,1,0:T(8,128)} custom-call(bf16[1,3,144,256]{3,2,1,0:T(8,128)(2,1)} %get-tuple-element.41.refs_0_, bf16[1,3,144,256]{3,2,1,0:T(8,128)(2,1)} %collective-permute-done.3.refs_1_, bf16[1,3,144,256]{3,2,1,0:T(8,128)(2,1)} %collective-permute-done.4.refs_2_, bf16[1,3,144,256]{3,2,1,0:T(8,128)(2,1)} %copy-done.10, ...), custom_call_target="tpu_custom_call" | custom-call | flops 15479341056 | bytes 10485760 | tf_op jit(solution)/shard_map/pallas_call | solution.py:298
  104.3 0.1 collective-permute-start.28
  104.3 1.3 collective-permute-start.31
  105.6 0.2 collective-permute-start.29
  105.8 0.5 copy-done.11
  106.4 0.8 collective-permute-start.30
  107.2 20.6 %shard_map.67 = f32[1,12,144,256]{3,2,1,0:T(8,128)} custom-call(bf16[1,3,144,256]{3,2,1,0:T(8,128)(2,1)} %get-tuple-element.80.refs_0_.refs_4_, bf16[1,3,144,256]{3,2,1,0:T(8,128)(2,1)} %collective-permute-done.18.refs_1_.refs_5_, bf16[1,3,144,256]{3,2,1,0:T(8,128)(2,1)} %collective-permute-done.19.refs_2_.refs_6_, bf16[1,3,144,256]{3,2,1,0:T(8,128)(2,1)} %copy-done.11, ...), custom_call_target="tpu_custom_call" | custom-call | flops 23219011584 | bytes 10485760 | tf_op jit(solution)/shard_map/pallas_call | solution.py:298
  127.8 0.5 collective-permute-done.30.refs_12_.refs_6_
  128.4 0.5 collective-permute-start.33
  128.9 2.4 %collective-permute-done.32.refs_14_.refs_8_ = bf16[1,12,144,256]{3,2,1,0:T(8,128)(2,1)S(1)} collective-permute-done((bf16[1,12,144,256]{3,2,1,0:T(8,128)(2,1)S(1)}, bf16[1,12,144,256]{3,2,1,0:T(8,128)(2,1)S(1)}, u32[]{:S(2)}, u32[]{:S(2)}) %collective-permute-start.32) | collective-permute-done | bytes 884768 | tf_op jit(solution)/shard_map/ppermute | solution.py:338
  131.3 0.9 copy-done.9
  132.2 23.7 %shard_map.68 = (bf16[1,3,144,256]{3,2,1,0:T(8,128)(2,1)}, bf16[1,3,144,256]{3,2,1,0:T(8,128)(2,1)}, bf16[1,3,144,256]{3,2,1,0:T(8,128)(2,1)}, bf16[1,3,144,256]{3,2,1,0:T(8,128)(2,1)}, f32[12,144,256]{2,1,0:T(8,128)}) custom-call(bf16[1,3,144,256]{3,2,1,0:T(8,128)(2,1)} %get-tuple-element.41.refs_0_, ...), custom_call_target="tpu_custom_call" | custom-call | flops 23219011584 | bytes 10485760 | tf_op jit(solution)/shard_map/pallas_call | solution.py:298
  155.9 2.2 %collective-permute-start.34 = (bf16[1,3,144,256]{3,2,1,0:T(8,128)(2,1)}, bf16[1,3,144,256]{3,2,1,0:T(8,128)(2,1)S(1)}, u32[]{:S(2)}, u32[]{:S(2)}) collective-permute-start(bf16[1,3,144,256]{3,2,1,0:T(8,128)(2,1)} %get-tuple-element.69), channel_id=1, source_target_pairs={{1,0},{2,1},{3,2},{0,3},{5,4},{6,5},{7,6},{4,7},{9,8},{10,9},{11,1... | collective-permute-start | bytes 663560 | tf_op jit(solution)/shard_map/ppermute | solution.py:334
  158.1 1.2 collective-permute-start.35
  159.3 15.1 %shard_map.69 = (bf16[1,3,144,256]{3,2,1,0:T(8,128)(2,1)}, bf16[1,3,144,256]{3,2,1,0:T(8,128)(2,1)}, bf16[1,3,144,256]{3,2,1,0:T(8,128)(2,1)}, bf16[1,3,144,256]{3,2,1,0:T(8,128)(2,1)}) custom-call(bf16[1,3,144,256]{3,2,1,0:T(8,128)(2,1)} %get-tuple-element.80.refs_0_.refs_4_, bf16[1,3,144,256]{3,2,1,0:T(8,128)(2,1)} %collective-permute-done.18.refs_1_.refs_5_, ...), custom_call_target="tpu_custom_call" | custom-call | flops 15479341056 | bytes 10485760 | tf_op jit(solution)/shard_map/pallas_call | solution.py:298
  174.4 3.9 %collective-permute-start.37 = (bf16[1,3,144,256]{3,2,1,0:T(8,128)(2,1)}, bf16[1,3,144,256]{3,2,1,0:T(8,128)(2,1)S(1)}, u32[]{:S(2)}, u32[]{:S(2)}) collective-permute-start(bf16[1,3,144,256]{3,2,1,0:T(8,128)(2,1)} %get-tuple-element.74), channel_id=1, source_target_pairs={{1,0},{2,1},{3,2},{0,3},{5,4},{6,5},{7,6},{4,7},{9,8},{10,9},{11,1... | collective-permute-start | bytes 663560 | tf_op jit(solution)/shard_map/ppermute | solution.py:334
  178.3 0.6 collective-permute-start.39
  178.9 1.1 collective-permute-done.35.refs_2_
  180.0 4.5 %collective-permute-done.37.refs_5_ = bf16[1,3,144,256]{3,2,1,0:T(8,128)(2,1)S(1)} collective-permute-done((bf16[1,3,144,256]{3,2,1,0:T(8,128)(2,1)}, bf16[1,3,144,256]{3,2,1,0:T(8,128)(2,1)S(1)}, u32[]{:S(2)}, u32[]{:S(2)}) %collective-permute-start.37) | collective-permute-done | bytes 221216 | tf_op jit(solution)/shard_map/ppermute | solution.py:334
  184.5 13.6 %collective-permute-done.38.refs_6_ = bf16[1,3,144,256]{3,2,1,0:T(8,128)(2,1)S(1)} collective-permute-done((bf16[1,3,144,256]{3,2,1,0:T(8,128)(2,1)}, bf16[1,3,144,256]{3,2,1,0:T(8,128)(2,1)S(1)}, u32[]{:S(2)}, u32[]{:S(2)}) %collective-permute-start.38) | collective-permute-done | bytes 221216 | tf_op jit(solution)/shard_map/ppermute | solution.py:334
  198.1 0.9 copy-done.2
  199.1 3.5 %shard_map.70 = f32[18,8,5184]{2,1,0:T(8,128)} custom-call(s32[1]{0:T(128)} %bitcast.level_ref, bf16[1,3,144,256]{3,2,1,0:T(8,128)(2,1)S(1)} %copy-done.1, bf16[1,3,144,256]{3,2,1,0:T(8,128)(2,1)S(1)} %collective-permute-done.34.refs_1_, bf16[1,3,144,256]{3,2,1,0:T(8,128)(2,1)S(1)} %collective-permute-done.35.refs_2_, ...), custom_call_target="tpu_custom_call" | custom-call | tf_op jit(solution)/shard_map/pallas_call | solution.py:107
  (66 shorter events, 0.6 us)
Async XLA Ops:
  0.0 1.4 copy-start
  3.4 14.8 %copy-start.4 = (s32[2]{0:T(128)S(1)}, s32[2]{0:T(128)}, u32[]{:S(2)}) copy-start(s32[2]{0:T(128)} %param.7) | copy-start | bytes 28
  4.3 11.4 %collective-permute-start.5 = (bf16[1,3,144,256]{3,2,1,0:T(8,128)(2,1)S(1)}, bf16[1,3,144,256]{3,2,1,0:T(8,128)(2,1)S(1)}, u32[]{:S(2)}, u32[]{:S(2)}) collective-permute-start(bf16[1,3,144,256]{3,2,1,0:T(8,128)(2,1)S(1)} %get-tuple-element.84), channel_id=1, source_target_pairs={{3,0},{0,1},{1,2},{2,3},{7,4},{4,5},{5,6},{6,7},{11,8},{8,9},{9,10... | collective-permute-start | bytes 663560 | tf_op jit(solution)/shard_map/ppermute | solution.py:334
  7.4 17.2 %collective-permute-start.4 = (bf16[1,3,144,256]{3,2,1,0:T(8,128)(2,1)}, bf16[1,3,144,256]{3,2,1,0:T(8,128)(2,1)}, u32[]{:S(2)}, u32[]{:S(2)}) collective-permute-start(bf16[1,3,144,256]{3,2,1,0:T(8,128)(2,1)} %get-tuple-element.85), channel_id=1, source_target_pairs={{2,0},{3,1},{0,2},{1,3},{6,4},{7,5},{4,6},{5,7},{10,8},{11,9},{8,1... | collective-permute-start | bytes 663560 | tf_op jit(solution)/shard_map/ppermute | solution.py:334
  9.9 14.6 %collective-permute-start.3 = (bf16[1,3,144,256]{3,2,1,0:T(8,128)(2,1)S(1)}, bf16[1,3,144,256]{3,2,1,0:T(8,128)(2,1)}, u32[]{:S(2)}, u32[]{:S(2)}) collective-permute-start(bf16[1,3,144,256]{3,2,1,0:T(8,128)(2,1)S(1)} %get-tuple-element.86), channel_id=1, source_target_pairs={{1,0},{2,1},{3,2},{0,3},{5,4},{6,5},{7,6},{4,7},{9,8},{10,9},{11,1... | collective-permute-start | bytes 663560 | tf_op jit(solution)/shard_map/ppermute | solution.py:334
  11.3 13.2 %collective-permute-start.2 = (bf16[1,3,144,256]{3,2,1,0:T(8,128)(2,1)S(1)}, bf16[1,3,144,256]{3,2,1,0:T(8,128)(2,1)S(1)}, u32[]{:S(2)}, u32[]{:S(2)}) collective-permute-start(bf16[1,3,144,256]{3,2,1,0:T(8,128)(2,1)S(1)} %get-tuple-element.88), channel_id=1, source_target_pairs={{0,24},{4,28},{8,16},{12,20},{16,8},{20,12},{24,0},{28,4},{1,25},{... | collective-permute-start | bytes 663560 | tf_op jit(solution)/shard_map/ppermute | solution.py:338
  13.7 10.8 %collective-permute-start.1 = (bf16[1,3,144,256]{3,2,1,0:T(8,128)(2,1)S(1)}, bf16[1,3,144,256]{3,2,1,0:T(8,128)(2,1)S(1)}, u32[]{:S(2)}, u32[]{:S(2)}) collective-permute-start(bf16[1,3,144,256]{3,2,1,0:T(8,128)(2,1)S(1)} %get-tuple-element.89), channel_id=1, source_target_pairs={{0,16},{4,20},{8,24},{12,28},{16,0},{20,4},{24,8},{28,12},{1,17},{... | collective-permute-start | bytes 663560 | tf_op jit(solution)/shard_map/ppermute | solution.py:338
  15.8 0.7 copy-start.10
  16.5 8.1 %collective-permute-start = (bf16[1,3,144,256]{3,2,1,0:T(8,128)(2,1)S(1)}, bf16[1,3,144,256]{3,2,1,0:T(8,128)(2,1)S(1)}, u32[]{:S(2)}, u32[]{:S(2)}) collective-permute-start(bf16[1,3,144,256]{3,2,1,0:T(8,128)(2,1)S(1)} %get-tuple-element.90), channel_id=1, source_target_pairs={{0,8},{4,12},{8,0},{12,4},{16,24},{20,28},{24,16},{28,20},{1,9},{5... | collective-permute-start | bytes 663560 | tf_op jit(solution)/shard_map/ppermute | solution.py:338
  24.6 1.5 collective-permute-start.10
  26.2 13.3 %collective-permute-start.11 = (bf16[1,3,144,256]{3,2,1,0:T(8,128)(2,1)S(1)}, bf16[1,3,144,256]{3,2,1,0:T(8,128)(2,1)S(1)}, u32[]{:S(2)}, u32[]{:S(2)}) collective-permute-start(bf16[1,3,144,256]{3,2,1,0:T(8,128)(2,1)S(1)} %select_select_fusion.1), channel_id=1, source_target_pairs={{1,0},{2,1},{3,2},{0,3},{5,4},{6,5},{7,6},{4,7},{9,8},{10,9},{11,1... | collective-permute-start | bytes 663560 | tf_op jit(solution)/shard_map/ppermute | solution.py:334
  32.6 24.4 %collective-permute-start.8 = (bf16[1,3,144,256]{3,2,1,0:T(8,128)(2,1)S(1)}, bf16[1,3,144,256]{3,2,1,0:T(8,128)(2,1)S(1)}, u32[]{:S(2)}, u32[]{:S(2)}) collective-permute-start(bf16[1,3,144,256]{3,2,1,0:T(8,128)(2,1)S(1)} %get-tuple-element.81), channel_id=1, source_target_pairs={{0,8},{4,12},{8,0},{12,4},{16,24},{20,28},{24,16},{28,20},{1,9},{5... | collective-permute-start | bytes 663560 | tf_op jit(solution)/shard_map/ppermute | solution.py:338
  34.1 22.8 %collective-permute-start.7 = (bf16[1,3,144,256]{3,2,1,0:T(8,128)(2,1)S(1)}, bf16[1,3,144,256]{3,2,1,0:T(8,128)(2,1)S(1)}, u32[]{:S(2)}, u32[]{:S(2)}) collective-permute-start(bf16[1,3,144,256]{3,2,1,0:T(8,128)(2,1)S(1)} %get-tuple-element.82), channel_id=1, source_target_pairs={{0,16},{4,20},{8,24},{12,28},{16,0},{20,4},{24,8},{28,12},{1,17},{... | collective-permute-start | bytes 663560 | tf_op jit(solution)/shard_map/ppermute | solution.py:338
  35.6 21.3 %collective-permute-start.6 = (bf16[1,3,144,256]{3,2,1,0:T(8,128)(2,1)S(1)}, bf16[1,3,144,256]{3,2,1,0:T(8,128)(2,1)S(1)}, u32[]{:S(2)}, u32[]{:S(2)}) collective-permute-start(bf16[1,3,144,256]{3,2,1,0:T(8,128)(2,1)S(1)} %get-tuple-element.83), channel_id=1, source_target_pairs={{0,24},{4,28},{8,16},{12,20},{16,8},{20,12},{24,0},{28,4},{1,25},{... | collective-permute-start | bytes 663560 | tf_op jit(solution)/shard_map/ppermute | solution.py:338
  36.1 19.4 %collective-permute-start.12 = (bf16[1,3,144,256]{3,2,1,0:T(8,128)(2,1)S(1)}, bf16[1,3,144,256]{3,2,1,0:T(8,128)(2,1)S(1)}, u32[]{:S(2)}, u32[]{:S(2)}) collective-permute-start(bf16[1,3,144,256]{3,2,1,0:T(8,128)(2,1)S(1)} %select_select_fusion.1), channel_id=1, source_target_pairs={{2,0},{3,1},{0,2},{1,3},{6,4},{7,5},{4,6},{5,7},{10,8},{11,9},{8,1... | collective-permute-start | bytes 663560 | tf_op jit(solution)/shard_map/ppermute | solution.py:334
  39.6 16.7 %collective-permute-start.13 = (bf16[1,3,144,256]{3,2,1,0:T(8,128)(2,1)S(1)}, bf16[1,3,144,256]{3,2,1,0:T(8,128)(2,1)S(1)}, u32[]{:S(2)}, u32[]{:S(2)}) collective-permute-start(bf16[1,3,144,256]{3,2,1,0:T(8,128)(2,1)S(1)} %select_select_fusion.1), channel_id=1, source_target_pairs={{3,0},{0,1},{1,2},{2,3},{7,4},{4,5},{5,6},{6,7},{11,8},{8,9},{9,10... | collective-permute-start | bytes 663560 | tf_op jit(solution)/shard_map/ppermute | solution.py:334
  56.9 3.9 %collective-permute-start.14 = (bf16[1,12,144,256]{3,2,1,0:T(8,128)(2,1)}, bf16[1,12,144,256]{3,2,1,0:T(8,128)(2,1)}, u32[]{:S(2)}, u32[]{:S(2)}) collective-permute-start(bf16[1,12,144,256]{3,2,1,0:T(8,128)(2,1)} %constant_dynamic-update-slice_fusion.refs_4_), channel_id=1, source_target_pairs={{0,4},{4,0},{8,12},{12,8},{16,20},{20,16},{24,28},{28,24},{1,5},{5... | collective-permute-start | bytes 2654216 | tf_op jit(solution)/shard_map/ppermute | solution.py:338
  57.0 3.6 %collective-permute-start.9 = (bf16[1,3,144,256]{3,2,1,0:T(8,128)(2,1)S(1)}, bf16[1,3,144,256]{3,2,1,0:T(8,128)(2,1)S(1)}, u32[]{:S(2)}, u32[]{:S(2)}) collective-permute-start(bf16[1,3,144,256]{3,2,1,0:T(8,128)(2,1)S(1)} %select_select_fusion.2), channel_id=1, source_target_pairs={{0,4},{4,0},{8,12},{12,8},{16,20},{20,16},{24,28},{28,24},{1,5},{5... | collective-permute-start | bytes 663560 | tf_op jit(solution)/shard_map/ppermute | solution.py:338
  57.6 21.9 %collective-permute-start.22 = (bf16[1,12,144,256]{3,2,1,0:T(8,128)(2,1)}, bf16[1,12,144,256]{3,2,1,0:T(8,128)(2,1)}, u32[]{:S(2)}, u32[]{:S(2)}) collective-permute-start(bf16[1,12,144,256]{3,2,1,0:T(8,128)(2,1)} %constant_dynamic-update-slice_fusion.refs_4_), channel_id=1, source_target_pairs={{0,16},{4,20},{8,24},{12,28},{16,0},{20,4},{24,8},{28,12},{1,17},{... | collective-permute-start | bytes 2654216 | tf_op jit(solution)/shard_map/ppermute | solution.py:338
  59.1 21.7 %collective-permute-start.21 = (bf16[1,12,144,256]{3,2,1,0:T(8,128)(2,1)}, bf16[1,12,144,256]{3,2,1,0:T(8,128)(2,1)}, u32[]{:S(2)}, u32[]{:S(2)}) collective-permute-start(bf16[1,12,144,256]{3,2,1,0:T(8,128)(2,1)} %constant_dynamic-update-slice_fusion.refs_4_), channel_id=1, source_target_pairs={{0,8},{4,12},{8,0},{12,4},{16,24},{20,28},{24,16},{28,20},{1,9},{5... | collective-permute-start | bytes 2654216 | tf_op jit(solution)/shard_map/ppermute | solution.py:338
  60.7 20.2 %collective-permute-start.17 = (bf16[1,3,144,256]{3,2,1,0:T(8,128)(2,1)S(1)}, bf16[1,3,144,256]{3,2,1,0:T(8,128)(2,1)S(1)}, u32[]{:S(2)}, u32[]{:S(2)}) collective-permute-start(bf16[1,3,144,256]{3,2,1,0:T(8,128)(2,1)S(1)} %select_select_fusion.3), channel_id=1, source_target_pairs={{3,0},{0,1},{1,2},{2,3},{7,4},{4,5},{5,6},{6,7},{11,8},{8,9},{9,10... | collective-permute-start | bytes 663560 | tf_op jit(solution)/shard_map/ppermute | solution.py:334
  60.7 20.1 %collective-permute-start.16 = (bf16[1,3,144,256]{3,2,1,0:T(8,128)(2,1)S(1)}, bf16[1,3,144,256]{3,2,1,0:T(8,128)(2,1)S(1)}, u32[]{:S(2)}, u32[]{:S(2)}) collective-permute-start(bf16[1,3,144,256]{3,2,1,0:T(8,128)(2,1)S(1)} %select_select_fusion.3), channel_id=1, source_target_pairs={{2,0},{3,1},{0,2},{1,3},{6,4},{7,5},{4,6},{5,7},{10,8},{11,9},{8,1... | collective-permute-start | bytes 663560 | tf_op jit(solution)/shard_map/ppermute | solution.py:334
  60.8 20.0 %collective-permute-start.15 = (bf16[1,3,144,256]{3,2,1,0:T(8,128)(2,1)S(1)}, bf16[1,3,144,256]{3,2,1,0:T(8,128)(2,1)S(1)}, u32[]{:S(2)}, u32[]{:S(2)}) collective-permute-start(bf16[1,3,144,256]{3,2,1,0:T(8,128)(2,1)S(1)} %select_select_fusion.3), channel_id=1, source_target_pairs={{1,0},{2,1},{3,2},{0,3},{5,4},{6,5},{7,6},{4,7},{9,8},{10,9},{11,1... | collective-permute-start | bytes 663560 | tf_op jit(solution)/shard_map/ppermute | solution.py:334
  79.5 4.0 %collective-permute-start.27 = (bf16[1,12,144,256]{3,2,1,0:T(8,128)(2,1)}, bf16[1,12,144,256]{3,2,1,0:T(8,128)(2,1)}, u32[]{:S(2)}, u32[]{:S(2)}) collective-permute-start(bf16[1,12,144,256]{3,2,1,0:T(8,128)(2,1)} %collective-permute-done.22.refs_6_.refs_8_), channel_id=1, source_target_pairs={{0,4},{4,0},{8,12},{12,8},{16,20},{20,16},{24,28},{28,24},{1,5},{5... | collective-permute-start | bytes 2654216 | tf_op jit(solution)/shard_map/ppermute | solution.py:338
  80.8 5.6 %collective-permute-start.26 = (bf16[1,12,144,256]{3,2,1,0:T(8,128)(2,1)}, bf16[1,12,144,256]{3,2,1,0:T(8,128)(2,1)}, u32[]{:S(2)}, u32[]{:S(2)}) collective-permute-start(bf16[1,12,144,256]{3,2,1,0:T(8,128)(2,1)} %collective-permute-done.21.refs_5_.refs_7_), channel_id=1, source_target_pairs={{0,4},{4,0},{8,12},{12,8},{16,20},{20,16},{24,28},{28,24},{1,5},{5... | collective-permute-start | bytes 2654216 | tf_op jit(solution)/shard_map/ppermute | solution.py:338
  80.9 8.0 %copy-start.3 = (bf16[1,12,144,256]{3,2,1,0:T(8,128)(2,1)}, bf16[1,12,144,256]{3,2,1,0:T(8,128)(2,1)S(1)}, u32[]{:S(2)}) copy-start(bf16[1,12,144,256]{3,2,1,0:T(8,128)(2,1)S(1)} %constant_dynamic-update-slice_fusion.4.refs_4_.refs_6_) | copy-start | bytes 2654212
  80.9 5.5 %collective-permute-start.25 = (bf16[1,12,144,256]{3,2,1,0:T(8,128)(2,1)S(1)}, bf16[1,12,144,256]{3,2,1,0:T(8,128)(2,1)}, u32[]{:S(2)}, u32[]{:S(2)}) collective-permute-start(bf16[1,12,144,256]{3,2,1,0:T(8,128)(2,1)S(1)} %constant_dynamic-update-slice_fusion.4.refs_4_.refs_6_), channel_id=1, source_target_pairs={{0,4},{4,0},{8,12},{12,8},{16,20},{20,16},{24,28},{28,24},{1,5},{5... | collective-permute-start | bytes 2654216 | tf_op jit(solution)/shard_map/ppermute | solution.py:338
  81.5 22.8 %collective-permute-start.24 = (bf16[1,12,144,256]{3,2,1,0:T(8,128)(2,1)S(1)}, bf16[1,12,144,256]{3,2,1,0:T(8,128)(2,1)}, u32[]{:S(2)}, u32[]{:S(2)}) collective-permute-start(bf16[1,12,144,256]{3,2,1,0:T(8,128)(2,1)S(1)} %constant_dynamic-update-slice_fusion.4.refs_4_.refs_6_), channel_id=1, source_target_pairs={{0,16},{4,20},{8,24},{12,28},{16,0},{20,4},{24,8},{28,12},{1,17},{... | collective-permute-start | bytes 2654216 | tf_op jit(solution)/shard_map/ppermute | solution.py:338
  82.0 22.3 %collective-permute-start.23 = (bf16[1,12,144,256]{3,2,1,0:T(8,128)(2,1)S(1)}, bf16[1,12,144,256]{3,2,1,0:T(8,128)(2,1)}, u32[]{:S(2)}, u32[]{:S(2)}) collective-permute-start(bf16[1,12,144,256]{3,2,1,0:T(8,128)(2,1)S(1)} %constant_dynamic-update-slice_fusion.4.refs_4_.refs_6_), channel_id=1, source_target_pairs={{0,8},{4,12},{8,0},{12,4},{16,24},{20,28},{24,16},{28,20},{1,9},{5... | collective-permute-start | bytes 2654216 | tf_op jit(solution)/shard_map/ppermute | solution.py:338
  83.5 22.1 %collective-permute-start.20 = (bf16[1,3,144,256]{3,2,1,0:T(8,128)(2,1)S(1)}, bf16[1,3,144,256]{3,2,1,0:T(8,128)(2,1)S(1)}, u32[]{:S(2)}, u32[]{:S(2)}) collective-permute-start(bf16[1,3,144,256]{3,2,1,0:T(8,128)(2,1)S(1)} %get-tuple-element.77), channel_id=1, source_target_pairs={{3,0},{0,1},{1,2},{2,3},{7,4},{4,5},{5,6},{6,7},{11,8},{8,9},{9,10... | collective-permute-start | bytes 663560 | tf_op jit(solution)/shard_map/ppermute | solution.py:334
  86.4 19.9 %collective-permute-start.19 = (bf16[1,3,144,256]{3,2,1,0:T(8,128)(2,1)S(1)}, bf16[1,3,144,256]{3,2,1,0:T(8,128)(2,1)}, u32[]{:S(2)}, u32[]{:S(2)}) collective-permute-start(bf16[1,3,144,256]{3,2,1,0:T(8,128)(2,1)S(1)} %get-tuple-element.78), channel_id=1, source_target_pairs={{2,0},{3,1},{0,2},{1,3},{6,4},{7,5},{4,6},{5,7},{10,8},{11,9},{8,1... | collective-permute-start | bytes 663560 | tf_op jit(solution)/shard_map/ppermute | solution.py:334
  86.4 20.7 %collective-permute-start.18 = (bf16[1,3,144,256]{3,2,1,0:T(8,128)(2,1)S(1)}, bf16[1,3,144,256]{3,2,1,0:T(8,128)(2,1)}, u32[]{:S(2)}, u32[]{:S(2)}) collective-permute-start(bf16[1,3,144,256]{3,2,1,0:T(8,128)(2,1)S(1)} %get-tuple-element.79), channel_id=1, source_target_pairs={{1,0},{2,1},{3,2},{0,3},{5,4},{6,5},{7,6},{4,7},{9,8},{10,9},{11,1... | collective-permute-start | bytes 663560 | tf_op jit(solution)/shard_map/ppermute | solution.py:334
  104.3 24.6 %collective-permute-start.28 = (bf16[1,12,144,256]{3,2,1,0:T(8,128)(2,1)}, bf16[1,12,144,256]{3,2,1,0:T(8,128)(2,1)S(1)}, u32[]{:S(2)}, u32[]{:S(2)}) collective-permute-start(bf16[1,12,144,256]{3,2,1,0:T(8,128)(2,1)} %collective-permute-done.23.refs_12_.refs_8_), channel_id=1, source_target_pairs={{0,4},{4,0},{8,12},{12,8},{16,20},{20,16},{24,28},{28,24},{1,5},{5... | collective-permute-start | bytes 2654216 | tf_op jit(solution)/shard_map/ppermute | solution.py:338
  104.3 24.0 %collective-permute-start.31 = (bf16[1,12,144,256]{3,2,1,0:T(8,128)(2,1)}, bf16[1,12,144,256]{3,2,1,0:T(8,128)(2,1)S(1)}, u32[]{:S(2)}, u32[]{:S(2)}) collective-permute-start(bf16[1,12,144,256]{3,2,1,0:T(8,128)(2,1)} %collective-permute-done.24.refs_9_.refs_16_), channel_id=1, source_target_pairs={{0,8},{4,12},{8,0},{12,4},{16,24},{20,28},{24,16},{28,20},{1,9},{5... | collective-permute-start | bytes 2654216 | tf_op jit(solution)/shard_map/ppermute | solution.py:338
  105.6 0.7 copy-start.11
  105.6 23.2 %collective-permute-start.29 = (bf16[1,12,144,256]{3,2,1,0:T(8,128)(2,1)}, bf16[1,12,144,256]{3,2,1,0:T(8,128)(2,1)S(1)}, u32[]{:S(2)}, u32[]{:S(2)}) collective-permute-start(bf16[1,12,144,256]{3,2,1,0:T(8,128)(2,1)} %collective-permute-done.24.refs_9_.refs_16_), channel_id=1, source_target_pairs={{0,4},{4,0},{8,12},{12,8},{16,20},{20,16},{24,28},{28,24},{1,5},{5... | collective-permute-start | bytes 2654216 | tf_op jit(solution)/shard_map/ppermute | solution.py:338
  106.4 21.9 %collective-permute-start.30 = (bf16[1,12,144,256]{3,2,1,0:T(8,128)(2,1)}, bf16[1,12,144,256]{3,2,1,0:T(8,128)(2,1)S(1)}, u32[]{:S(2)}, u32[]{:S(2)}) collective-permute-start(bf16[1,12,144,256]{3,2,1,0:T(8,128)(2,1)} %collective-permute-done.21.refs_5_.refs_7_), channel_id=1, source_target_pairs={{0,16},{4,20},{8,24},{12,28},{16,0},{20,4},{24,8},{28,12},{1,17},{... | collective-permute-start | bytes 2654216 | tf_op jit(solution)/shard_map/ppermute | solution.py:338
  128.3 3.9 %copy-start.8 = (bf16[1,12,144,256]{3,2,1,0:T(8,128)(2,1)}, bf16[1,12,144,256]{3,2,1,0:T(8,128)(2,1)S(1)}, u32[]{:S(2)}) copy-start(bf16[1,12,144,256]{3,2,1,0:T(8,128)(2,1)S(1)} %collective-permute-done.30.refs_12_.refs_6_) | copy-start | bytes 2654212
  128.3 3.9 %copy-start.6 = (bf16[1,12,144,256]{3,2,1,0:T(8,128)(2,1)}, bf16[1,12,144,256]{3,2,1,0:T(8,128)(2,1)S(1)}, u32[]{:S(2)}) copy-start(bf16[1,12,144,256]{3,2,1,0:T(8,128)(2,1)S(1)} %collective-permute-done.31.refs_13_.refs_7_) | copy-start | bytes 2654212
  128.3 3.0 %collective-permute-start.32 = (bf16[1,12,144,256]{3,2,1,0:T(8,128)(2,1)S(1)}, bf16[1,12,144,256]{3,2,1,0:T(8,128)(2,1)S(1)}, u32[]{:S(2)}, u32[]{:S(2)}) collective-permute-start(bf16[1,12,144,256]{3,2,1,0:T(8,128)(2,1)S(1)} %collective-permute-done.30.refs_12_.refs_6_), channel_id=1, source_target_pairs={{0,4},{4,0},{8,12},{12,8},{16,20},{20,16},{24,28},{28,24},{1,5},{5... | collective-permute-start | bytes 2654216 | tf_op jit(solution)/shard_map/ppermute | solution.py:338
  128.4 3.8 %collective-permute-start.33 = (bf16[1,12,144,256]{3,2,1,0:T(8,128)(2,1)S(1)}, bf16[1,12,144,256]{3,2,1,0:T(8,128)(2,1)}, u32[]{:S(2)}, u32[]{:S(2)}) collective-permute-start(bf16[1,12,144,256]{3,2,1,0:T(8,128)(2,1)S(1)} %collective-permute-done.31.refs_13_.refs_7_), channel_id=1, source_target_pairs={{0,4},{4,0},{8,12},{12,8},{16,20},{20,16},{24,28},{28,24},{1,5},{5... | collective-permute-start | bytes 2654216 | tf_op jit(solution)/shard_map/ppermute | solution.py:338
  128.9 3.3 %copy-start.5 = (bf16[1,12,144,256]{3,2,1,0:T(8,128)(2,1)}, bf16[1,12,144,256]{3,2,1,0:T(8,128)(2,1)S(1)}, u32[]{:S(2)}) copy-start(bf16[1,12,144,256]{3,2,1,0:T(8,128)(2,1)S(1)} %collective-permute-done.28.refs_10_.refs_4_) | copy-start | bytes 2654212
  128.9 3.3 %copy-start.7 = (bf16[1,12,144,256]{3,2,1,0:T(8,128)(2,1)}, bf16[1,12,144,256]{3,2,1,0:T(8,128)(2,1)S(1)}, u32[]{:S(2)}) copy-start(bf16[1,12,144,256]{3,2,1,0:T(8,128)(2,1)S(1)} %collective-permute-done.29.refs_11_.refs_5_) | copy-start | bytes 2654212
  131.3 0.9 copy-start.9
  155.9 22.4 %collective-permute-start.34 = (bf16[1,3,144,256]{3,2,1,0:T(8,128)(2,1)}, bf16[1,3,144,256]{3,2,1,0:T(8,128)(2,1)S(1)}, u32[]{:S(2)}, u32[]{:S(2)}) collective-permute-start(bf16[1,3,144,256]{3,2,1,0:T(8,128)(2,1)} %get-tuple-element.69), channel_id=1, source_target_pairs={{1,0},{2,1},{3,2},{0,3},{5,4},{6,5},{7,6},{4,7},{9,8},{10,9},{11,1... | collective-permute-start | bytes 663560 | tf_op jit(solution)/shard_map/ppermute | solution.py:334
  158.1 21.8 %collective-permute-start.35 = (bf16[1,3,144,256]{3,2,1,0:T(8,128)(2,1)}, bf16[1,3,144,256]{3,2,1,0:T(8,128)(2,1)S(1)}, u32[]{:S(2)}, u32[]{:S(2)}) collective-permute-start(bf16[1,3,144,256]{3,2,1,0:T(8,128)(2,1)} %get-tuple-element.70), channel_id=1, source_target_pairs={{2,0},{3,1},{0,2},{1,3},{6,4},{7,5},{4,6},{5,7},{10,8},{11,9},{8,1... | collective-permute-start | bytes 663560 | tf_op jit(solution)/shard_map/ppermute | solution.py:334
  159.3 20.7 %collective-permute-start.36 = (bf16[1,3,144,256]{3,2,1,0:T(8,128)(2,1)}, bf16[1,3,144,256]{3,2,1,0:T(8,128)(2,1)S(1)}, u32[]{:S(2)}, u32[]{:S(2)}) collective-permute-start(bf16[1,3,144,256]{3,2,1,0:T(8,128)(2,1)} %get-tuple-element.71), channel_id=1, source_target_pairs={{3,0},{0,1},{1,2},{2,3},{7,4},{4,5},{5,6},{6,7},{11,8},{8,9},{9,10... | collective-permute-start | bytes 663560 | tf_op jit(solution)/shard_map/ppermute | solution.py:334
  159.3 38.8 %copy-start.1 = (bf16[1,3,144,256]{3,2,1,0:T(8,128)(2,1)S(1)}, bf16[1,3,144,256]{3,2,1,0:T(8,128)(2,1)}, u32[]{:S(2)}) copy-start(bf16[1,3,144,256]{3,2,1,0:T(8,128)(2,1)} %get-tuple-element.68.refs_0_) | copy-start | bytes 663556
  174.4 10.1 %collective-permute-start.37 = (bf16[1,3,144,256]{3,2,1,0:T(8,128)(2,1)}, bf16[1,3,144,256]{3,2,1,0:T(8,128)(2,1)S(1)}, u32[]{:S(2)}, u32[]{:S(2)}) collective-permute-start(bf16[1,3,144,256]{3,2,1,0:T(8,128)(2,1)} %get-tuple-element.74), channel_id=1, source_target_pairs={{1,0},{2,1},{3,2},{0,3},{5,4},{6,5},{7,6},{4,7},{9,8},{10,9},{11,1... | collective-permute-start | bytes 663560 | tf_op jit(solution)/shard_map/ppermute | solution.py:334
  178.2 19.9 %collective-permute-start.38 = (bf16[1,3,144,256]{3,2,1,0:T(8,128)(2,1)}, bf16[1,3,144,256]{3,2,1,0:T(8,128)(2,1)S(1)}, u32[]{:S(2)}, u32[]{:S(2)}) collective-permute-start(bf16[1,3,144,256]{3,2,1,0:T(8,128)(2,1)} %get-tuple-element.75), channel_id=1, source_target_pairs={{2,0},{3,1},{0,2},{1,3},{6,4},{7,5},{4,6},{5,7},{10,8},{11,9},{8,1... | collective-permute-start | bytes 663560 | tf_op jit(solution)/shard_map/ppermute | solution.py:334
  178.3 19.9 %collective-permute-start.39 = (bf16[1,3,144,256]{3,2,1,0:T(8,128)(2,1)}, bf16[1,3,144,256]{3,2,1,0:T(8,128)(2,1)S(1)}, u32[]{:S(2)}, u32[]{:S(2)}) collective-permute-start(bf16[1,3,144,256]{3,2,1,0:T(8,128)(2,1)} %get-tuple-element.76), channel_id=1, source_target_pairs={{3,0},{0,1},{1,2},{2,3},{7,4},{4,5},{5,6},{6,7},{11,8},{8,9},{9,10... | collective-permute-start | bytes 663560 | tf_op jit(solution)/shard_map/ppermute | solution.py:334
  198.1 0.9 copy-start.2
